TPU v7x, 128 devices: a whole 4x4x4 slice. The times are simulated.
128 devices in a mesh: section: 2 (over core), group: 8 (over x, z_lo), replica: 8 (over z_hi, y).
Axes of the slice: x: 4, y: 4, z: 4 (z_hi: 2, z_lo: 2; z = z_hi * 2 + z_lo), core: 2. Of those that a mesh axis runs over, the one named last changes fastest.
Arguments:
- tokens: bfloat16 [16, 1024, 768], P('replica', 'group'), may hold values from -6 to 6
- cotangent: float32 [16, 1024, 768], P('replica', 'group'), may hold values from -6 to 6
- lengths: int32 [16, 3], P('replica'), may hold values from 1 to 1022, as said below
- ln1_gain: bfloat16 [2, 768], P('section', 'group'), may hold values from 0.5 to 1.5
- ln1_bias: bfloat16 [2, 768], P('section', 'group'), may hold values from -3 to 3
- w_qkv: bfloat16 [2, 768, 2304], P('section', 'group'), may hold values from -0.21875 to 0.21875
- b_query: bfloat16 [2, 768], P('section', 'group'), may hold values from -3 to 3
- b_value: bfloat16 [2, 768], P('section', 'group'), may hold values from -3 to 3
- w_out: bfloat16 [2, 768, 768], P('section', 'group'), may hold values from -0.875 to 0.875
- b_out: bfloat16 [2, 768], P('section', 'group'), may hold values from -3 to 3
- ln2_gain: bfloat16 [2, 768], P('section', 'group'), may hold values from 0.5 to 1.5
- ln2_bias: bfloat16 [2, 768], P('section', 'group'), may hold values from -3 to 3
- w_fc: bfloat16 [2, 768, 3072], P('section', 'group'), may hold values from -0.21875 to 0.21875
- b_fc: bfloat16 [2, 3072], P('section', 'group'), may hold values from -3 to 3
- w_proj: bfloat16 [2, 3072, 768], P('section', 'group'), may hold values from -0.109375 to 0.109375
- b_proj: bfloat16 [2, 768], P('section', 'group'), may hold values from -3 to 3
Outputs:
- acts: bfloat16 [2, 16, 1024, 768], P('section', 'replica', 'group')
- in_grads: bfloat16 [2, 16, 1024, 768], P('section', 'replica', 'group')
- grad_ln1_gain: float32 [2, 768], P('section', 'group')
- grad_ln1_bias: float32 [2, 768], P('section', 'group')
- grad_w_qkv: float32 [2, 768, 2304], P('section', 'group')
- grad_b_query: float32 [2, 768], P('section', 'group')
- grad_b_value: float32 [2, 768], P('section', 'group')
- grad_w_out: float32 [2, 768, 768], P('section', 'group')
- grad_b_out: float32 [2, 768], P('section', 'group')
- grad_ln2_gain: float32 [2, 768], P('section', 'group')
- grad_ln2_bias: float32 [2, 768], P('section', 'group')
- grad_w_fc: float32 [2, 768, 3072], P('section', 'group')
- grad_b_fc: float32 [2, 3072], P('section', 'group')
- grad_w_proj: float32 [2, 3072, 768], P('section', 'group')
- grad_b_proj: float32 [2, 768], P('section', 'group')
Inputs may be any that keep to these rules, and one draw needn't show every extreme that they name: In each row the three lengths sum to 1024; the first and the last lie between 1 and 127, so the middle document reaches from the first index of group to the last.
All inputs are finite; a program needn't handle non-finite values.
Results may differ from a plain program's by a relative error of at most 0.02.
Values may be sent and summed in bfloat16 or wider, within the bound.
No kernel may reach another device: no remote copies, remote signals or barrier semaphores. Data moves between devices by JAX's collectives and lax.ppermute only.
A program may use at most 256 MiB of HBM per device.

v0:
```python
import jax
import jax.numpy as jnp
from jax import lax
from jax.sharding import PartitionSpec as P

HEADS = 12


EPSILON = 1e-05


def in_one_piece(arrays, axis, dim, along):
    columns = [a.reshape(*a.shape[:along], -1) for a in arrays]
    both = jnp.concatenate(columns, axis=along)
    result, at, done = (lax.all_gather(both, axis, axis=dim, tiled=True), 0, [])
    for a, column in zip(arrays, columns):
        slab = result[..., at : at + column.shape[along]]
        done.append(slab.reshape(*slab.shape[:along], *a.shape[along:]))
        at += column.shape[along]
    return tuple(done)


def side_by_side(arrays, axis, dim, along):
    ends, at = ([], 0)
    for a in arrays[:-1]:
        at += a.shape[along]
        ends.append(at)
    both = jnp.concatenate(arrays, axis=along)
    return tuple(jnp.split(lax.all_gather(both, axis, axis=dim, tiled=True), ends, axis=along))


def passed_along(value, axis, by):
    devices = lax.axis_size(axis)
    pairs = [(i, i + by) for i in range(devices) if 0 <= i + by < devices]
    return lax.ppermute(value, axis, pairs)


def shortened(value):

    def short(part):
        return part.astype(jnp.bfloat16) if part.dtype == jnp.float32 else part

    return jax.tree.map(short, value)


def layer_norm(inputs, gain, bias_term):
    center = inputs - jnp.mean(inputs, axis=-1, keepdims=True)
    variance = jnp.mean(center * center, axis=-1, keepdims=True)
    return center * lax.rsqrt(variance + EPSILON) * gain + bias_term


def gelu_tanh(values):
    return jax.nn.gelu(values, approximate=True)


def matmul(left, right):
    return jnp.dot(left, right, preferred_element_type=jnp.float32)


def left_inner(left, right):
    return lax.dot_general(
        left, right, (((0,), (0,)), ((), ())), preferred_element_type=jnp.float32
    )


def right_inner(left, right):
    return lax.dot_general(
        left, right, (((1,), (1,)), ((), ())), preferred_element_type=jnp.float32
    )


def split_heads(rows):
    return rows.reshape(rows.shape[0], HEADS, -1).transpose(1, 0, 2)


def merge_heads(heads_rows):
    return heads_rows.transpose(1, 0, 2).reshape(heads_rows.shape[1], -1)


def body(
    tokens,
    cotangent,
    lengths,
    ln1_gain,
    ln1_bias,
    w_qkv,
    b_query,
    b_value,
    w_out,
    b_out,
    ln2_gain,
    ln2_bias,
    w_fc,
    b_fc,
    w_proj,
    b_proj,
):
    shards = (
        ln1_gain,
        ln1_bias,
        w_qkv,
        b_query,
        b_value,
        w_out,
        b_out,
        ln2_gain,
        ln2_bias,
        w_fc,
        b_fc,
        w_proj,
        b_proj,
    )
    gathered = (
        *in_one_piece(
            (
                shards[0],
                shards[1],
                shards[2],
                shards[3],
                shards[4],
                shards[5],
                shards[6],
                shards[7],
                shards[8],
                shards[9],
            ),
            "group",
            1,
            2,
        ),
        *in_one_piece((shards[10], shards[11]), "group", 1, 2),
        lax.all_gather(shards[12], "group", axis=1, tiled=True),
    )
    weights = tuple((piece[0] for piece in gathered))
    (
        gain_one,
        bias_one,
        mat_qkv,
        bias_query,
        bias_value,
        mat_out,
        bias_out,
        gain_two,
        bias_two,
        mat_fc,
        bias_fc,
        mat_proj,
        bias_proj,
    ) = weights
    section = lax.axis_index("section")
    micro = tokens.shape[0]
    tok_rows = tokens.shape[1]
    width = tokens.shape[2]
    seq_len = tok_rows * lax.axis_size("group")
    query_pos = lax.axis_index("group") * tok_rows + jnp.arange(tok_rows, dtype=jnp.int32)
    key_pos = jnp.arange(seq_len, dtype=jnp.int32)

    def doc_of(positions, length_row):
        first_end = length_row[0]
        second_end = first_end + length_row[1]
        return (positions >= first_end).astype(jnp.int32) + (positions >= second_end).astype(
            jnp.int32
        )

    def visible(length_row):
        query_doc = doc_of(query_pos, length_row)
        key_doc = doc_of(key_pos, length_row)
        return (query_doc[:, None] == key_doc[None, :]) & (key_pos[None, :] <= query_pos[:, None])

    def attend_queries(query_rows, key_all, value_all, grad_mixed, logsum, allowed):

        def one_head(packed):
            query_one, key_one, value_one, grad_one, logsum_one = packed
            scores = right_inner(query_one, key_one) * 0.125
            scores = jnp.where(allowed, scores, -1e30)
            probs = jnp.exp(scores - logsum_one[:, None])
            grad_probs = right_inner(grad_one, value_one)
            delta = jnp.sum(probs * grad_probs, axis=-1, keepdims=True)
            grad_scores = (probs * (grad_probs - delta)).astype(jnp.bfloat16)
            grad_query = matmul(grad_scores, key_one) * 0.125
            return (grad_query, delta[:, 0])

        return lax.map(
            one_head,
            (
                split_heads(query_rows),
                split_heads(key_all),
                split_heads(value_all),
                split_heads(grad_mixed),
                logsum,
            ),
        )

    def attend_keys(query_all, key_rows, value_rows, grad_all, logsum_all, delta_all, allowed):

        def one_head(packed):
            query_one, key_one, value_one, grad_one, logsum_one, delta_one = packed
            scores = right_inner(query_one, key_one) * 0.125
            scores = jnp.where(allowed, scores, -1e30)
            probs = jnp.exp(scores - logsum_one[:, None])
            grad_probs = right_inner(grad_one, value_one)
            grad_scores = (probs * (grad_probs - delta_one[:, None])).astype(jnp.bfloat16)
            grad_key = left_inner(grad_scores, query_one) * 0.125
            grad_value = left_inner(probs.astype(jnp.bfloat16), grad_one)
            return (grad_key, grad_value)

        return lax.map(
            one_head,
            (
                split_heads(query_all),
                split_heads(key_rows),
                split_heads(value_rows),
                split_heads(grad_all),
                logsum_all,
                delta_all,
            ),
        )

    def pick_section(first_item, second_item):
        return jnp.where(section == 0, first_item, second_item)

    received = jnp.zeros((tok_rows, width), jnp.bfloat16)
    output_slots = []
    saved_slots = []
    for slot in range(micro + 1):
        own_rows = tokens[min(slot, micro - 1)].astype(jnp.float32)
        inputs = jnp.where(section == 0, own_rows, received.astype(jnp.float32))
        micro_index = jnp.clip(slot - section, 0, micro - 1)
        forward_length_row = lengths[micro_index]
        normed_low = layer_norm(inputs, gain_one, bias_one).astype(jnp.bfloat16)
        projected = matmul(normed_low, mat_qkv)
        forward_query_rows = (projected[:, :width] + bias_query).astype(jnp.bfloat16)
        forward_key_rows = projected[:, width : 2 * width].astype(jnp.bfloat16)
        forward_value_rows = (projected[:, 2 * width :] + bias_value).astype(jnp.bfloat16)
        forward_key_all, forward_value_all = side_by_side(
            (forward_key_rows, forward_value_rows), "group", 0, 1
        )
        attend_allowed = visible(forward_length_row)

        def attend_one_head(packed):
            query_one, key_one, value_one = packed
            scores = right_inner(query_one, key_one) * 0.125
            scores = jnp.where(attend_allowed, scores, -1e30)
            maximum = jnp.max(scores, axis=-1, keepdims=True)
            expo = jnp.exp(scores - maximum)
            total = jnp.sum(expo, axis=-1, keepdims=True)
            probs = (expo / total).astype(jnp.bfloat16)
            return (matmul(probs, value_one), (maximum + jnp.log(total))[:, 0])

        mixed, forward_logsum = lax.map(
            attend_one_head,
            (
                split_heads(forward_query_rows),
                split_heads(forward_key_all),
                split_heads(forward_value_all),
            ),
        )
        mixed_low = merge_heads(mixed).astype(jnp.bfloat16)
        middle = inputs + matmul(mixed_low, mat_out) + bias_out
        normed_two_low = layer_norm(middle, gain_two, bias_two).astype(jnp.bfloat16)
        hidden_pre = matmul(normed_two_low, mat_fc) + bias_fc
        active_low = gelu_tanh(hidden_pre).astype(jnp.bfloat16)
        result = middle + matmul(active_low, mat_proj) + bias_proj
        forward_saved = {
            "inputs": inputs,
            "length_row": forward_length_row,
            "normed_low": normed_low,
            "query_rows": forward_query_rows,
            "key_rows": forward_key_rows,
            "value_rows": forward_value_rows,
            "logsum": forward_logsum,
            "mixed_low": mixed_low,
            "middle": middle,
            "normed_two_low": normed_two_low,
            "hidden_pre": hidden_pre,
            "active_low": active_low,
        }
        forward_saved["key_all"] = forward_key_all
        forward_saved["value_all"] = forward_value_all
        result, saved = (result, forward_saved)
        result_low = result.astype(jnp.bfloat16)
        output_slots.append(result_low)
        saved_slots.append(saved)
        if slot < micro:
            received = passed_along(result_low, "section", 1)
    acts = jnp.stack(
        [pick_section(output_slots[index], output_slots[index + 1]) for index in range(micro)]
    )
    received_grad = jnp.zeros((tok_rows, width), jnp.bfloat16)
    grad_slots = []
    totals = None
    for slot in range(micro + 1):
        own_grad = cotangent[min(slot, micro - 1)]
        grad_out = jnp.where(section == 1, own_grad, received_grad.astype(jnp.float32))
        saved = jax.tree.map(
            pick_section, saved_slots[max(slot - 1, 0)], saved_slots[min(slot + 1, micro)]
        )
        grad_branch = grad_out.astype(jnp.bfloat16)
        grad_mat_proj = left_inner(saved["active_low"], grad_branch)
        grad_bias_proj = jnp.sum(grad_branch.astype(jnp.float32), axis=0)
        grad_active = right_inner(grad_branch, mat_proj)
        gelu_pull = jax.vjp(gelu_tanh, saved["hidden_pre"])[1]
        grad_hidden = gelu_pull(grad_active)[0].astype(jnp.bfloat16)
        grad_mat_fc = left_inner(saved["normed_two_low"], grad_hidden)
        grad_bias_fc = jnp.sum(grad_hidden.astype(jnp.float32), axis=0)
        grad_normed_two = right_inner(grad_hidden, mat_fc)
        norm_two_pull = jax.vjp(layer_norm, saved["middle"], gain_two, bias_two)[1]
        grad_mid_part, grad_gain_two, grad_bias_two = norm_two_pull(grad_normed_two)
        grad_middle = grad_out + grad_mid_part
        grad_attn = grad_middle.astype(jnp.bfloat16)
        grad_mat_out = left_inner(saved["mixed_low"], grad_attn)
        grad_bias_out = jnp.sum(grad_attn.astype(jnp.float32), axis=0)
        backward_grad_mixed = right_inner(grad_attn, mat_out).astype(jnp.bfloat16)
        backward_key_all = saved["key_all"]
        backward_value_all = saved["value_all"]
        backward_grad_query, backward_delta = attend_queries(
            saved["query_rows"],
            backward_key_all,
            backward_value_all,
            backward_grad_mixed,
            saved["logsum"],
            visible(saved["length_row"]),
        )
        backward_query_all, backward_grad_all = side_by_side(
            (saved["query_rows"], backward_grad_mixed), "group", 0, 1
        )
        backward_logsum_all, backward_delta_all = side_by_side(
            (saved["logsum"], backward_delta), "group", 1, 0
        )
        visible_length_row = saved["length_row"]
        visible_query_doc = doc_of(key_pos, visible_length_row)
        visible_key_doc = doc_of(query_pos, visible_length_row)
        backward_grad_key, backward_grad_value = attend_keys(
            backward_query_all,
            saved["key_rows"],
            saved["value_rows"],
            backward_grad_all,
            backward_logsum_all,
            backward_delta_all,
            (visible_query_doc[:, None] == visible_key_doc[None, :])
            & (query_pos[None, :] <= key_pos[:, None]),
        )
        key_sum = merge_heads(backward_grad_key)
        value_sum = merge_heads(backward_grad_value)
        query_low = merge_heads(backward_grad_query).astype(jnp.bfloat16)
        key_low = key_sum.astype(jnp.bfloat16)
        value_low = value_sum.astype(jnp.bfloat16)
        grad_packed = jnp.concatenate([query_low, key_low, value_low], axis=1)
        grad_mat_qkv = left_inner(saved["normed_low"], grad_packed)
        grad_bias_query = jnp.sum(query_low.astype(jnp.float32), axis=0)
        grad_bias_value = jnp.sum(value_low.astype(jnp.float32), axis=0)
        grad_normed = right_inner(grad_packed, mat_qkv)
        norm_one_pull = jax.vjp(layer_norm, saved["inputs"], gain_one, bias_one)[1]
        grad_in_part, grad_gain_one, grad_bias_one = norm_one_pull(grad_normed)
        grads = (
            grad_gain_one,
            grad_bias_one,
            grad_mat_qkv,
            grad_bias_query,
            grad_bias_value,
            grad_mat_out,
            grad_bias_out,
            grad_gain_two,
            grad_bias_two,
            grad_mat_fc,
            grad_bias_fc,
            grad_mat_proj,
            grad_bias_proj,
        )
        grad_in, grads = (grad_middle + grad_in_part, grads)
        weight_flag = jnp.where(section == 1, float(slot < micro), float(slot >= 1)).astype(
            jnp.float32
        )
        scaled = tuple((piece * weight_flag for piece in grads))
        totals = (
            scaled
            if totals is None
            else tuple(
                (first_item + second_item for first_item, second_item in zip(totals, scaled))
            )
        )
        grad_low = grad_in.astype(jnp.bfloat16)
        grad_slots.append(grad_low)
        if slot < micro:
            received_grad = passed_along(grad_low, "section", -1)
    in_grads = jnp.stack(
        [pick_section(grad_slots[index + 1], grad_slots[index]) for index in range(micro)]
    )
    pieces = jax.tree.map(
        lambda part: part.astype(jnp.float32),
        lax.psum_scatter(shortened(totals), "group", scatter_dimension=0, tiled=True),
    )
    reduced = jax.tree.map(
        lambda part: part.astype(jnp.float32), lax.psum(shortened(pieces), "replica")
    )
    grad_outputs = tuple((piece[None] for piece in reduced))
    return (acts[None], in_grads[None]) + grad_outputs


def solution(mesh):
    placed = (
        P("replica", "group", None),
        P("replica", "group", None),
        P("replica", None),
        P("section", "group"),
        P("section", "group"),
        P("section", "group", None),
        P("section", "group"),
        P("section", "group"),
        P("section", "group", None),
        P("section", "group"),
        P("section", "group"),
        P("section", "group"),
        P("section", "group", None),
        P("section", "group"),
        P("section", "group", None),
        P("section", "group"),
    )
    return jax.shard_map(
        body,
        mesh=mesh,
        in_specs=placed,
        out_specs=(
            P("section", "replica", "group", None),
            P("section", "replica", "group", None),
            P("section", "group"),
            P("section", "group"),
            P("section", "group", None),
            P("section", "group"),
            P("section", "group"),
            P("section", "group", None),
            P("section", "group"),
            P("section", "group"),
            P("section", "group"),
            P("section", "group", None),
            P("section", "group"),
            P("section", "group", None),
            P("section", "group"),
        ),
        check_vma=False,
    )
```

profile of v0, /device:TPU:1, one launch (start us, length us, event | category | flops | bytes accessed | tf_op | source)
XLA Modules:
  0.0 1631.9 jit_solution(1828727543704199468)
XLA Ops:
  12.7 3.7 concatenate.42
  18.2 193.3 %all-gather.9.cloned.1.call-done = bf16[1,768,6151]{2,1,0:T(8,128)(2,1)} async-done(((bf16[1,96,6151]{2,1,0:T(8,128)(2,1)}), bf16[1,768,6151]{2,1,0:T(8,128)(2,1)}) %all-gather.9.cloned.1.call-update) | async-done | bytes 9447952 | tf_op jit(solution)/shard_map/all_gather | solution.py:15
  213.8 3.4 fusion.284
  220.8 21.5 %all-reduce = bf16[768]{0:T(1024)(128)(2,1)S(1)} all-reduce(bf16[768]{0:T(1024)(128)(2,1)S(1)} %dynamic-update-slice), channel_id=1, replica_groups=mesh['section'=2,'group'=8,'replica'=8] {'group'}, use_global_device_ids=true, to_apply=%add | all-reduce | flops 768 | bytes 3072
  247.0 83.1 %all-gather.13.cloned.1.call-done = bf16[1,3072,769]{2,1,0:T(8,128)(2,1)} async-done(((bf16[1,384,769]{2,1,0:T(8,128)(2,1)}), bf16[1,3072,769]{2,1,0:T(8,128)(2,1)}) %all-gather.13.cloned.1.call-update) | async-done | bytes 4724752 | tf_op jit(solution)/shard_map/all_gather | solution.py:15
  331.7 71.8 %all-gather.11.cloned.1.call-done = bf16[1024,1536]{1,0:T(8,128)(2,1)} async-done(((bf16[128,1536]{1,0:T(8,128)(2,1)}), bf16[1024,1536]{1,0:T(8,128)(2,1)}) %all-gather.11.cloned.1.call-update) | async-done | bytes 3145744 | tf_op jit(solution)/shard_map/all_gather | solution.py:29
  403.5 3.2 fusion.414
  411.0 33.6 %while.117 = (s32[]{:T(128)}, bf16[12,128,64]{1,2,0:T(8,128)(2,1)S(1)}, f32[12,128]{1,0:T(8,128)S(1)}, bf16[12,128,64]{1,2,0:T(8,128)(2,1)S(1)}, bf16[12,1024,64...) while((s32[]{:T(128)}, ...), condition=%wide.region_5.6_spmd.clone, body=%wide.region_2.5_spmd.clone.sunk | while | flops 34996096 | bytes 1896569 | solution.py:250
  447.0 4.1 convolution_add_fusion.2
  451.2 4.7 fusion.296
  459.6 3.4 fusion.283
  469.9 67.3 %all-gather.15.cloned.1.call-done = bf16[1024,1536]{1,0:T(8,128)(2,1)} async-done(((bf16[128,1536]{1,0:T(8,128)(2,1)}), bf16[1024,1536]{1,0:T(8,128)(2,1)}) %all-gather.15.cloned.1.call-update) | async-done | bytes 3145744 | tf_op jit(solution)/shard_map/all_gather | solution.py:29
  537.1 3.7 fusion.413
  546.1 33.7 %while.118 = (s32[]{:T(128)}, bf16[12,128,64]{1,2,0:T(8,128)(2,1)S(1)}, f32[12,128]{1,0:T(8,128)S(1)}, bf16[12,128,64]{1,2,0:T(8,128)(2,1)S(1)}, bf16[12,1024,64...) while((s32[]{:T(128)}, ...), condition=%wide.region_13.14_spmd.clone, body=%wide.region_10.13_spmd.clone.sunk | while | flops 34996096 | bytes 1896569 | solution.py:250
  582.1 4.1 convolution_add_fusion.1
  586.2 5.2 fusion.295
  596.7 3.4 fusion.282
  618.0 6.8 convert_reduce_fusion.3
  637.8 35.7 %all-gather.17.cloned.1.call-done = bf16[1024,1536]{1,0:T(8,128)(2,1)} async-done(((bf16[128,1536]{1,0:T(8,128)(2,1)}), bf16[1024,1536]{1,0:T(8,128)(2,1)}) %all-gather.17.cloned.1.call-update) | async-done | bytes 3145744 | tf_op jit(solution)/shard_map/all_gather | solution.py:29
  673.5 7.4 broadcast_select_fusion
  686.2 33.6 %while.119 = (s32[]{:T(128)}, bf16[12,128,64]{1,2,0:T(8,128)(2,1)S(1)}, f32[12,128]{1,0:T(8,128)S(1)}, bf16[12,128,64]{1,2,0:T(8,128)(2,1)}, bf16[12,1024,64]{1,...) while((s32[]{:T(128)}, ...), condition=%wide.region_21.22_spmd.clone, body=%wide.region_18.21_spmd.clone.sunk | while | flops 34996096 | bytes 1896569 | solution.py:250
  723.9 5.1 multiply_reduce_fusion.5
  741.9 52.6 %while.120 = (s32[]{:T(128)}, bf16[12,128,64]{1,2,0:T(8,128)(2,1)}, f32[12,128]{1,0:T(8,128)S(1)}, bf16[12,128,64]{1,2,0:T(8,128)(2,1)}, bf16[12,1024,64]{1,2,0:...) while((s32[]{:T(128)}, bf16[12,128,64]{1,2,0:T(8,128)(2,1)}, ...), condition=%wide.region_30.31_spmd.clone, body=%wide.region_28.30_spmd.clone.sunk | while | flops 51781504 | bytes 3092109 | solution.py:183
  797.1 2.6 copy.190
  799.7 22.1 %all_gather.43 = f32[24,1024]{1,0:T(8,128)S(1)} all-gather(f32[24,128]{1,0:T(8,128)S(1)} %pad_maximum_fusion.16), channel_id=1, replica_groups=mesh['section'=2,'group'=8,'replica'=8] {'group'}, dimensions={1}, use_global_device_ids=true | all-gather | bytes 110592 | tf_op jit(solution)/shard_map/all_gather | solution.py:29
  825.5 5.3 convolution_add_fusion
  830.9 3.7 fusion.412
  841.2 70.2 %while.121 = (s32[]{:T(128)}, bf16[12,128,64]{1,2,0:T(8,128)(2,1)}, bf16[12,128,64]{1,2,0:T(8,128)(2,1)}, bf16[12,1024,64]{1,2,0:T(8,128)(2,1)}, bf16[12,128,64]...) while((s32[]{:T(128)}, bf16[12,128,64]{1,2,0:T(8,128)(2,1)}, ...), condition=%wide.region_32.33_spmd.clone, body=%wide.region_31.32_spmd.clone.sunk | while | flops 68427776 | bytes 2229385 | solution.py:207
  911.4 5.1 multiply_reduce_fusion.8
  917.9 9.0 collective-permute-start.2
  928.1 6.0 convert_reduce_fusion.2
  934.1 5.4 multiply_reduce_fusion.4
  944.1 45.6 %while.122 = (s32[]{:T(128)}, bf16[12,128,64]{1,2,0:T(8,128)(2,1)S(1)}, f32[12,128]{1,0:T(8,128)S(1)}, bf16[12,128,64]{1,2,0:T(8,128)(2,1)}, bf16[12,1024,64]{1,...) while((s32[]{:T(128)}, ...), condition=%wide.region_43.44_spmd.clone, body=%wide.region_41.43_spmd.clone.sunk | while | flops 51781504 | bytes 3092109 | solution.py:183
  989.8 22.8 %all_gather.45 = f32[24,1024]{1,0:T(8,128)S(1)} all-gather(f32[24,128]{1,0:T(8,128)S(1)} %pad_maximum_fusion.17), channel_id=1, replica_groups=mesh['section'=2,'group'=8,'replica'=8] {'group'}, dimensions={1}, use_global_device_ids=true | all-gather | bytes 110592 | tf_op jit(solution)/shard_map/all_gather | solution.py:29
  1014.6 3.7 fusion.411
  1020.9 2.6 copy.197
  1025.0 70.3 %while.123 = (s32[]{:T(128)}, bf16[12,128,64]{1,2,0:T(8,128)(2,1)}, bf16[12,128,64]{1,2,0:T(8,128)(2,1)}, bf16[12,1024,64]{1,2,0:T(8,128)(2,1)}, bf16[12,128,64]...) while((s32[]{:T(128)}, bf16[12,128,64]{1,2,0:T(8,128)(2,1)}, ...), condition=%wide.region_45.46_spmd.clone, body=%wide.region_44.45_spmd.clone.sunk | while | flops 68427776 | bytes 2229385 | solution.py:207
  1095.3 5.2 multiply_reduce_fusion.7
  1101.6 6.8 collective-permute-start.3
  1109.6 6.0 convert_reduce_fusion.1
  1115.7 5.3 multiply_reduce_fusion.3
  1129.6 6.6 fusion.331
  1136.1 5.8 fusion.302
  1147.2 2.6 copy.204
  1149.8 2.6 copy.206
  1155.1 4.2 fusion.321
  1162.2 6.4 fusion.329
  1168.7 5.8 fusion.300
  1174.6 4.2 fusion.320
  1178.9 9.9 add_convert_fusion.1
  1189.5 45.7 %while.124 = (s32[]{:T(128)}, bf16[12,128,64]{1,2,0:T(8,128)(2,1)S(1)}, f32[12,128]{1,0:T(8,128)S(1)}, bf16[12,128,64]{1,2,0:T(8,128)(2,1)}, bf16[12,1024,64]{1,...) while((s32[]{:T(128)}, ...), condition=%wide.region_56.57_spmd.clone, body=%wide.region_54.56_spmd.clone.sunk | while | flops 51781504 | bytes 3092109 | solution.py:183
  1235.2 27.9 %all_gather.47 = f32[24,1024]{1,0:T(8,128)S(1)} all-gather(f32[24,128]{1,0:T(8,128)S(1)} %pad_maximum_fusion.18), channel_id=1, replica_groups=mesh['section'=2,'group'=8,'replica'=8] {'group'}, dimensions={1}, use_global_device_ids=true | all-gather | bytes 110592 | tf_op jit(solution)/shard_map/all_gather | solution.py:29
  1263.1 10.4 add_convert_fusion
  1273.9 3.3 fusion.410
  1277.2 2.6 copy.211
  1281.6 47.1 %while.125 = (s32[]{:T(128)}, bf16[12,128,64]{1,2,0:T(8,128)(2,1)S(1)}, bf16[12,128,64]{1,2,0:T(8,128)(2,1)S(1)}, bf16[12,1024,64]{1,2,0:T(8,128)(2,1)}, bf16[12...) while((s32[]{:T(128)}, ...), condition=%wide.region_58.59_spmd.clone, body=%wide.region_57.58_spmd.clone.sunk | while | flops 68427776 | bytes 2229385 | solution.py:207
  1328.7 8.4 add_convert_fusion.2
  1339.4 4.7 fusion.298
  1346.2 4.2 multiply_reduce_fusion.6
  1350.5 33.8 %all-reduce.12 = (bf16[768]{0:T(1024)(128)(2,1)S(1)}, bf16[768]{0:T(1024)(128)(2,1)S(1)}, bf16[768]{0:T(1024)(128)(2,1)S(1)}, bf16[768]{0:T(1024)(128)(2,1)S(1)}...) all-reduce(bf16[768]{0:T(1024)(128)(2,1)S(1)} %add_convert_fusion.2, ...), channel_id=2, replica_groups=mesh['section'=2,'group'=8,'replica'=8] {'group'}, use_global_device_ids=true, to_apply=%region_66.67.clone | all-reduce | flops 9216 | bytes 36864
  1384.3 62.6 %reduce-scatter.11.cloned.1.call-done = bf16[384,768]{1,0:T(8,128)(2,1)} async-done(((bf16[3072,768]{1,0:T(8,128)(2,1)}), bf16[384,768]{1,0:T(8,128)(2,1)}) %reduce-scatter.11.cloned.1.call-update) | async-done | bytes 589840 | tf_op jit(solution)/shard_map/reduce_scatter | solution.py:391
  1446.9 80.8 %reduce-scatter.5.cloned.1.call-done = bf16[96,2304]{1,0:T(8,128)(2,1)} async-done(((bf16[768,2304]{1,0:T(8,128)(2,1)}), bf16[96,2304]{1,0:T(8,128)(2,1)}) %reduce-scatter.5.cloned.1.call-update) | async-done | bytes 442384 | tf_op jit(solution)/shard_map/reduce_scatter | solution.py:391
  1528.4 21.5 %all-reduce.10 = (bf16[1,96]{1,0:T(2,128)(2,1)S(1)}, bf16[1,96]{1,0:T(2,128)(2,1)S(1)}, bf16[1,96]{1,0:T(2,128)(2,1)S(1)}, bf16[1,96]{1,0:T(2,128)(2,1)S(1)}, bf...) all-reduce(bf16[1,96]{1,0:T(2,128)(2,1)S(1)} %dynamic-slice_bitcast, ...), channel_id=1, replica_groups=mesh['section'=2,'group'=8,'replica'=8] {'replica'}, use_global_device_ids=true, to_apply=%region_67.68 | all-reduce | flops 1152 | bytes 4608 | tf_op jit(solution)/shard_map/psum | solution.py:394
  1555.7 63.2 %all-reduce.15.cloned.1.call-done = (bf16[1,96,2304]{2,1,0:T(8,128)(2,1)}, bf16[1,96,768]{2,1,0:T(8,128)(2,1)}, bf16[1,96,3072]{2,1,0:T(8,128)(2,1)}, bf16[1,384,768]{2,1,0:T(8,128)(2,1)}) async-done(((bf16[1,96,2304]{2,1,0:T(8,128)(2,1)}, bf16[1,96,768]{2,1,0:T(8,128)(2,1)}, bf16[1,96,3072]{2,1,0:T(8,128)(2,1)}, bf16[1,384,768]{2,1,0:T(8,128)(2,1)}), (bf16[1,96,2304]{2,1,0:T(8,128)(2,1)}, ...) | async-done | bytes 1769488 | tf_op jit(solution)/shard_map/psum | solution.py:394
  (1057 shorter events, 587.9 us)
Async XLA Ops:
  7.2 204.4 %all-gather.9.cloned.1.call-start = ((), (), s32[]{:S(2)}) async-start(), calls=%async_computation.4 | async-start | bytes 10838016 | tf_op jit(solution)/shard_map/all_gather | solution.py:15
  16.4 313.7 %all-gather.13.cloned.1.call-start = ((), (), s32[]{:S(2)}) async-start(), calls=%async_computation.6 | async-start | bytes 6193152 | tf_op jit(solution)/shard_map/all_gather | solution.py:15
  17.8 385.7 %all-gather.11.cloned.1.call-start = ((), (), s32[]{:S(2)}) async-start(), calls=%async_computation.5 | async-start | bytes 3538944 | tf_op jit(solution)/shard_map/all_gather | solution.py:29
  213.8 365.9 %copy-start.105 = (f32[768]{0:T(1024)}, f32[768]{0:T(1024)S(1)}, u32[]{:S(2)}) copy-start(f32[768]{0:T(1024)S(1)} %get-tuple-element.881) | copy-start | bytes 9220
  217.3 25.0 %copy-start.113 = (s32[2,3]{1,0:T(2,128)S(1)}, s32[2,3]{1,0:T(2,128)}, u32[]{:S(2)}) copy-start(s32[2,3]{1,0:T(2,128)} %param.36) | copy-start | bytes 76
  218.3 244.7 %copy-start.28 = (bf16[128,768]{1,0:T(8,128)(2,1)}, bf16[128,768]{1,0:T(8,128)(2,1)S(1)}, u32[]{:S(2)}) copy-start(bf16[128,768]{1,0:T(8,128)(2,1)S(1)} %get-tuple-element.1219) | copy-start | bytes 589828
  218.3 244.7 %copy-start.30 = (bf16[128,768]{1,0:T(8,128)(2,1)}, bf16[128,768]{1,0:T(8,128)(2,1)S(1)}, u32[]{:S(2)}) copy-start(bf16[128,768]{1,0:T(8,128)(2,1)S(1)} %get-tuple-element.1220) | copy-start | bytes 589828
  219.2 317.9 %all-gather.15.cloned.1.call-start = ((), (), s32[]{:S(2)}) async-start(), calls=%async_computation.7 | async-start | bytes 3538944 | tf_op jit(solution)/shard_map/all_gather | solution.py:29
  242.3 208.9 %copy-start.110 = (f32[768]{0:T(1024)}, f32[768]{0:T(1024)S(1)}, u32[]{:S(2)}) copy-start(f32[768]{0:T(1024)S(1)} %add.844) | copy-start | bytes 9220
  444.7 6.5 copy-start.70
  455.9 7.1 copy-start.81
  455.9 3.3 collective-permute-start
  466.5 207.1 %all-gather.17.cloned.1.call-start = ((), (), s32[]{:S(2)}) async-start(), calls=%async_computation.8 | async-start | bytes 3538944 | tf_op jit(solution)/shard_map/all_gather | solution.py:29
  579.7 6.5 copy-start.71
  591.5 8.6 copy-start.83
  591.5 3.3 collective-permute-start.1
  594.9 125.0 %copy-start.18 = (bf16[128,768]{1,0:T(8,128)(2,1)}, bf16[128,768]{1,0:T(8,128)(2,1)S(1)}, u32[]{:S(2)}) copy-start(bf16[128,768]{1,0:T(8,128)(2,1)S(1)} %collective-permute-done.1) | copy-start | bytes 589828
  600.2 6.7 copy-start.103
  601.3 14.1 copy-start.33
  602.8 228.0 %all-gather.19.cloned.1.call-start = ((), (), s32[]{:S(2)}) async-start(), calls=%async_computation.9 | async-start | bytes 3538944 | tf_op jit(solution)/shard_map/all_gather | solution.py:29
  624.8 7.3 copy-start.29
  635.4 45.5 %copy-start.116 = (f32[128]{0:T(128)}, f32[128]{0:T(128)S(1)}, u32[]{:S(2)}) copy-start(f32[128]{0:T(128)S(1)} %broadcast_multiply_fusion.2) | copy-start | bytes 1540
  635.4 45.5 %copy-start.120 = (f32[128]{0:T(128)}, f32[128]{0:T(128)S(1)}, u32[]{:S(2)}) copy-start(f32[128]{0:T(128)S(1)} %broadcast_multiply_fusion.4) | copy-start | bytes 1540
  636.8 44.2 %copy-start.138 = (f32[128]{0:T(128)}, f32[128]{0:T(128)S(1)}, u32[]{:S(2)}) copy-start(f32[128]{0:T(128)S(1)} %get-tuple-element.1283) | copy-start | bytes 1540
  636.8 44.2 %copy-start.142 = (f32[128]{0:T(128)}, f32[128]{0:T(128)S(1)}, u32[]{:S(2)}) copy-start(f32[128]{0:T(128)S(1)} %get-tuple-element.1284) | copy-start | bytes 1540
  686.2 33.7 %copy-start.106 = (f32[768]{0:T(1024)S(1)}, f32[768]{0:T(1024)}, u32[]{:S(2)}) copy-start(f32[768]{0:T(1024)} %copy-done.105) | copy-start | bytes 9220
  723.7 100.5 %copy-start.25 = (f32[128,768]{1,0:T(8,128)}, f32[128,768]{1,0:T(8,128)S(1)}, u32[]{:S(2)}) copy-start(f32[128,768]{1,0:T(8,128)S(1)} %get-tuple-element.1146) | copy-start | bytes 1179652
  735.9 278.7 %all-gather.21.cloned.1.call-start = ((), (), s32[]{:S(2)}) async-start(), calls=%async_computation.10 | async-start | bytes 3538944 | tf_op jit(solution)/shard_map/all_gather | solution.py:29
  797.1 27.1 %copy-start.147 = (f32[128]{0:T(128)S(1)}, f32[128]{0:T(128)}, u32[]{:S(2)}) copy-start(f32[128]{0:T(128)} %get-tuple-element.1145) | copy-start | bytes 1540
  824.2 6.7 copy-start.118
  841.2 70.2 %copy-start.121 = (f32[128]{0:T(128)S(1)}, f32[128]{0:T(128)}, u32[]{:S(2)}) copy-start(f32[128]{0:T(128)} %copy-done.120) | copy-start | bytes 1540
  841.2 70.2 %copy-start.141 = (f32[128]{0:T(128)S(1)}, f32[128]{0:T(128)}, u32[]{:S(2)}) copy-start(f32[128]{0:T(128)} %fusion.359) | copy-start | bytes 1540
  916.6 10.4 copy-start.144
  916.6 11.5 copy-start.5
  917.9 10.1 copy-start.64
  917.9 10.1 collective-permute-start.2
  943.6 330.3 %all-gather.23.cloned.1.call-start = ((), (), s32[]{:S(2)}) async-start(), calls=%async_computation.11 | async-start | bytes 3538944 | tf_op jit(solution)/shard_map/all_gather | solution.py:29
  989.8 28.5 %copy-start.48 = (bf16[12,128,64]{1,2,0:T(8,128)(2,1)}, bf16[12,128,64]{1,2,0:T(8,128)(2,1)S(1)}, u32[]{:S(2)}) copy-start(bf16[12,128,64]{1,2,0:T(8,128)(2,1)S(1)} %get-tuple-element.442) | copy-start | bytes 589828
  1025.0 70.3 %copy-start.117 = (f32[128]{0:T(128)S(1)}, f32[128]{0:T(128)}, u32[]{:S(2)}) copy-start(f32[128]{0:T(128)} %copy-done.116) | copy-start | bytes 1540
  1025.0 70.3 %copy-start.137 = (f32[128]{0:T(128)S(1)}, f32[128]{0:T(128)}, u32[]{:S(2)}) copy-start(f32[128]{0:T(128)} %fusion.361) | copy-start | bytes 1540
  1095.3 14.2 copy-start.11
  1100.5 8.0 copy-start.140
  1100.5 9.1 copy-start.2
  1100.5 9.1 copy-start.6
  1101.6 7.9 copy-start.68
  1101.6 7.9 collective-permute-start.3
  1121.4 8.1 copy-start.90
  1121.4 8.1 copy-start.92
  1121.4 8.1 copy-start.101
  1125.6 258.7 %reduce-scatter.7.cloned.1.call-start = ((), (), s32[]{:S(2)}) async-start(), calls=%async_computation.13 | async-start | bytes 1327104 | tf_op jit(solution)/shard_map/reduce_scatter | solution.py:391
  1129.6 6.6 copy-start.3
  1129.6 6.6 copy-start.12
  1161.9 222.4 %reduce-scatter.9.cloned.1.call-start = ((), (), s32[]{:S(2)}) async-start(), calls=%async_computation.14 | async-start | bytes 5308416 | tf_op jit(solution)/shard_map/reduce_scatter | solution.py:391
  1188.8 258.1 %reduce-scatter.11.cloned.1.call-start = ((), (), s32[]{:S(2)}) async-start(), calls=%async_computation.15 | async-start | bytes 5308416 | tf_op jit(solution)/shard_map/reduce_scatter | solution.py:391
  1189.5 73.6 %copy-start.4 = (f32[128,3072]{1,0:T(8,128)S(1)}, f32[128,3072]{1,0:T(8,128)}, u32[]{:S(2)}) copy-start(f32[128,3072]{1,0:T(8,128)} %copy-done.1) | copy-start | bytes 4718596
  1189.5 73.6 %copy-start.61 = (bf16[128,768]{1,0:T(8,128)(2,1)S(1)}, bf16[128,768]{1,0:T(8,128)(2,1)}, u32[]{:S(2)}) copy-start(bf16[128,768]{1,0:T(8,128)(2,1)} %copy-done.60) | copy-start | bytes 589828
  1273.6 254.2 %reduce-scatter.5.cloned.1.call-start = ((), (), s32[]{:S(2)}) async-start(), calls=%async_computation.12 | async-start | bytes 3981312 | tf_op jit(solution)/shard_map/reduce_scatter | solution.py:391
  1281.6 47.2 %copy-start.96 = (f32[128]{0:T(128)S(1)}, f32[128]{0:T(128)}, u32[]{:S(2)}) copy-start(f32[128]{0:T(128)} %copy-done.94) | copy-start | bytes 1540
  1281.6 47.2 %copy-start.99 = (f32[128]{0:T(128)S(1)}, f32[128]{0:T(128)}, u32[]{:S(2)}) copy-start(f32[128]{0:T(128)} %copy-done.97) | copy-start | bytes 1540
  1328.7 8.5 copy-start.56
  1337.3 281.7 %all-reduce.15.cloned.1.call-start = ((), (), s32[]{:S(2)}) async-start(), calls=%async_computation.16 | async-start | bytes 3538944 | tf_op jit(solution)/shard_map/psum | solution.py:394
  1350.4 204.4 %copy-start.17 = (f32[128,768]{1,0:T(8,128)S(1)}, f32[128,768]{1,0:T(8,128)}, u32[]{:S(2)}) copy-start(f32[128,768]{1,0:T(8,128)} %copy-done.15) | copy-start | bytes 1179652
  1350.4 204.4 %copy-start.69 = (bf16[128,768]{1,0:T(8,128)(2,1)S(1)}, bf16[128,768]{1,0:T(8,128)(2,1)}, u32[]{:S(2)}) copy-start(bf16[128,768]{1,0:T(8,128)(2,1)} %copy-done.68) | copy-start | bytes 589828
  1527.8 27.2 %copy-start.66 = (bf16[1,128,768]{2,1,0:T(8,128)(2,1)S(1)}, bf16[1,128,768]{2,1,0:T(8,128)(2,1)}, u32[]{:S(2)}) copy-start(bf16[1,128,768]{2,1,0:T(8,128)(2,1)} %get-tuple-element.1128) | copy-start | bytes 589828
  (102 other events, 344.4 us)
Sparse Core Ops, SparseCore 0:
  16.5 194.9 all-gather.8
  213.7 116.3 all-gather.12
  332.4 71.1 all-gather.10
  466.6 70.5 all-gather.14
  603.0 70.4 all-gather.16
  736.0 71.5 all-gather.18
  943.7 70.7 all-gather.20
  1125.8 69.7 all-gather.22
  1198.5 36.9 reduce-scatter.6
  1237.8 104.5 reduce-scatter.8
  1344.8 102.1 reduce-scatter.10
  1449.2 78.4 reduce-scatter.4
  1530.7 88.1 all-reduce.14
where the time goes:
time: 1650 us; the launch traced here: 1630 us
  waiting for transfers between devices  665 us (40%)
  matrix products  564 us (34%)
  blocking collectives  149 us (9%)
  local copies, waits for them, and re-layouts  132 us (8%)
  other arithmetic  71.7 us (4%)
  between operations  26.5 us (2%)
  starting transfers between devices  20.7 us (1%)
    all_gather x2, waiting for transfers between devices, in_one_piece(): result, at, done = (lax.all_gather(both, axis, axis=dim, tiled=True), 0, [])  276 us
    dot_general x156, matrix products, right_inner(): lax.dot_general(left, right, (((1,), (1,)), ((), ())), preferred_element_...  240 us
    dot_general x84, matrix products, left_inner(): lax.dot_general(left, right, (((0,), (0,)), ((), ())), preferred_element_...  184 us
    all_gather x6, waiting for transfers between devices, side_by_side(): lax.all_gather(both, axis, axis=dim, tiled=True)  176 us
    reduce_scatter x4, waiting for transfers between devices, body(): lax.psum_scatter(shortened(totals), 'group', scatter_dimension=0, tiled=T...  143 us
    dot_general x84, matrix products, matmul(): return jnp.dot(left, right, preferred_element_type=jnp.float32)  139 us
    all_gather x3, blocking collectives, side_by_side(): lax.all_gather(both, axis, axis=dim, tiled=True)  72.7 us
    psum x1, waiting for transfers between devices, body(): lax.psum(shortened(pieces), 'replica')  63.2 us
  transfers between devices with their start and end apart: 17, of which 13 were waited for; matrix products, arithmetic and copies ran while one was open for 22% of the time, Pallas kernels for 0%

commit v1 on v0

v1 whole, which is shorter than its diff:
```python
import functools

import jax
import jax.numpy as jnp
from jax import lax
from jax.experimental import pallas as pl
from jax.experimental.pallas import tpu as pltpu
from jax.sharding import PartitionSpec as P

WIDTH = 768
GROUPS = 8
PAIRS = 6
SEQ = 1024
ROWS = 128
BLOCK = 256
SHARD = 96
EPSILON = 1e-05
VMEM_BYTES = 40 * 1024 * 1024
GELU_C = 0.7978845608028654
BF = jnp.bfloat16
F32 = jnp.float32


def torus_pairs(move):
    pairs = []
    for source in range(64):
        group, replica = divmod(source, 8)
        x, z_lo = divmod(group, 2)
        z_hi, y = divmod(replica, 4)
        x, y, z = move(x, y, z_hi * 2 + z_lo)
        pairs.append((source, ((x % 4) * 2 + z % 2) * 8 + (z % 4) // 2 * 4 + y % 4))
    return pairs


def along_x(value, by):
    return lax.ppermute(value, ("group", "replica"), torus_pairs(lambda x, y, z: (x + by, y, z)))


def along_y(value, by):
    return lax.ppermute(value, ("group", "replica"), torus_pairs(lambda x, y, z: (x, y + by, z)))


def along_z(value, by):
    return lax.ppermute(value, ("group", "replica"), torus_pairs(lambda x, y, z: (x, y, z + by)))


def swap(value):
    return lax.ppermute(value, "section", [(0, 1), (1, 0)])


def gather_group(shard):
    group = lax.axis_index("group")
    x, z = group // 2, group % 2
    blocks = shard.shape[0]
    half = blocks // 2
    full = jnp.zeros((blocks, GROUPS) + shard.shape[1:], shard.dtype)

    def put(full, piece, dx, flip, first):
        at = lax.rem(x + dx + 4, 4) * 2 + (1 - z if flip else z)
        return lax.dynamic_update_slice(full, piece[:, None], (first, at, 0, 0))

    low, high = shard[:half], shard[half:]
    left = along_x(shard, 1)
    right = along_x(shard, -1)
    far_low = along_x(left[:half], 1)
    far_high = along_x(right[half:], -1)
    z_low = along_z(low, 1)
    z_high = along_z(high, -1)
    z_left = along_z(left, 1)
    z_right = along_z(right, -1)
    z_far_low = along_z(far_low, 1)
    z_far_high = along_z(far_high, -1)
    full = put(full, shard, 0, False, 0)
    full = put(full, left, -1, False, 0)
    full = put(full, right, 1, False, 0)
    full = put(full, far_low, 2, False, 0)
    full = put(full, far_high, 2, False, half)
    full = put(full, z_low, 0, True, 0)
    full = put(full, z_high, 0, True, half)
    full = put(full, z_left, -1, True, 0)
    full = put(full, z_right, 1, True, 0)
    full = put(full, z_far_low, 2, True, 0)
    full = put(full, z_far_high, 2, True, half)
    return full


def add(left, right):
    return left.astype(F32) + right.astype(F32)


def ring_sum(pieces, place, along):
    two = pieces(2)
    half = two.shape[0] // 2
    from_left = along(two[:half], 1)
    from_right = along(two[half:], -1)
    one, minus = pieces(1), pieces(3)
    one = jnp.concatenate([add(one[:half], from_left).astype(BF), one[half:]], axis=0)
    minus = jnp.concatenate([minus[:half], add(minus[half:], from_right).astype(BF)], axis=0)
    return pieces(0).astype(F32) + along(one, 1).astype(F32) + along(minus, -1).astype(F32)


def reduce_group(parts):
    group = lax.axis_index("group")
    x, z = group // 2, group % 2
    blocks, _, rows, width = parts.shape
    half = blocks // 2
    parts = parts.reshape(blocks, 4, 2, rows, width)
    away = lax.dynamic_index_in_dim(parts, 1 - z, 2, keepdims=False)
    own = lax.dynamic_index_in_dim(parts, z, 2, keepdims=False)
    low = add(own[:half], along_z(away[:half], 1)).astype(BF)
    high = add(own[half:], along_z(away[half:], -1)).astype(BF)
    own = jnp.concatenate([low, high], axis=0)

    def piece(k):
        return lax.dynamic_index_in_dim(own, lax.rem(x + k, 4), 1, keepdims=False)

    return ring_sum(piece, x, along_x)


def reduce_replica(total):
    y = lax.rem(lax.axis_index("replica"), 4)
    rows, width = total.shape
    quarter = rows // 4
    half = quarter // 2
    low = total.astype(BF)

    def piece(k):
        return lax.dynamic_slice(low, (lax.rem(y + k, 4) * quarter, 0), (quarter, width))

    mine = ring_sum(piece, y, along_y).astype(BF)
    mine = add(mine, along_z(mine, 2)).astype(BF)
    left = along_y(mine, 1)
    right = along_y(mine, -1)
    far_low = along_y(left[:half], 1)
    far_high = along_y(right[half:], -1)
    far = jnp.concatenate([far_low, far_high], axis=0)
    full = jnp.zeros((4, quarter, width), BF)
    for piece_k, k in ((mine, 0), (left, 3), (right, 1), (far, 2)):
        full = lax.dynamic_update_slice(full, piece_k[None], (lax.rem(y + k, 4), 0, 0))
    return full.reshape(rows, width)


def dot(left, right):
    return jnp.dot(left, right, preferred_element_type=F32)


def dot_rows(left, right):
    return lax.dot_general(left, right, (((0,), (0,)), ((), ())), preferred_element_type=F32)


def dot_columns(left, right):
    return lax.dot_general(left, right, (((1,), (1,)), ((), ())), preferred_element_type=F32)


def normalized(rows):
    center = rows - jnp.mean(rows, axis=-1, keepdims=True)
    scale = lax.rsqrt(jnp.mean(center * center, axis=-1, keepdims=True) + EPSILON)
    return center * scale, scale


def norm_back(grad, gain, unit, scale):
    inner = grad * gain
    return scale * (
        inner
        - jnp.mean(inner, axis=-1, keepdims=True)
        - unit * jnp.mean(inner * unit, axis=-1, keepdims=True)
    )


def column_sums(rows):
    return jnp.sum(rows, axis=0, keepdims=True)


def put_pairs(ref, rows, index=None):
    for pair in range(PAIRS):
        part = rows[:, pair * 128 : (pair + 1) * 128]
        if index is None:
            ref[pair] = part
        else:
            ref[pair, index] = part
    for pair in range(PAIRS, GROUPS):
        empty = jnp.zeros((ROWS, 128), BF)
        if index is None:
            ref[pair] = empty
        else:
            ref[pair, index] = empty


def pre_forward(x_ref, vec_ref, first_ref, value_ref, n1_ref, send_ref):
    unit, _ = normalized(x_ref[...].astype(F32))
    n1 = (unit * vec_ref[0:1, :] + vec_ref[1:2, :]).astype(BF)
    n1_ref[...] = n1
    put_pairs(send_ref, (dot(n1, first_ref[0]) + vec_ref[2:3, :]).astype(BF), 0)
    put_pairs(send_ref, dot(n1, first_ref[1]).astype(BF), 1)
    put_pairs(send_ref, (dot(n1, value_ref[0]) + vec_ref[3:4, :]).astype(BF), 2)


def visible(length_ref, at, columns):
    first_end = length_ref[0]
    second_end = first_end + length_ref[1]
    row = lax.broadcasted_iota(jnp.int32, (BLOCK, 1), 0) + at
    start = jnp.where(row >= second_end, second_end, jnp.where(row >= first_end, first_end, 0))
    column = lax.broadcasted_iota(jnp.int32, (BLOCK, columns), 1)
    return (column >= start) & (column <= row)


def of_head(rows, head):
    lane = lax.broadcasted_iota(jnp.int32, rows.shape, 1)
    keep = lane < 64 if head == 0 else lane >= 64
    return jnp.where(keep, rows, jnp.zeros_like(rows))


def both_heads(first, second):
    lane = lax.broadcasted_iota(jnp.int32, first.shape, 1)
    return jnp.where(lane < 64, first, second)


def attend_forward(length_ref, qkv_ref, out_ref, logsum_ref):
    for block in range(SEQ // BLOCK):
        keys = (block + 1) * BLOCK
        query = qkv_ref[2 * block : 2 * block + 2, 0].reshape(BLOCK, 128)
        query = (query.astype(F32) * 0.125).astype(BF)
        key = qkv_ref[: 2 * block + 2, 1].reshape(keys, 128)
        value = qkv_ref[: 2 * block + 2, 2].reshape(keys, 128)
        allowed = visible(length_ref, block * BLOCK, keys)
        mixed, sums = [], []
        for head in range(2):
            scores = dot_columns(of_head(query, head), key)
            scores = jnp.where(allowed, scores, -1e30)
            maximum = jnp.max(scores, axis=-1, keepdims=True)
            expo = jnp.exp(scores - maximum)
            total = jnp.sum(expo, axis=-1, keepdims=True)
            mixed.append(dot((expo * (1.0 / total)).astype(BF), value))
            sums.append(jnp.broadcast_to(maximum + jnp.log(total), (BLOCK, 128)))
        out_ref[2 * block : 2 * block + 2] = both_heads(*mixed).astype(BF).reshape(2, 128, 128)
        logsum_ref[block * BLOCK : (block + 1) * BLOCK, :] = both_heads(*sums)


def attend_backward(length_ref, qkv_ref, grad_ref, logsum_ref, out_ref, key_acc, value_acc):
    key_acc[...] = jnp.zeros_like(key_acc)
    value_acc[...] = jnp.zeros_like(value_acc)
    for block in range(SEQ // BLOCK):
        keys = (block + 1) * BLOCK
        query = qkv_ref[2 * block : 2 * block + 2, 0].reshape(BLOCK, 128)
        query = (query.astype(F32) * 0.125).astype(BF)
        grad = grad_ref[2 * block : 2 * block + 2].reshape(BLOCK, 128)
        key = qkv_ref[: 2 * block + 2, 1].reshape(keys, 128)
        value = qkv_ref[: 2 * block + 2, 2].reshape(keys, 128)
        allowed = visible(length_ref, block * BLOCK, keys)
        grad_query = []
        for head in range(2):
            query_one, grad_one = of_head(query, head), of_head(grad, head)
            logsum = logsum_ref[block * BLOCK : (block + 1) * BLOCK, 64 * head : 64 * head + 1]
            scores = jnp.where(allowed, dot_columns(query_one, key), -1e30)
            probs = jnp.exp(scores - logsum)
            grad_probs = dot_columns(grad_one, value)
            delta = jnp.sum(probs * grad_probs, axis=-1, keepdims=True)
            grad_scores = (probs * (grad_probs - delta)).astype(BF)
            grad_query.append(dot(grad_scores, key))
            key_acc[:keys, :] += dot_rows(grad_scores, query_one)
            value_acc[:keys, :] += dot_rows(probs.astype(BF), grad_one)
        out = (both_heads(*grad_query) * 0.125).astype(BF)
        out_ref[2 * block : 2 * block + 2, 0] = out.reshape(2, 128, 128)
    out_ref[:, 1] = key_acc[...].astype(BF).reshape(GROUPS, 128, 128)
    out_ref[:, 2] = value_acc[...].astype(BF).reshape(GROUPS, 128, 128)


def proj_block(proj_ref):
    return jnp.concatenate([proj_ref[j, g] for g in range(2) for j in range(4)], axis=0)


def post_forward(
    mixed_ref, x_ref, vec_ref, bias_ref, out_w_ref, fc_ref, proj_ref, y_ref, x1_ref, n2_ref, u_ref, acc
):
    step = pl.program_id(0)

    @pl.when(step == 0)
    def _():
        mixed = jnp.concatenate([mixed_ref[pair] for pair in range(PAIRS)], axis=1)
        x1 = x_ref[...].astype(F32) + dot(mixed, out_w_ref[0]) + vec_ref[4:5, :]
        x1_ref[...] = x1
        unit, _ = normalized(x1)
        n2_ref[...] = (unit * vec_ref[5:6, :] + vec_ref[6:7, :]).astype(BF)
        acc[...] = x1 + vec_ref[7:8, :]

    u = dot(n2_ref[...], fc_ref[0]) + bias_ref[0]
    u_ref[0] = u
    active = 0.5 * u * (1.0 + jnp.tanh(GELU_C * (u + 0.044715 * (u * u * u))))
    acc[...] += dot(active.astype(BF), proj_block(proj_ref))

    @pl.when(step == 3)
    def _():
        y_ref[...] = acc[...].astype(BF)


def post_backward(
    dy_ref,
    u_ref,
    n2_ref,
    x1_ref,
    mixed_ref,
    vec_ref,
    out_w_ref,
    fc_ref,
    proj_ref,
    dx1_ref,
    send_ref,
    dout_ref,
    dfc_ref,
    dproj_ref,
    dvec_ref,
    dbias_ref,
    acc,
):
    step = pl.program_id(0)
    dy = dy_ref[...].astype(F32)
    low = dy.astype(BF)

    @pl.when(step == 0)
    def _():
        acc[...] = jnp.zeros_like(acc)

    u = u_ref[0]
    square = u * u
    tanh = jnp.tanh(GELU_C * (u + 0.044715 * (square * u)))
    active = (0.5 * u * (1.0 + tanh)).astype(BF)
    slope = 0.5 * (1.0 + tanh) + 0.5 * u * (1.0 - tanh * tanh) * (
        GELU_C * (1.0 + 3.0 * 0.044715 * square)
    )
    du = (dot_columns(low, proj_block(proj_ref)) * slope).astype(BF)
    dproj = dot_rows(active, low).astype(BF)
    for g in range(2):
        for j in range(4):
            at = (g * 4 + j) * SHARD
            dproj_ref[j, g] = dproj[at : at + SHARD]
    dfc_ref[0] = dot_rows(n2_ref[...], du).astype(BF)
    dbias_ref[0] = column_sums(du.astype(F32))
    acc[...] += dot_columns(du, fc_ref[0])

    @pl.when(step == 3)
    def _():
        dn2 = acc[...]
        unit, scale = normalized(x1_ref[...])
        dx1 = dy + norm_back(dn2, vec_ref[5:6, :], unit, scale)
        dx1_ref[...] = dx1
        back = dx1.astype(BF)
        mixed = jnp.concatenate([mixed_ref[pair] for pair in range(PAIRS)], axis=1)
        dout_ref[...] = dot_rows(mixed, back).astype(BF)
        put_pairs(send_ref, dot_columns(back, out_w_ref[0]).astype(BF))
        dvec_ref[0:4, :] = jnp.zeros((4, WIDTH), F32)
        dvec_ref[4:5, :] = column_sums(back.astype(F32))
        dvec_ref[5:6, :] = column_sums(dn2 * unit)
        dvec_ref[6:7, :] = column_sums(dn2)
        dvec_ref[7:8, :] = column_sums(low.astype(F32))


def pre_backward(
    grads_ref, n1_ref, x_ref, dx1_ref, vec_ref, first_ref, value_ref, dx_ref, dfirst_ref, dvalue_ref, dvec_ref
):
    rows = [
        jnp.concatenate([grads_ref[pair, index] for pair in range(PAIRS)], axis=1)
        for index in range(3)
    ]
    n1 = n1_ref[...]
    dn1 = (
        dot_columns(rows[0], first_ref[0])
        + dot_columns(rows[1], first_ref[1])
        + dot_columns(rows[2], value_ref[0])
    )
    dfirst_ref[0] = dot_rows(n1, rows[0]).astype(BF)
    dfirst_ref[1] = dot_rows(n1, rows[1]).astype(BF)
    dvalue_ref[...] = dot_rows(n1, rows[2]).astype(BF)
    unit, scale = normalized(x_ref[...].astype(F32))
    dx_ref[...] = (dx1_ref[...] + norm_back(dn1, vec_ref[0:1, :], unit, scale)).astype(BF)
    dvec_ref[0:1, :] = column_sums(dn1 * unit)
    dvec_ref[1:2, :] = column_sums(dn1)
    dvec_ref[2:3, :] = column_sums(rows[0].astype(F32))
    dvec_ref[3:4, :] = column_sums(rows[2].astype(F32))
    dvec_ref[4:8, :] = jnp.zeros((4, WIDTH), F32)


def whole(*shape):
    return pl.BlockSpec(shape, lambda *_: (0,) * len(shape))


def stepped(*shape):
    return pl.BlockSpec(shape, lambda step: (step,) + (0,) * (len(shape) - 1))


def out(shape, kind):
    return jax.ShapeDtypeStruct(shape, kind)


def params():
    return pltpu.CompilerParams(vmem_limit_bytes=VMEM_BYTES)


def cost(us):
    return pl.CostEstimate(
        flops=int(us * 4e8), bytes_accessed=int(us * 3e6), transcendentals=0
    )


PROJ_SPEC = pl.BlockSpec((4, 2, SHARD, WIDTH), lambda step: (0, step, 0, 0))
SMEM_SPEC = pl.BlockSpec(memory_space=pltpu.SMEM)


def run_pre_forward(x, vec, first, second):
    return pl.pallas_call(
        pre_forward,
        grid=(1,),
        in_specs=[
            whole(ROWS, WIDTH),
            whole(8, WIDTH),
            whole(2, WIDTH, WIDTH),
            whole(1, WIDTH, WIDTH),
        ],
        out_specs=[whole(ROWS, WIDTH), whole(GROUPS, 3, ROWS, 128)],
        out_shape=[out((ROWS, WIDTH), BF), out((GROUPS, 3, ROWS, 128), BF)],
        compiler_params=params(),
        cost_estimate=cost(4),
        name="pre_forward",
    )(x, vec, first, second)


def run_attend_forward(length_row, qkv):
    return pl.pallas_call(
        attend_forward,
        grid=(1,),
        in_specs=[SMEM_SPEC, whole(GROUPS, 3, ROWS, 128)],
        out_specs=[whole(GROUPS, ROWS, 128), whole(SEQ, 128)],
        out_shape=[out((GROUPS, ROWS, 128), BF), out((SEQ, 128), F32)],
        compiler_params=params(),
        cost_estimate=cost(8),
        name="attend_forward",
    )(length_row, qkv)


def run_attend_backward(length_row, qkv, grad, logsum):
    return pl.pallas_call(
        attend_backward,
        grid=(1,),
        in_specs=[
            SMEM_SPEC,
            whole(GROUPS, 3, ROWS, 128),
            whole(GROUPS, ROWS, 128),
            whole(SEQ, 128),
        ],
        out_specs=whole(GROUPS, 3, ROWS, 128),
        out_shape=out((GROUPS, 3, ROWS, 128), BF),
        scratch_shapes=[pltpu.VMEM((SEQ, 128), F32), pltpu.VMEM((SEQ, 128), F32)],
        compiler_params=params(),
        cost_estimate=cost(16),
        name="attend_backward",
    )(length_row, qkv, grad, logsum)


def run_post_forward(mixed, x, vec, bias, second, fc, proj):
    return pl.pallas_call(
        post_forward,
        grid=(4,),
        in_specs=[
            whole(GROUPS, ROWS, 128),
            whole(ROWS, WIDTH),
            whole(8, WIDTH),
            stepped(1, 1, WIDTH),
            pl.BlockSpec((1, WIDTH, WIDTH), lambda step: (1, 0, 0)),
            stepped(1, WIDTH, WIDTH),
            PROJ_SPEC,
        ],
        out_specs=[
            whole(ROWS, WIDTH),
            whole(ROWS, WIDTH),
            whole(ROWS, WIDTH),
            stepped(1, ROWS, WIDTH),
        ],
        out_shape=[
            out((ROWS, WIDTH), BF),
            out((ROWS, WIDTH), F32),
            out((ROWS, WIDTH), BF),
            out((4, ROWS, WIDTH), F32),
        ],
        scratch_shapes=[pltpu.VMEM((ROWS, WIDTH), F32)],
        compiler_params=params(),
        cost_estimate=cost(8),
        name="post_forward",
    )(mixed, x, vec, bias, second, fc, proj)


def run_post_backward(dy, u, n2, x1, mixed, vec, second, fc, proj):
    return pl.pallas_call(
        post_backward,
        grid=(4,),
        in_specs=[
            whole(ROWS, WIDTH),
            stepped(1, ROWS, WIDTH),
            whole(ROWS, WIDTH),
            whole(ROWS, WIDTH),
            whole(GROUPS, ROWS, 128),
            whole(8, WIDTH),
            pl.BlockSpec((1, WIDTH, WIDTH), lambda step: (1, 0, 0)),
            stepped(1, WIDTH, WIDTH),
            PROJ_SPEC,
        ],
        out_specs=[
            whole(ROWS, WIDTH),
            whole(GROUPS, ROWS, 128),
            whole(WIDTH, WIDTH),
            stepped(1, WIDTH, WIDTH),
            PROJ_SPEC,
            whole(8, WIDTH),
            stepped(1, 1, WIDTH),
        ],
        out_shape=[
            out((ROWS, WIDTH), F32),
            out((GROUPS, ROWS, 128), BF),
            out((WIDTH, WIDTH), BF),
            out((4, WIDTH, WIDTH), BF),
            out((4, GROUPS, SHARD, WIDTH), BF),
            out((8, WIDTH), F32),
            out((4, 1, WIDTH), F32),
        ],
        scratch_shapes=[pltpu.VMEM((ROWS, WIDTH), F32)],
        compiler_params=params(),
        cost_estimate=cost(14),
        name="post_backward",
    )(dy, u, n2, x1, mixed, vec, second, fc, proj)


def run_pre_backward(grads, n1, x, dx1, vec, first, second):
    return pl.pallas_call(
        pre_backward,
        grid=(1,),
        in_specs=[
            whole(GROUPS, 3, ROWS, 128),
            whole(ROWS, WIDTH),
            whole(ROWS, WIDTH),
            whole(ROWS, WIDTH),
            whole(8, WIDTH),
            whole(2, WIDTH, WIDTH),
            whole(1, WIDTH, WIDTH),
        ],
        out_specs=[
            whole(ROWS, WIDTH),
            whole(2, WIDTH, WIDTH),
            whole(WIDTH, WIDTH),
            whole(8, WIDTH),
        ],
        out_shape=[
            out((ROWS, WIDTH), BF),
            out((2, WIDTH, WIDTH), BF),
            out((WIDTH, WIDTH), BF),
            out((8, WIDTH), F32),
        ],
        compiler_params=params(),
        cost_estimate=cost(8),
        name="pre_backward",
    )(grads, n1, x, dx1, vec, first, second)


def exchange(value):
    return lax.all_to_all(value, "group", 0, 0, tiled=True)


def body(
    tokens,
    cotangent,
    lengths,
    ln1_gain,
    ln1_bias,
    w_qkv,
    b_query,
    b_value,
    w_out,
    b_out,
    ln2_gain,
    ln2_bias,
    w_fc,
    b_fc,
    w_proj,
    b_proj,
):
    section = lax.axis_index("section")
    group = lax.axis_index("group")

    def pick(on_first, on_second):
        return jnp.where(section == 0, on_first, on_second)

    def ordered(mine, other):
        return pick(mine, other), pick(other, mine)

    qkv = w_qkv[0].reshape(SHARD, 3, WIDTH).transpose(1, 0, 2)
    fc = w_fc[0].reshape(SHARD, 4, WIDTH).transpose(1, 0, 2)
    half_a = jnp.concatenate([qkv[:2], fc], axis=0)
    half_b = jnp.concatenate([qkv[2:], w_out, w_proj[0].reshape(4, SHARD, WIDTH)], axis=0)
    got = swap(pick(half_b, half_a))
    shard_zero, shard_one = pick(half_a, got), pick(got, half_b)

    vectors = jnp.concatenate(
        [ln1_gain, ln1_bias, b_query, b_value, b_out, ln2_gain, ln2_bias, b_proj, b_fc.reshape(4, SHARD)],
        axis=0,
    )
    vectors = jnp.concatenate(ordered(vectors, swap(vectors)), axis=0)
    vectors = lax.all_gather(vectors, "group", axis=0).astype(F32)

    def vector_rows(layer):
        own = vectors[:, 12 * layer : 12 * layer + 12]
        rows = own[:, :8].transpose(1, 0, 2).reshape(8, WIDTH)
        return rows, own[:, 8:].reshape(4, 1, WIDTH)

    def both_halves(shard):
        mine = gather_group(shard)
        return ordered(mine, swap(mine))

    def gather_layer(shard):
        first, second = both_halves(shard[:2])
        wide, proj = both_halves(shard[2:])
        return (
            first.reshape(2, WIDTH, WIDTH),
            second.reshape(2, WIDTH, WIDTH),
            wide.reshape(4, WIDTH, WIDTH),
            proj,
        )

    weights = (gather_layer(shard_zero), gather_layer(shard_one))
    length_row = lax.dynamic_index_in_dim(lengths, section, 0, keepdims=False)
    rows = lax.dynamic_index_in_dim(tokens, section, 0, keepdims=False)

    outputs, kept = [], []
    for layer in range(2):
        first, second, wide, proj = weights[layer]
        vec, bias = vector_rows(layer)
        n1, send = run_pre_forward(rows, vec, first, second)
        heads = exchange(send)
        mixed, logsum = run_attend_forward(length_row, heads)
        mixed = exchange(mixed)
        result, x1, n2, u = run_post_forward(mixed, rows, vec, bias, second, wide, proj)
        kept.append((rows, vec, n1, heads, logsum, mixed, x1, n2, u))
        outputs.append(result)
        rows = result

    grad = lax.dynamic_index_in_dim(cotangent, section, 0, keepdims=False)
    grads_in, sums_vec, sums = [None, None], [None, None], [None, None]
    for layer in (1, 0):
        first, second, wide, proj = weights[layer]
        rows, vec, n1, heads, logsum, mixed, x1, n2, u = kept[layer]
        dx1, send, dout, dwide, dproj, dvec_two, dbias = run_post_backward(
            grad, u, n2, x1, mixed, vec, second, wide, proj
        )
        dwide = dwide.reshape(4, GROUPS, SHARD, WIDTH)
        arrived = swap(pick(dproj, dwide))
        part = add(pick(dwide, dproj), arrived).astype(BF)
        wide_sum = reduce_group(part)
        wide_sum = reduce_replica(wide_sum.reshape(4 * SHARD, WIDTH))
        grad_heads = exchange(send)
        dheads = run_attend_backward(length_row, heads, grad_heads, logsum)
        dheads = exchange(dheads)
        grad, dfirst, dvalue, dvec_one = run_pre_backward(dheads, n1, rows, dx1, vec, first, second)
        grads_in[layer] = grad
        dsecond = jnp.stack([dvalue, dout])
        arrived = swap(pick(dsecond, dfirst))
        part = add(pick(dfirst, dsecond), arrived).astype(BF).reshape(2, GROUPS, SHARD, WIDTH)
        dvec = jnp.concatenate([dvec_one + dvec_two, dbias.reshape(4, WIDTH)], axis=0)
        sums_vec[layer] = dvec
        extra = 0
        if layer == 0:
            vecs = jnp.stack(sums_vec)
            vecs = vecs + swap(vecs)
            plain = vecs[:, :8].reshape(2, 8, GROUPS, SHARD).transpose(2, 0, 1, 3)
            bias = vecs[:, 8:].reshape(2, GROUPS, 4, SHARD).transpose(1, 0, 2, 3)
            packed = jnp.concatenate([plain, bias], axis=2).reshape(GROUPS, 3, WIDTH).astype(BF)
            extra = 16
            packed = jnp.pad(packed[None], ((0, 1), (0, 0), (0, extra - 3), (0, 0)))
            part = jnp.concatenate([part, packed], axis=2)
        slim = reduce_group(part)
        slim = reduce_replica(slim.reshape(2 * (SHARD + extra), WIDTH))
        slim = slim.reshape(2, SHARD + extra, WIDTH)
        if layer == 0:
            vec_sums = slim[0, SHARD : SHARD + 3].reshape(2, 12, SHARD)
        sums[layer] = (slim[:, :SHARD], wide_sum.reshape(4, SHARD, WIDTH))

    def own_layer(zero, one):
        mine, other = pick(zero, one), swap(pick(one, zero))
        first, second = ordered(mine, other)
        return first.astype(F32), second.astype(F32)

    both = [jnp.concatenate(sums[layer], axis=0) for layer in range(2)]
    first, second = own_layer(*both)
    grad_qkv = jnp.concatenate([first[0], first[1], second[0]], axis=1)
    grad_out = second[1]
    grad_fc = first[2:].transpose(1, 0, 2).reshape(SHARD, 4 * WIDTH)
    grad_proj = second[2:].reshape(4 * SHARD, WIDTH)
    vec_sums = pick(vec_sums[0], vec_sums[1]).astype(F32)

    def both_micro(zero, one):
        mine, other = pick(zero, one), swap(pick(one, zero))
        return jnp.stack(ordered(mine, other))[None]

    acts = both_micro(*outputs)
    in_grads = both_micro(*grads_in)
    v = vec_sums
    return (
        acts,
        in_grads,
        v[0:1],
        v[1:2],
        grad_qkv[None],
        v[2:3],
        v[3:4],
        grad_out[None],
        v[4:5],
        v[5:6],
        v[6:7],
        grad_fc[None],
        v[8:12].reshape(1, 4 * SHARD),
        grad_proj[None],
        v[7:8],
    )


def solution(mesh):
    placed = (
        P("replica", "group", None),
        P("replica", "group", None),
        P("replica", None),
        P("section", "group"),
        P("section", "group"),
        P("section", "group", None),
        P("section", "group"),
        P("section", "group"),
        P("section", "group", None),
        P("section", "group"),
        P("section", "group"),
        P("section", "group"),
        P("section", "group", None),
        P("section", "group"),
        P("section", "group", None),
        P("section", "group"),
    )
    return jax.shard_map(
        body,
        mesh=mesh,
        in_specs=placed,
        out_specs=(
            P("section", "replica", "group", None),
            P("section", "replica", "group", None),
            P("section", "group"),
            P("section", "group"),
            P("section", "group", None),
            P("section", "group"),
            P("section", "group"),
            P("section", "group", None),
            P("section", "group"),
            P("section", "group"),
            P("section", "group"),
            P("section", "group", None),
            P("section", "group"),
            P("section", "group", None),
            P("section", "group"),
        ),
        check_vma=False,
    )
```

time: 1650 us -> 716 us (0.43)
  the two profiles are of different devices: /device:TPU:1 before, /device:TPU:121 now
where the time goes in v1:
time: 716 us; the launch traced here: 706 us
  waiting for transfers between devices  229 us (32%)
  starting transfers between devices  203 us (28%)
  local copies, waits for them, and re-layouts  94.8 us (13%)
  other arithmetic  79.4 us (11%)
  Pallas kernels  63.7 us (9%)
  blocking collectives  32.4 us (5%)
    ppermute x36, waiting for transfers between devices, along_z(): lax.ppermute(value, ('group', 'replica'), torus_pairs(lambda x, y, z: (x,...  108 us
    ppermute x14, starting transfers between devices, swap(): return lax.ppermute(value, 'section', [(0, 1), (1, 0)])  76.4 us
    ppermute x32, waiting for transfers between devices, along_x(): lax.ppermute(value, ('group', 'replica'), torus_pairs(lambda x, y, z: (x...  66.7 us
    unnamed x204, local copies, waits for them, and re-layouts  44.6 us
    select_n x14, other arithmetic, pick(): return jnp.where(section == 0, on_first, on_second)  41.3 us
    ppermute x32, starting transfers between devices, along_x(): lax.ppermute(value, ('group', 'replica'), torus_pairs(lambda x, y, z: (x...  39.6 us
    ppermute x32, waiting for transfers between devices, along_y(): lax.ppermute(value, ('group', 'replica'), torus_pairs(lambda x, y, z: (x,...  31.1 us
    ppermute x36, starting transfers between devices, along_z(): lax.ppermute(value, ('group', 'replica'), torus_pairs(lambda x, y, z: (x,...  29.6 us
  transfers between devices with their start and end apart: 121, of which 62 were waited for; matrix products, arithmetic and copies ran while one was open for 17% of the time, Pallas kernels for 6%

profile of v1, /device:TPU:121, one launch (start us, length us, event | category | flops | bytes accessed | tf_op | source)
XLA Modules:
  0.0 705.8 jit_solution(9718375879596554932)
XLA Ops:
  25.5 6.5 collective-permute-done.24
  34.4 4.0 collective-permute-done.2
  40.7 12.5 %collective-permute-done.26 = bf16[1,96,768]{2,1,0:T(8,128)(2,1)S(1)} collective-permute-done((bf16[1,96,768]{2,1,0:T(8,128)(2,1)S(1)}, bf16[1,96,768]{2,1,0:T(8,128)(2,1)S(1)}, u32[]{:S(2)}, u32[]{:S(2)}) %collective-permute-start.26) | collective-permute-done | bytes 147488 | tf_op jit(solution)/shard_map/ppermute | solution.py:36
  58.2 3.3 collective-permute-done.28
  62.3 4.4 collective-permute-done.29
  68.0 4.3 collective-permute-done.4
  76.7 4.0 collective-permute-done.6
  80.7 5.2 collective-permute-done.7
  86.9 4.5 collective-permute-done.30
  94.5 3.3 collective-permute-done.8
  101.6 3.1 collective-permute-done.31
  109.1 5.8 collective-permute-done.9
  115.7 6.3 collective-permute-done.33
  133.6 3.5 collective-permute-done.19
  143.7 4.0 collective-permute-done.22
  148.8 20.7 %collective-permute-start.23 = (bf16[4,8,96,768]{3,2,1,0:T(8,128)(2,1)}, bf16[4,8,96,768]{3,2,1,0:T(8,128)(2,1)}, u32[]{:S(2)}, u32[]{:S(2)}) collective-permute-start(bf16[4,8,96,768]{3,2,1,0:T(8,128)(2,1)} %bitcast_dynamic-update-slice_fusion.20), channel_id=1, source_target_pairs={{0,64},{64,0},{1,65},{65,1},{2,66},{66,2},{3,67},{67,3},{4,68},{68... | collective-permute-start | bytes 14155784 | tf_op jit(solution)/shard_map/ppermute | solution.py:48
  169.6 3.0 collective-permute-start.38
  172.7 4.1 collective-permute-start.12
  184.2 5.7 collective-permute-done.41
  199.8 4.7 collective-permute-start.45
  205.9 6.1 collective-permute-done
  212.0 22.2 %all-gather = bf16[192,96]{1,0:T(8,128)(2,1)S(1)} all-gather(bf16[24,96]{1,0:T(8,128)(2,1)S(1)} %pad_maximum_fusion.24), channel_id=2, replica_groups=mesh['section'=2,'group'=8,'replica'=8] {'group'}, dimensions={0}, use_global_device_ids=true | all-gather | bytes 41472 | tf_op jit(solution)/shard_map/all_gather | solution.py:604
  240.1 5.4 all-to-all-start
  245.8 5.0 broadcast_select_fusion.8
  253.8 5.5 attend_forward.2
  260.8 3.6 all-to-all-start.1
  264.4 7.9 %broadcast_select_fusion.4 = (bf16[4,8,96,768]{3,2,1,0:T(8,128)(2,1)}, bf16[4,8,96,768]{3,2,1,0:T(8,128)(2,1)}) fusion(bf16[4,8,96,768]{3,2,1,0:T(8,128)(2,1)} %collective-permute-done.23, bf16[4,8,96,768]{3,2,1,0:T(8,128)(2,1)} %bitcast_dynamic-update-slice_fusion.20, pred[]{:T(512)S(6)} %eq.11), kind=kLoop, calls=%fused_computation.8 | loop fusion | flops 4718592 | bytes 18874368 | tf_op jit(solution)/shard_map/jit(_where)/select_n | solution.py:587
  277.2 5.3 post_forward.2
  285.4 5.2 all-to-all-start.2
  291.5 7.4 %all-to-all-done.2.qkv_ref = bf16[8,3,128,128]{3,2,1,0:T(8,128)(2,1)} async-done(((bf16[8,3,128,128]{3,2,1,0:T(8,128)(2,1)}), bf16[8,3,128,128]{3,2,1,0:T(8,128)(2,1)}, u32[]{:S(2)}, u32[]{:S(2)}) %all-to-all-start.2) | async-done | bytes 786464 | tf_op jit(solution)/shard_map/all_to_all | solution.py:562
  298.9 5.5 attend_forward.3
  305.9 3.8 all-to-all-start.3
  309.7 8.1 %broadcast_select_fusion.2 = (bf16[4,8,96,768]{3,2,1,0:T(8,128)(2,1)}, bf16[4,8,96,768]{3,2,1,0:T(8,128)(2,1)}) fusion(bf16[4,8,96,768]{3,2,1,0:T(8,128)(2,1)} %collective-permute-done.45, bf16[4,8,96,768]{3,2,1,0:T(8,128)(2,1)} %bitcast_dynamic-update-slice_fusion.31, pred[]{:T(512)S(6)} %eq.11), kind=kLoop, calls=%fused_computation.6 | loop fusion | flops 4718592 | bytes 18874368 | tf_op jit(solution)/shard_map/jit(_where)/select_n | solution.py:587
  323.4 5.2 post_forward.3
  329.4 10.6 %post_backward.2 = (f32[128,768]{1,0:T(8,128)S(1)}, bf16[8,128,128]{2,1,0:T(8,128)(2,1)S(1)}, bf16[768,768]{1,0:T(8,128)(2,1)S(1)}, bf16[4,768,768]{2,1,0:T(8,12...) custom-call(f32[128,768]{1,0:T(8,128)S(1)} %copy-done.39, ...), custom_call_target="tpu_custom_call" | custom-call | flops 5600000000 | bytes 42000000 | tf_op jit(solution)/shard_map/post_backward/pallas_call | solution.py:491
  343.2 10.2 %all_to_all.40.grad_ref = bf16[8,128,128]{2,1,0:T(8,128)(2,1)S(1)} all-to-all(bf16[8,128,128]{2,1,0:T(8,128)(2,1)S(1)} %get-tuple-element.62), channel_id=1, replica_groups=mesh['section'=2,'group'=8,'replica'=8] {'group'}, dimensions={0} | all-to-all | bytes 524288 | tf_op jit(solution)/shard_map/all_to_all | solution.py:562
  353.5 7.0 attend_backward.2
  361.4 4.0 all-to-all-start.5
  365.4 5.1 broadcast_select_fusion
  370.4 11.8 %collective-permute-start.97 = (bf16[4,8,96,768]{3,2,1,0:T(8,128)(2,1)}, bf16[4,8,96,768]{3,2,1,0:T(8,128)(2,1)}, u32[]{:S(2)}, u32[]{:S(2)}) collective-permute-start(bf16[4,8,96,768]{3,2,1,0:T(8,128)(2,1)} %broadcast_select_fusion), channel_id=1, source_target_pairs={{0,64},{64,0},{1,65},{65,1},{2,66},{66,2},{3,67},{67,3},{4,68},{68... | collective-permute-start | bytes 14155784 | tf_op jit(solution)/shard_map/ppermute | solution.py:48
  393.9 3.2 collective-permute-start.81
  397.2 10.5 %post_backward.3 = (f32[128,768]{1,0:T(8,128)S(1)}, bf16[8,128,128]{2,1,0:T(8,128)(2,1)S(1)}, bf16[768,768]{1,0:T(8,128)(2,1)S(1)}, bf16[4,768,768]{2,1,0:T(8,12...) custom-call(bf16[128,768]{1,0:T(8,128)(2,1)S(1)} %get-tuple-element.66.dy_ref, ...), custom_call_target="tpu_custom_call" | custom-call | flops 5600000000 | bytes 42000000 | tf_op jit(solution)/shard_map/post_backward/pallas_call | solution.py:491
  412.1 3.6 all-to-all-start.6
  417.6 3.9 all-to-all-done.6.grad_ref
  422.6 7.9 %attend_backward.3 = bf16[8,3,128,128]{3,2,1,0:T(8,128)(2,1)} custom-call(s32[3]{0:T(128)S(1)} %fusion.51.length_ref, bf16[8,3,128,128]{3,2,1,0:T(8,128)(2,1)} %all-to-all-done.qkv_ref, bf16[8,128,128]{2,1,0:T(8,128)(2,1)S(1)} %all-to-all-done.6.grad_ref, f32[1024,128]{1,0:T(8,128)S(1)} %copy-done.69), custom_call_target="tpu_custom_call" | custom-call | flops 6400000000 | bytes 48000000 | tf_op jit(solution)/shard_map/attend_backward/pallas_call | solution.py:440
  430.5 3.6 all-to-all-start.7
  434.9 4.9 broadcast_select_fusion.1
  453.3 3.2 collective-permute-start.49
  463.2 10.7 %collective-permute-done.82 = bf16[1,4,96,768]{3,2,1,0:T(8,128)(2,1)S(1)} collective-permute-done((bf16[1,4,96,768]{3,2,1,0:T(8,128)(2,1)S(1)}, bf16[1,4,96,768]{3,2,1,0:T(8,128)(2,1)S(1)}, u32[]{:S(2)}, u32[]{:S(2)}) %collective-permute-start.82) | collective-permute-done | bytes 589856 | tf_op jit(solution)/shard_map/ppermute | solution.py:44
  477.0 4.8 collective-permute-done.84
  482.6 3.2 collective-permute-done.86
  489.7 3.2 collective-permute-done.85
  496.0 3.2 add_convert_fusion.3
  505.1 3.2 collective-permute-start.92
  510.8 4.0 collective-permute-start.50
  517.1 8.4 %add_convert_fusion = bf16[4,8,96,768]{3,2,1,0:T(8,128)(2,1)} fusion(bf16[4,8,96,768]{3,2,1,0:T(8,128)(2,1)} %collective-permute-done.97, bf16[4,8,96,768]{3,2,1,0:T(8,128)(2,1)S(1)} %bitcast.499, bf16[4,8,96,768]{3,2,1,0:T(8,128)(2,1)} %get-tuple-element.90, pred[]{:T(512)S(6)} %eq.11), kind=kLoop, calls=%fused_computation | loop fusion | flops 11796480 | bytes 18874368 | tf_op jit(solution)/shard_map/convert_element_type | solution.py:652
  549.5 8.2 %add_convert_fusion.1 = bf16[4,8,96,768]{3,2,1,0:T(8,128)(2,1)} fusion(bf16[4,8,96,768]{3,2,1,0:T(8,128)(2,1)} %collective-permute-done.65, bf16[4,8,96,768]{3,2,1,0:T(8,128)(2,1)S(1)} %bitcast.503, bf16[4,8,96,768]{3,2,1,0:T(8,128)(2,1)} %get-tuple-element.85, pred[]{:T(512)S(6)} %eq.11), kind=kLoop, calls=%fused_computation.1 | loop fusion | flops 11796480 | bytes 18874368 | tf_op jit(solution)/shard_map/convert_element_type | solution.py:652
  567.5 28.0 %collective-permute-done.60 = bf16[56,768]{1,0:T(8,128)(2,1)S(1)} collective-permute-done((bf16[56,768]{1,0:T(8,128)(2,1)S(1)}, bf16[56,768]{1,0:T(8,128)(2,1)S(1)}, u32[]{:S(2)}, u32[]{:S(2)}) %collective-permute-start.60) | collective-permute-done | bytes 86048 | tf_op jit(solution)/shard_map/ppermute | solution.py:44
  595.8 4.2 collective-permute-done.96
  600.0 3.3 collective-permute-done.61
  603.4 4.9 collective-permute-done.62
  625.8 5.3 collective-permute-done.69
  634.2 9.6 %collective-permute-done.101 = bf16[4,96,768]{2,1,0:T(8,128)(2,1)S(1)} collective-permute-done((bf16[4,96,768]{2,1,0:T(8,128)(2,1)S(1)}, bf16[4,96,768]{2,1,0:T(8,128)(2,1)S(1)}, u32[]{:S(2)}, u32[]{:S(2)}) %collective-permute-start.101) | collective-permute-done | bytes 589856 | tf_op jit(solution)/shard_map/ppermute | solution.py:36
  666.0 17.6 %collective-permute-start.47 = (bf16[128,768]{1,0:T(8,128)(2,1)S(1)}, bf16[128,768]{1,0:T(8,128)(2,1)S(1)}, u32[]{:S(2)}, u32[]{:S(2)}) collective-permute-start(bf16[128,768]{1,0:T(8,128)(2,1)S(1)} %copy-done.80), channel_id=1, source_target_pairs={{0,64},{64,0},{1,65},{65,1},{2,66},{66,2},{3,67},{67,3},{4,68},{68... | collective-permute-start | bytes 589832 | tf_op jit(solution)/shard_map/ppermute | solution.py:48
  (632 shorter events, 282.0 us)
Async XLA Ops:
  9.9 76.0 %collective-permute-start.35 = (bf16[4,96,768]{2,1,0:T(8,128)(2,1)S(1)}, bf16[4,96,768]{2,1,0:T(8,128)(2,1)S(1)}, u32[]{:S(2)}, u32[]{:S(2)}) collective-permute-start(bf16[4,96,768]{2,1,0:T(8,128)(2,1)S(1)} %slice.658), channel_id=1, source_target_pairs={{0,16},{1,17},{2,18},{3,19},{4,20},{5,21},{6,22},{7,23},{8,24},{9,... | collective-permute-start | bytes 1769480 | tf_op jit(solution)/shard_map/ppermute | solution.py:36
  11.2 82.2 %collective-permute-start.36 = (bf16[4,96,768]{2,1,0:T(8,128)(2,1)S(1)}, bf16[4,96,768]{2,1,0:T(8,128)(2,1)S(1)}, u32[]{:S(2)}, u32[]{:S(2)}) collective-permute-start(bf16[4,96,768]{2,1,0:T(8,128)(2,1)S(1)} %slice.658), channel_id=1, source_target_pairs={{0,48},{1,49},{2,50},{3,51},{4,52},{5,53},{6,54},{7,55},{8,56},{9,... | collective-permute-start | bytes 1769480 | tf_op jit(solution)/shard_map/ppermute | solution.py:36
  12.7 19.3 %collective-permute-start.24 = (bf16[2,96,768]{2,1,0:T(8,128)(2,1)S(1)}, bf16[2,96,768]{2,1,0:T(8,128)(2,1)S(1)}, u32[]{:S(2)}, u32[]{:S(2)}) collective-permute-start(bf16[2,96,768]{2,1,0:T(8,128)(2,1)S(1)} %get-tuple-element.137), channel_id=1, source_target_pairs={{0,16},{1,17},{2,18},{3,19},{4,20},{5,21},{6,22},{7,23},{8,24},{9,... | collective-permute-start | bytes 884744 | tf_op jit(solution)/shard_map/ppermute | solution.py:36
  12.8 21.3 %collective-permute-start.25 = (bf16[2,96,768]{2,1,0:T(8,128)(2,1)S(1)}, bf16[2,96,768]{2,1,0:T(8,128)(2,1)S(1)}, u32[]{:S(2)}, u32[]{:S(2)}) collective-permute-start(bf16[2,96,768]{2,1,0:T(8,128)(2,1)S(1)} %get-tuple-element.137), channel_id=1, source_target_pairs={{0,48},{1,49},{2,50},{3,51},{4,52},{5,53},{6,54},{7,55},{8,56},{9,... | collective-permute-start | bytes 884744 | tf_op jit(solution)/shard_map/ppermute | solution.py:36
  25.4 13.0 %collective-permute-start.2 = (bf16[2,96,768]{2,1,0:T(8,128)(2,1)S(1)}, bf16[2,96,768]{2,1,0:T(8,128)(2,1)S(1)}, u32[]{:S(2)}, u32[]{:S(2)}) collective-permute-start(bf16[2,96,768]{2,1,0:T(8,128)(2,1)S(1)} %get-tuple-element.144), channel_id=1, source_target_pairs={{0,16},{1,17},{2,18},{3,19},{4,20},{5,21},{6,22},{7,23},{8,24},{9,... | collective-permute-start | bytes 884744 | tf_op jit(solution)/shard_map/ppermute | solution.py:36
  34.1 63.9 %collective-permute-start.13 = (bf16[4,96,768]{2,1,0:T(8,128)(2,1)S(1)}, bf16[4,96,768]{2,1,0:T(8,128)(2,1)S(1)}, u32[]{:S(2)}, u32[]{:S(2)}) collective-permute-start(bf16[4,96,768]{2,1,0:T(8,128)(2,1)S(1)} %slice.646), channel_id=1, source_target_pairs={{0,16},{1,17},{2,18},{3,19},{4,20},{5,21},{6,22},{7,23},{8,24},{9,... | collective-permute-start | bytes 1769480 | tf_op jit(solution)/shard_map/ppermute | solution.py:36
  38.4 67.1 %collective-permute-start.14 = (bf16[4,96,768]{2,1,0:T(8,128)(2,1)S(1)}, bf16[4,96,768]{2,1,0:T(8,128)(2,1)S(1)}, u32[]{:S(2)}, u32[]{:S(2)}) collective-permute-start(bf16[4,96,768]{2,1,0:T(8,128)(2,1)S(1)} %slice.646), channel_id=1, source_target_pairs={{0,48},{1,49},{2,50},{3,51},{4,52},{5,53},{6,54},{7,55},{8,56},{9,... | collective-permute-start | bytes 1769480 | tf_op jit(solution)/shard_map/ppermute | solution.py:36
  39.7 13.6 %collective-permute-start.26 = (bf16[1,96,768]{2,1,0:T(8,128)(2,1)S(1)}, bf16[1,96,768]{2,1,0:T(8,128)(2,1)S(1)}, u32[]{:S(2)}, u32[]{:S(2)}) collective-permute-start(bf16[1,96,768]{2,1,0:T(8,128)(2,1)S(1)} %slice.653), channel_id=1, source_target_pairs={{0,16},{1,17},{2,18},{3,19},{4,20},{5,21},{6,22},{7,23},{8,24},{9,... | collective-permute-start | bytes 442376 | tf_op jit(solution)/shard_map/ppermute | solution.py:36
  85.9 92.7 %collective-permute-start.39 = (bf16[2,96,768]{2,1,0:T(8,128)(2,1)S(1)}, bf16[2,96,768]{2,1,0:T(8,128)(2,1)S(1)}, u32[]{:S(2)}, u32[]{:S(2)}) collective-permute-start(bf16[2,96,768]{2,1,0:T(8,128)(2,1)S(1)} %get-tuple-element.136), channel_id=1, source_target_pairs={{0,8},{1,9},{2,10},{3,11},{4,12},{5,13},{6,14},{7,15},{8,4},{9,5},... | collective-permute-start | bytes 884744 | tf_op jit(solution)/shard_map/ppermute | solution.py:44
  93.4 87.2 %collective-permute-start.40 = (bf16[2,96,768]{2,1,0:T(8,128)(2,1)S(1)}, bf16[2,96,768]{2,1,0:T(8,128)(2,1)S(1)}, u32[]{:S(2)}, u32[]{:S(2)}) collective-permute-start(bf16[2,96,768]{2,1,0:T(8,128)(2,1)S(1)} %get-tuple-element.135), channel_id=1, source_target_pairs={{0,12},{1,13},{2,14},{3,15},{4,8},{5,9},{6,10},{7,11},{8,0},{9,1},... | collective-permute-start | bytes 884744 | tf_op jit(solution)/shard_map/ppermute | solution.py:44
  98.0 31.4 %collective-permute-start.17 = (bf16[2,96,768]{2,1,0:T(8,128)(2,1)S(1)}, bf16[2,96,768]{2,1,0:T(8,128)(2,1)S(1)}, u32[]{:S(2)}, u32[]{:S(2)}) collective-permute-start(bf16[2,96,768]{2,1,0:T(8,128)(2,1)S(1)} %get-tuple-element.143), channel_id=1, source_target_pairs={{0,8},{1,9},{2,10},{3,11},{4,12},{5,13},{6,14},{7,15},{8,4},{9,5},... | collective-permute-start | bytes 884744 | tf_op jit(solution)/shard_map/ppermute | solution.py:44
  104.7 10.2 %collective-permute-start.9 = (bf16[2,96,768]{2,1,0:T(8,128)(2,1)S(1)}, bf16[2,96,768]{2,1,0:T(8,128)(2,1)S(1)}, u32[]{:S(2)}, u32[]{:S(2)}) collective-permute-start(bf16[2,96,768]{2,1,0:T(8,128)(2,1)S(1)} %collective-permute-done.3), channel_id=1, source_target_pairs={{0,12},{1,13},{2,14},{3,15},{4,8},{5,9},{6,10},{7,11},{8,0},{9,1},... | collective-permute-start | bytes 884744 | tf_op jit(solution)/shard_map/ppermute | solution.py:44
  105.5 9.5 %collective-permute-start.32 = (bf16[1,96,768]{2,1,0:T(8,128)(2,1)S(1)}, bf16[1,96,768]{2,1,0:T(8,128)(2,1)S(1)}, u32[]{:S(2)}, u32[]{:S(2)}) collective-permute-start(bf16[1,96,768]{2,1,0:T(8,128)(2,1)S(1)} %collective-permute-done.26), channel_id=1, source_target_pairs={{0,8},{1,9},{2,10},{3,11},{4,12},{5,13},{6,14},{7,15},{8,4},{9,5},... | collective-permute-start | bytes 442376 | tf_op jit(solution)/shard_map/ppermute | solution.py:44
  115.0 10.1 %collective-permute-start.15 = (bf16[2,96,768]{2,1,0:T(8,128)(2,1)S(1)}, bf16[2,96,768]{2,1,0:T(8,128)(2,1)S(1)}, u32[]{:S(2)}, u32[]{:S(2)}) collective-permute-start(bf16[2,96,768]{2,1,0:T(8,128)(2,1)S(1)} %slice.647), channel_id=1, source_target_pairs={{0,16},{1,17},{2,18},{3,19},{4,20},{5,21},{6,22},{7,23},{8,24},{9,... | collective-permute-start | bytes 884744 | tf_op jit(solution)/shard_map/ppermute | solution.py:36
  128.1 9.0 %collective-permute-start.19 = (bf16[4,96,768]{2,1,0:T(8,128)(2,1)S(1)}, bf16[4,96,768]{2,1,0:T(8,128)(2,1)S(1)}, u32[]{:S(2)}, u32[]{:S(2)}) collective-permute-start(bf16[4,96,768]{2,1,0:T(8,128)(2,1)S(1)} %collective-permute-done.13), channel_id=1, source_target_pairs={{0,8},{1,9},{2,10},{3,11},{4,12},{5,13},{6,14},{7,15},{8,4},{9,5},... | collective-permute-start | bytes 1769480 | tf_op jit(solution)/shard_map/ppermute | solution.py:44
  129.4 11.5 %collective-permute-start.20 = (bf16[4,96,768]{2,1,0:T(8,128)(2,1)S(1)}, bf16[4,96,768]{2,1,0:T(8,128)(2,1)S(1)}, u32[]{:S(2)}, u32[]{:S(2)}) collective-permute-start(bf16[4,96,768]{2,1,0:T(8,128)(2,1)S(1)} %collective-permute-done.14), channel_id=1, source_target_pairs={{0,12},{1,13},{2,14},{3,15},{4,8},{5,9},{6,10},{7,11},{8,0},{9,1},... | collective-permute-start | bytes 1769480 | tf_op jit(solution)/shard_map/ppermute | solution.py:44
  132.9 15.9 %collective-permute-start.10 = (bf16[1,96,768]{2,1,0:T(8,128)(2,1)S(1)}, bf16[1,96,768]{2,1,0:T(8,128)(2,1)S(1)}, u32[]{:S(2)}, u32[]{:S(2)}) collective-permute-start(bf16[1,96,768]{2,1,0:T(8,128)(2,1)S(1)} %collective-permute-done.4), channel_id=1, source_target_pairs={{0,8},{1,9},{2,10},{3,11},{4,12},{5,13},{6,14},{7,15},{8,4},{9,5},... | collective-permute-start | bytes 442376 | tf_op jit(solution)/shard_map/ppermute | solution.py:44
  143.0 26.6 %collective-permute-start.11 = (bf16[1,96,768]{2,1,0:T(8,128)(2,1)S(1)}, bf16[1,96,768]{2,1,0:T(8,128)(2,1)S(1)}, u32[]{:S(2)}, u32[]{:S(2)}) collective-permute-start(bf16[1,96,768]{2,1,0:T(8,128)(2,1)S(1)} %collective-permute-done.5), channel_id=1, source_target_pairs={{0,12},{1,13},{2,14},{3,15},{4,8},{5,9},{6,10},{7,11},{8,0},{9,1},... | collective-permute-start | bytes 442376 | tf_op jit(solution)/shard_map/ppermute | solution.py:44
  147.7 25.0 %collective-permute-start.37 = (bf16[2,96,768]{2,1,0:T(8,128)(2,1)S(1)}, bf16[2,96,768]{2,1,0:T(8,128)(2,1)S(1)}, u32[]{:S(2)}, u32[]{:S(2)}) collective-permute-start(bf16[2,96,768]{2,1,0:T(8,128)(2,1)S(1)} %slice.659), channel_id=1, source_target_pairs={{0,16},{1,17},{2,18},{3,19},{4,20},{5,21},{6,22},{7,23},{8,24},{9,... | collective-permute-start | bytes 884744 | tf_op jit(solution)/shard_map/ppermute | solution.py:36
  148.8 115.6 %collective-permute-start.23 = (bf16[4,8,96,768]{3,2,1,0:T(8,128)(2,1)}, bf16[4,8,96,768]{3,2,1,0:T(8,128)(2,1)}, u32[]{:S(2)}, u32[]{:S(2)}) collective-permute-start(bf16[4,8,96,768]{3,2,1,0:T(8,128)(2,1)} %bitcast_dynamic-update-slice_fusion.20), channel_id=1, source_target_pairs={{0,64},{64,0},{1,65},{65,1},{2,66},{66,2},{3,67},{67,3},{4,68},{68... | collective-permute-start | bytes 14155784 | tf_op jit(solution)/shard_map/ppermute | solution.py:48
  172.7 61.6 %collective-permute-start.12 = (bf16[2,8,96,768]{3,2,1,0:T(8,128)(2,1)S(1)}, bf16[2,8,96,768]{3,2,1,0:T(8,128)(2,1)}, u32[]{:S(2)}, u32[]{:S(2)}) collective-permute-start(bf16[2,8,96,768]{3,2,1,0:T(8,128)(2,1)S(1)} %bitcast_dynamic-update-slice_fusion.44), channel_id=1, source_target_pairs={{0,64},{64,0},{1,65},{65,1},{2,66},{66,2},{3,67},{67,3},{4,68},{68... | collective-permute-start | bytes 7077896 | tf_op jit(solution)/shard_map/ppermute | solution.py:48
  177.5 12.5 %collective-permute-start.41 = (bf16[4,96,768]{2,1,0:T(8,128)(2,1)S(1)}, bf16[4,96,768]{2,1,0:T(8,128)(2,1)S(1)}, u32[]{:S(2)}, u32[]{:S(2)}) collective-permute-start(bf16[4,96,768]{2,1,0:T(8,128)(2,1)S(1)} %collective-permute-done.35), channel_id=1, source_target_pairs={{0,8},{1,9},{2,10},{3,11},{4,12},{5,13},{6,14},{7,15},{8,4},{9,5},... | collective-permute-start | bytes 1769480 | tf_op jit(solution)/shard_map/ppermute | solution.py:44
  178.6 13.7 %collective-permute-start.42 = (bf16[4,96,768]{2,1,0:T(8,128)(2,1)S(1)}, bf16[4,96,768]{2,1,0:T(8,128)(2,1)S(1)}, u32[]{:S(2)}, u32[]{:S(2)}) collective-permute-start(bf16[4,96,768]{2,1,0:T(8,128)(2,1)S(1)} %collective-permute-done.36), channel_id=1, source_target_pairs={{0,12},{1,13},{2,14},{3,15},{4,8},{5,9},{6,10},{7,11},{8,0},{9,1},... | collective-permute-start | bytes 1769480 | tf_op jit(solution)/shard_map/ppermute | solution.py:44
  180.6 65.2 %collective-permute-start.34 = (bf16[2,8,96,768]{3,2,1,0:T(8,128)(2,1)}, bf16[2,8,96,768]{3,2,1,0:T(8,128)(2,1)}, u32[]{:S(2)}, u32[]{:S(2)}) collective-permute-start(bf16[2,8,96,768]{3,2,1,0:T(8,128)(2,1)} %bitcast_dynamic-update-slice_fusion.38), channel_id=1, source_target_pairs={{0,64},{64,0},{1,65},{65,1},{2,66},{66,2},{3,67},{67,3},{4,68},{68... | collective-permute-start | bytes 7077896 | tf_op jit(solution)/shard_map/ppermute | solution.py:48
  199.8 109.9 %collective-permute-start.45 = (bf16[4,8,96,768]{3,2,1,0:T(8,128)(2,1)}, bf16[4,8,96,768]{3,2,1,0:T(8,128)(2,1)}, u32[]{:S(2)}, u32[]{:S(2)}) collective-permute-start(bf16[4,8,96,768]{3,2,1,0:T(8,128)(2,1)} %bitcast_dynamic-update-slice_fusion.31), channel_id=1, source_target_pairs={{0,64},{64,0},{1,65},{65,1},{2,66},{66,2},{3,67},{67,3},{4,68},{68... | collective-permute-start | bytes 14155784 | tf_op jit(solution)/shard_map/ppermute | solution.py:48
  240.1 13.7 %all-to-all-start = ((bf16[8,3,128,128]{3,2,1,0:T(8,128)(2,1)}), bf16[8,3,128,128]{3,2,1,0:T(8,128)(2,1)}, u32[]{:S(2)}, u32[]{:S(2)}) async-start(bf16[8,3,128,128]{3,2,1,0:T(8,128)(2,1)} %copy-done.32), calls=%async_computation | async-start | bytes 1572864 | tf_op jit(solution)/shard_map/all_to_all | solution.py:562
  260.8 11.5 %all-to-all-start.1 = ((bf16[8,128,128]{2,1,0:T(8,128)(2,1)}), bf16[8,128,128]{2,1,0:T(8,128)(2,1)S(1)}, u32[]{:S(2)}, u32[]{:S(2)}) async-start(bf16[8,128,128]{2,1,0:T(8,128)(2,1)} %copy-done.41), calls=%async_computation.1 | async-start | bytes 524288 | tf_op jit(solution)/shard_map/all_to_all | solution.py:562
  285.4 13.4 %all-to-all-start.2 = ((bf16[8,3,128,128]{3,2,1,0:T(8,128)(2,1)}), bf16[8,3,128,128]{3,2,1,0:T(8,128)(2,1)}, u32[]{:S(2)}, u32[]{:S(2)}) async-start(bf16[8,3,128,128]{3,2,1,0:T(8,128)(2,1)} %copy-done.33), calls=%async_computation.2 | async-start | bytes 1572864 | tf_op jit(solution)/shard_map/all_to_all | solution.py:562
  305.9 11.9 %all-to-all-start.3 = ((bf16[8,128,128]{2,1,0:T(8,128)(2,1)}), bf16[8,128,128]{2,1,0:T(8,128)(2,1)S(1)}, u32[]{:S(2)}, u32[]{:S(2)}) async-start(bf16[8,128,128]{2,1,0:T(8,128)(2,1)} %copy-done.42), calls=%async_computation.3 | async-start | bytes 524288 | tf_op jit(solution)/shard_map/all_to_all | solution.py:562
  361.4 21.4 %all-to-all-start.5 = ((bf16[8,3,128,128]{3,2,1,0:T(8,128)(2,1)}), bf16[8,3,128,128]{3,2,1,0:T(8,128)(2,1)S(1)}, u32[]{:S(2)}, u32[]{:S(2)}) async-start(bf16[8,3,128,128]{3,2,1,0:T(8,128)(2,1)} %copy-done.31), calls=%async_computation.5 | async-start | bytes 1572864 | tf_op jit(solution)/shard_map/all_to_all | solution.py:562
  370.4 146.7 %collective-permute-start.97 = (bf16[4,8,96,768]{3,2,1,0:T(8,128)(2,1)}, bf16[4,8,96,768]{3,2,1,0:T(8,128)(2,1)}, u32[]{:S(2)}, u32[]{:S(2)}) collective-permute-start(bf16[4,8,96,768]{3,2,1,0:T(8,128)(2,1)} %broadcast_select_fusion), channel_id=1, source_target_pairs={{0,64},{64,0},{1,65},{65,1},{2,66},{66,2},{3,67},{67,3},{4,68},{68... | collective-permute-start | bytes 14155784 | tf_op jit(solution)/shard_map/ppermute | solution.py:48
  393.9 62.6 %collective-permute-start.81 = (bf16[2,768,768]{2,1,0:T(8,128)(2,1)}, bf16[2,768,768]{2,1,0:T(8,128)(2,1)}, u32[]{:S(2)}, u32[]{:S(2)}) collective-permute-start(bf16[2,768,768]{2,1,0:T(8,128)(2,1)} %broadcast_select_fusion.6), channel_id=1, source_target_pairs={{0,64},{64,0},{1,65},{65,1},{2,66},{66,2},{3,67},{67,3},{4,68},{68... | collective-permute-start | bytes 7077896 | tf_op jit(solution)/shard_map/ppermute | solution.py:48
  412.1 9.5 %all-to-all-start.6 = ((bf16[8,128,128]{2,1,0:T(8,128)(2,1)}), bf16[8,128,128]{2,1,0:T(8,128)(2,1)S(1)}, u32[]{:S(2)}, u32[]{:S(2)}) async-start(bf16[8,128,128]{2,1,0:T(8,128)(2,1)} %copy-done.40), calls=%async_computation.6 | async-start | bytes 524288 | tf_op jit(solution)/shard_map/all_to_all | solution.py:562
  415.7 18.4 %collective-permute-start.46 = (bf16[128,768]{1,0:T(8,128)(2,1)S(1)}, bf16[128,768]{1,0:T(8,128)(2,1)S(1)}, u32[]{:S(2)}, u32[]{:S(2)}) collective-permute-start(bf16[128,768]{1,0:T(8,128)(2,1)S(1)} %broadcast_select_fusion.19), channel_id=1, source_target_pairs={{0,64},{64,0},{1,65},{65,1},{2,66},{66,2},{3,67},{67,3},{4,68},{68... | collective-permute-start | bytes 589832 | tf_op jit(solution)/shard_map/ppermute | solution.py:48
  430.5 13.5 %all-to-all-start.7 = ((bf16[8,3,128,128]{3,2,1,0:T(8,128)(2,1)}), bf16[8,3,128,128]{3,2,1,0:T(8,128)(2,1)S(1)}, u32[]{:S(2)}, u32[]{:S(2)}) async-start(bf16[8,3,128,128]{3,2,1,0:T(8,128)(2,1)} %attend_backward.3), calls=%async_computation.7 | async-start | bytes 1572864 | tf_op jit(solution)/shard_map/all_to_all | solution.py:562
  439.8 108.5 %collective-permute-start.65 = (bf16[4,8,96,768]{3,2,1,0:T(8,128)(2,1)}, bf16[4,8,96,768]{3,2,1,0:T(8,128)(2,1)}, u32[]{:S(2)}, u32[]{:S(2)}) collective-permute-start(bf16[4,8,96,768]{3,2,1,0:T(8,128)(2,1)} %broadcast_select_fusion.1), channel_id=1, source_target_pairs={{0,64},{64,0},{1,65},{65,1},{2,66},{66,2},{3,67},{67,3},{4,68},{68... | collective-permute-start | bytes 14155784 | tf_op jit(solution)/shard_map/ppermute | solution.py:48
  453.3 33.3 %collective-permute-start.49 = (f32[2,12,768]{2,1,0:T(8,128)S(1)}, f32[2,12,768]{2,1,0:T(8,128)S(1)}, u32[]{:S(2)}, u32[]{:S(2)}) collective-permute-start(f32[2,12,768]{2,1,0:T(8,128)S(1)} %pad_maximum_fusion.18), channel_id=1, source_target_pairs={{0,64},{64,0},{1,65},{65,1},{2,66},{66,2},{3,67},{67,3},{4,68},{68... | collective-permute-start | bytes 221192 | tf_op jit(solution)/shard_map/ppermute | solution.py:48
  459.2 14.8 %collective-permute-start.82 = (bf16[1,4,96,768]{3,2,1,0:T(8,128)(2,1)S(1)}, bf16[1,4,96,768]{3,2,1,0:T(8,128)(2,1)S(1)}, u32[]{:S(2)}, u32[]{:S(2)}) collective-permute-start(bf16[1,4,96,768]{3,2,1,0:T(8,128)(2,1)S(1)} %slice_bitcast_fusion.7), channel_id=1, source_target_pairs={{0,8},{1,9},{2,10},{3,11},{4,12},{5,13},{6,14},{7,15},{8,4},{9,5},... | collective-permute-start | bytes 1769480 | tf_op jit(solution)/shard_map/ppermute | solution.py:44
  460.4 15.7 %collective-permute-start.83 = (bf16[1,4,96,768]{3,2,1,0:T(8,128)(2,1)S(1)}, bf16[1,4,96,768]{3,2,1,0:T(8,128)(2,1)S(1)}, u32[]{:S(2)}, u32[]{:S(2)}) collective-permute-start(bf16[1,4,96,768]{3,2,1,0:T(8,128)(2,1)S(1)} %dynamic-slice_bitcast_fusion.9), channel_id=1, source_target_pairs={{0,12},{1,13},{2,14},{3,15},{4,8},{5,9},{6,10},{7,11},{8,0},{9,1},... | collective-permute-start | bytes 1769480 | tf_op jit(solution)/shard_map/ppermute | solution.py:44
  474.0 22.1 %collective-permute-start.48 = (bf16[2,768,768]{2,1,0:T(8,128)(2,1)}, bf16[2,768,768]{2,1,0:T(8,128)(2,1)}, u32[]{:S(2)}, u32[]{:S(2)}) collective-permute-start(bf16[2,768,768]{2,1,0:T(8,128)(2,1)} %broadcast_select_fusion.7), channel_id=1, source_target_pairs={{0,64},{64,0},{1,65},{65,1},{2,66},{66,2},{3,67},{67,3},{4,68},{68... | collective-permute-start | bytes 7077896 | tf_op jit(solution)/shard_map/ppermute | solution.py:48
  510.8 14.7 %collective-permute-start.50 = (bf16[1,4,112,768]{3,2,1,0:T(8,128)(2,1)S(1)}, bf16[1,4,112,768]{3,2,1,0:T(8,128)(2,1)S(1)}, u32[]{:S(2)}, u32[]{:S(2)}) collective-permute-start(bf16[1,4,112,768]{3,2,1,0:T(8,128)(2,1)S(1)} %slice_bitcast_fusion.5), channel_id=1, source_target_pairs={{0,8},{1,9},{2,10},{3,11},{4,12},{5,13},{6,14},{7,15},{8,4},{9,5},... | collective-permute-start | bytes 2064392 | tf_op jit(solution)/shard_map/ppermute | solution.py:44
  514.8 11.0 %collective-permute-start.51 = (bf16[1,4,112,768]{3,2,1,0:T(8,128)(2,1)S(1)}, bf16[1,4,112,768]{3,2,1,0:T(8,128)(2,1)S(1)}, u32[]{:S(2)}, u32[]{:S(2)}) collective-permute-start(bf16[1,4,112,768]{3,2,1,0:T(8,128)(2,1)S(1)} %slice_bitcast_fusion.3), channel_id=1, source_target_pairs={{0,12},{1,13},{2,14},{3,15},{4,8},{5,9},{6,10},{7,11},{8,0},{9,1},... | collective-permute-start | bytes 2064392 | tf_op jit(solution)/shard_map/ppermute | solution.py:44
  514.8 46.1 %collective-permute-start.94 = (bf16[48,768]{1,0:T(8,128)(2,1)}, bf16[48,768]{1,0:T(8,128)(2,1)S(1)}, u32[]{:S(2)}, u32[]{:S(2)}) collective-permute-start(bf16[48,768]{1,0:T(8,128)(2,1)} %get-tuple-element.94), channel_id=1, source_target_pairs={{0,3},{1,0},{2,1},{3,2},{4,7},{5,4},{6,5},{7,6},{8,11},{9,8},{10,9... | collective-permute-start | bytes 221192 | tf_op jit(solution)/shard_map/ppermute | solution.py:40
  532.7 8.8 %collective-permute-start.53 = (bf16[2,112,768]{2,1,0:T(8,128)(2,1)S(1)}, bf16[2,112,768]{2,1,0:T(8,128)(2,1)S(1)}, u32[]{:S(2)}, u32[]{:S(2)}) collective-permute-start(bf16[2,112,768]{2,1,0:T(8,128)(2,1)S(1)} %pad_maximum_fusion.10), channel_id=1, source_target_pairs={{0,16},{1,17},{2,18},{3,19},{4,20},{5,21},{6,22},{7,23},{8,24},{9,... | collective-permute-start | bytes 1032200 | tf_op jit(solution)/shard_map/ppermute | solution.py:36
  532.9 8.6 %collective-permute-start.55 = (bf16[2,112,768]{2,1,0:T(8,128)(2,1)S(1)}, bf16[2,112,768]{2,1,0:T(8,128)(2,1)S(1)}, u32[]{:S(2)}, u32[]{:S(2)}) collective-permute-start(bf16[2,112,768]{2,1,0:T(8,128)(2,1)S(1)} %pad_maximum_fusion.11), channel_id=1, source_target_pairs={{0,48},{1,49},{2,50},{3,51},{4,52},{5,53},{6,54},{7,55},{8,56},{9,... | collective-permute-start | bytes 1032200 | tf_op jit(solution)/shard_map/ppermute | solution.py:36
  536.9 71.4 %collective-permute-start.98 = (bf16[2,4,96,768]{3,2,1,0:T(8,128)(2,1)}, bf16[2,4,96,768]{3,2,1,0:T(8,128)(2,1)}, u32[]{:S(2)}, u32[]{:S(2)}) collective-permute-start(bf16[2,4,96,768]{3,2,1,0:T(8,128)(2,1)} %slice_bitcast_fusion.1), channel_id=1, source_target_pairs={{0,8},{1,9},{2,10},{3,11},{4,12},{5,13},{6,14},{7,15},{8,4},{9,5},... | collective-permute-start | bytes 3538952 | tf_op jit(solution)/shard_map/ppermute | solution.py:44
  544.8 63.6 %collective-permute-start.99 = (bf16[2,4,96,768]{3,2,1,0:T(8,128)(2,1)S(1)}, bf16[2,4,96,768]{3,2,1,0:T(8,128)(2,1)}, u32[]{:S(2)}, u32[]{:S(2)}) collective-permute-start(bf16[2,4,96,768]{3,2,1,0:T(8,128)(2,1)S(1)} %dynamic-slice_bitcast_fusion.2), channel_id=1, source_target_pairs={{0,12},{1,13},{2,14},{3,15},{4,8},{5,9},{6,10},{7,11},{8,0},{9,1},... | collective-permute-start | bytes 3538952 | tf_op jit(solution)/shard_map/ppermute | solution.py:44
  547.8 14.8 %collective-permute-start.57 = (bf16[56,768]{1,0:T(8,128)(2,1)S(1)}, bf16[56,768]{1,0:T(8,128)(2,1)S(1)}, u32[]{:S(2)}, u32[]{:S(2)}) collective-permute-start(bf16[56,768]{1,0:T(8,128)(2,1)S(1)} %pad_maximum_fusion.19), channel_id=1, source_target_pairs={{0,1},{1,2},{2,3},{3,0},{4,5},{5,6},{6,7},{7,4},{8,9},{9,10},{10,1... | collective-permute-start | bytes 258056 | tf_op jit(solution)/shard_map/ppermute | solution.py:40
  548.3 16.6 %collective-permute-start.59 = (bf16[56,768]{1,0:T(8,128)(2,1)S(1)}, bf16[56,768]{1,0:T(8,128)(2,1)S(1)}, u32[]{:S(2)}, u32[]{:S(2)}) collective-permute-start(bf16[56,768]{1,0:T(8,128)(2,1)S(1)} %pad_maximum_fusion.20), channel_id=1, source_target_pairs={{0,3},{1,0},{2,1},{3,2},{4,7},{5,4},{6,5},{7,6},{8,11},{9,8},{10,9... | collective-permute-start | bytes 258056 | tf_op jit(solution)/shard_map/ppermute | solution.py:40
  562.6 48.8 %collective-permute-start.66 = (bf16[2,4,96,768]{3,2,1,0:T(8,128)(2,1)S(1)}, bf16[2,4,96,768]{3,2,1,0:T(8,128)(2,1)S(1)}, u32[]{:S(2)}, u32[]{:S(2)}) collective-permute-start(bf16[2,4,96,768]{3,2,1,0:T(8,128)(2,1)S(1)} %slice_bitcast_fusion.2), channel_id=1, source_target_pairs={{0,8},{1,9},{2,10},{3,11},{4,12},{5,13},{6,14},{7,15},{8,4},{9,5},... | collective-permute-start | bytes 3538952 | tf_op jit(solution)/shard_map/ppermute | solution.py:44
  565.0 46.4 %collective-permute-start.67 = (bf16[2,4,96,768]{3,2,1,0:T(8,128)(2,1)S(1)}, bf16[2,4,96,768]{3,2,1,0:T(8,128)(2,1)S(1)}, u32[]{:S(2)}, u32[]{:S(2)}) collective-permute-start(bf16[2,4,96,768]{3,2,1,0:T(8,128)(2,1)S(1)} %dynamic-slice_bitcast_fusion.5), channel_id=1, source_target_pairs={{0,12},{1,13},{2,14},{3,15},{4,8},{5,9},{6,10},{7,11},{8,0},{9,1},... | collective-permute-start | bytes 3538952 | tf_op jit(solution)/shard_map/ppermute | solution.py:44
  565.0 30.4 %collective-permute-start.60 = (bf16[56,768]{1,0:T(8,128)(2,1)S(1)}, bf16[56,768]{1,0:T(8,128)(2,1)S(1)}, u32[]{:S(2)}, u32[]{:S(2)}) collective-permute-start(bf16[56,768]{1,0:T(8,128)(2,1)S(1)} %add_convert_fusion.9), channel_id=1, source_target_pairs={{0,4},{1,5},{2,6},{3,7},{4,0},{5,1},{6,2},{7,3},{8,12},{9,13},{10,... | collective-permute-start | bytes 258056 | tf_op jit(solution)/shard_map/ppermute | solution.py:44
  608.3 57.6 %collective-permute-start.63 = (bf16[28,768]{1,0:T(8,128)(2,1)S(1)}, bf16[28,768]{1,0:T(8,128)(2,1)S(1)}, u32[]{:S(2)}, u32[]{:S(2)}) collective-permute-start(bf16[28,768]{1,0:T(8,128)(2,1)S(1)} %slice.675), channel_id=1, source_target_pairs={{0,1},{1,2},{2,3},{3,0},{4,5},{5,6},{6,7},{7,4},{8,9},{9,10},{10,1... | collective-permute-start | bytes 129032 | tf_op jit(solution)/shard_map/ppermute | solution.py:40
  619.7 11.5 %collective-permute-start.69 = (bf16[4,96,768]{2,1,0:T(8,128)(2,1)S(1)}, bf16[4,96,768]{2,1,0:T(8,128)(2,1)S(1)}, u32[]{:S(2)}, u32[]{:S(2)}) collective-permute-start(bf16[4,96,768]{2,1,0:T(8,128)(2,1)S(1)} %pad_maximum_fusion.6), channel_id=1, source_target_pairs={{0,16},{1,17},{2,18},{3,19},{4,20},{5,21},{6,22},{7,23},{8,24},{9,... | collective-permute-start | bytes 1769480 | tf_op jit(solution)/shard_map/ppermute | solution.py:36
  619.9 13.8 %collective-permute-start.71 = (bf16[4,96,768]{2,1,0:T(8,128)(2,1)S(1)}, bf16[4,96,768]{2,1,0:T(8,128)(2,1)S(1)}, u32[]{:S(2)}, u32[]{:S(2)}) collective-permute-start(bf16[4,96,768]{2,1,0:T(8,128)(2,1)S(1)} %pad_maximum_fusion.7), channel_id=1, source_target_pairs={{0,48},{1,49},{2,50},{3,51},{4,52},{5,53},{6,54},{7,55},{8,56},{9,... | collective-permute-start | bytes 1769480 | tf_op jit(solution)/shard_map/ppermute | solution.py:36
  622.8 20.9 %collective-permute-start.101 = (bf16[4,96,768]{2,1,0:T(8,128)(2,1)S(1)}, bf16[4,96,768]{2,1,0:T(8,128)(2,1)S(1)}, u32[]{:S(2)}, u32[]{:S(2)}) collective-permute-start(bf16[4,96,768]{2,1,0:T(8,128)(2,1)S(1)} %pad_maximum_fusion.8), channel_id=1, source_target_pairs={{0,16},{1,17},{2,18},{3,19},{4,20},{5,21},{6,22},{7,23},{8,24},{9,... | collective-permute-start | bytes 1769480 | tf_op jit(solution)/shard_map/ppermute | solution.py:36
  623.1 23.3 %collective-permute-start.103 = (bf16[4,96,768]{2,1,0:T(8,128)(2,1)S(1)}, bf16[4,96,768]{2,1,0:T(8,128)(2,1)S(1)}, u32[]{:S(2)}, u32[]{:S(2)}) collective-permute-start(bf16[4,96,768]{2,1,0:T(8,128)(2,1)S(1)} %pad_maximum_fusion.9), channel_id=1, source_target_pairs={{0,48},{1,49},{2,50},{3,51},{4,52},{5,53},{6,54},{7,55},{8,56},{9,... | collective-permute-start | bytes 1769480 | tf_op jit(solution)/shard_map/ppermute | solution.py:36
  631.1 34.8 %collective-permute-start.64 = (bf16[28,768]{1,0:T(8,128)(2,1)S(1)}, bf16[28,768]{1,0:T(8,128)(2,1)S(1)}, u32[]{:S(2)}, u32[]{:S(2)}) collective-permute-start(bf16[28,768]{1,0:T(8,128)(2,1)S(1)} %slice.676), channel_id=1, source_target_pairs={{0,3},{1,0},{2,1},{3,2},{4,7},{5,4},{6,5},{7,6},{8,11},{9,8},{10,9... | collective-permute-start | bytes 129032 | tf_op jit(solution)/shard_map/ppermute | solution.py:40
  634.0 12.8 %collective-permute-start.72 = (bf16[48,768]{1,0:T(8,128)(2,1)S(1)}, bf16[48,768]{1,0:T(8,128)(2,1)S(1)}, u32[]{:S(2)}, u32[]{:S(2)}) collective-permute-start(bf16[48,768]{1,0:T(8,128)(2,1)S(1)} %get-tuple-element.149), channel_id=1, source_target_pairs={{0,1},{1,2},{2,3},{3,0},{4,5},{5,6},{6,7},{7,4},{8,9},{9,10},{10,1... | collective-permute-start | bytes 221192 | tf_op jit(solution)/shard_map/ppermute | solution.py:40
  661.3 22.3 %collective-permute-start.77 = (bf16[96,768]{1,0:T(8,128)(2,1)S(1)}, bf16[96,768]{1,0:T(8,128)(2,1)S(1)}, u32[]{:S(2)}, u32[]{:S(2)}) collective-permute-start(bf16[96,768]{1,0:T(8,128)(2,1)S(1)} %get-tuple-element.92), channel_id=1, source_target_pairs={{0,1},{1,2},{2,3},{3,0},{4,5},{5,6},{6,7},{7,4},{8,9},{9,10},{10,1... | collective-permute-start | bytes 442376 | tf_op jit(solution)/shard_map/ppermute | solution.py:40
  661.9 23.3 %collective-permute-start.78 = (bf16[96,768]{1,0:T(8,128)(2,1)S(1)}, bf16[96,768]{1,0:T(8,128)(2,1)S(1)}, u32[]{:S(2)}, u32[]{:S(2)}) collective-permute-start(bf16[96,768]{1,0:T(8,128)(2,1)S(1)} %get-tuple-element.92), channel_id=1, source_target_pairs={{0,3},{1,0},{2,1},{3,2},{4,7},{5,4},{6,5},{7,6},{8,11},{9,8},{10,9... | collective-permute-start | bytes 442376 | tf_op jit(solution)/shard_map/ppermute | solution.py:40
  664.1 21.2 %collective-permute-start.109 = (bf16[96,768]{1,0:T(8,128)(2,1)S(1)}, bf16[96,768]{1,0:T(8,128)(2,1)S(1)}, u32[]{:S(2)}, u32[]{:S(2)}) collective-permute-start(bf16[96,768]{1,0:T(8,128)(2,1)S(1)} %get-tuple-element.96), channel_id=1, source_target_pairs={{0,1},{1,2},{2,3},{3,0},{4,5},{5,6},{6,7},{7,4},{8,9},{9,10},{10,1... | collective-permute-start | bytes 442376 | tf_op jit(solution)/shard_map/ppermute | solution.py:40
  665.9 22.1 %collective-permute-start.110 = (bf16[96,768]{1,0:T(8,128)(2,1)S(1)}, bf16[96,768]{1,0:T(8,128)(2,1)S(1)}, u32[]{:S(2)}, u32[]{:S(2)}) collective-permute-start(bf16[96,768]{1,0:T(8,128)(2,1)S(1)} %get-tuple-element.96), channel_id=1, source_target_pairs={{0,3},{1,0},{2,1},{3,2},{4,7},{5,4},{6,5},{7,6},{8,11},{9,8},{10,9... | collective-permute-start | bytes 442376 | tf_op jit(solution)/shard_map/ppermute | solution.py:40
  666.0 30.4 %collective-permute-start.47 = (bf16[128,768]{1,0:T(8,128)(2,1)S(1)}, bf16[128,768]{1,0:T(8,128)(2,1)S(1)}, u32[]{:S(2)}, u32[]{:S(2)}) collective-permute-start(bf16[128,768]{1,0:T(8,128)(2,1)S(1)} %copy-done.80), channel_id=1, source_target_pairs={{0,64},{64,0},{1,65},{65,1},{2,66},{66,2},{3,67},{67,3},{4,68},{68... | collective-permute-start | bytes 589832 | tf_op jit(solution)/shard_map/ppermute | solution.py:48
  (158 other events, 1561.3 us)

commit v2 on v1

v2 whole, which is shorter than its diff:
```python
import functools

import jax
import jax.numpy as jnp
from jax import lax
from jax.experimental import pallas as pl
from jax.experimental.pallas import tpu as pltpu
from jax.sharding import PartitionSpec as P

WIDTH = 768
GROUPS = 8
PAIRS = 6
SEQ = 1024
ROWS = 128
BLOCK = 256
SHARD = 96
HALF = 48
SLIM = 192
WIDE = 384
VEC_ROWS = 16
EPSILON = 1e-05
VMEM_BYTES = 40 * 1024 * 1024
GELU_C = 0.7978845608028654
BF = jnp.bfloat16
F32 = jnp.float32


def torus_pairs(move):
    pairs = []
    for source in range(64):
        group, replica = divmod(source, 8)
        x, z_lo = divmod(group, 2)
        z_hi, y = divmod(replica, 4)
        x, y, z = move(x, y, z_hi * 2 + z_lo)
        pairs.append((source, ((x % 4) * 2 + z % 2) * 8 + (z % 4) // 2 * 4 + y % 4))
    return pairs


def along_x(value, by):
    return lax.ppermute(value, ("group", "replica"), torus_pairs(lambda x, y, z: (x + by, y, z)))


def along_y(value, by):
    return lax.ppermute(value, ("group", "replica"), torus_pairs(lambda x, y, z: (x, y + by, z)))


def along_z(value, by):
    return lax.ppermute(value, ("group", "replica"), torus_pairs(lambda x, y, z: (x, y, z + by)))


def swap(value):
    return lax.ppermute(value, "section", [(0, 1), (1, 0)])


def tie(*values):
    return lax.optimization_barrier(values)


def pick(on_first, on_second):
    return jnp.where(lax.axis_index("section") == 0, on_first, on_second)


class Gather:
    def __init__(self, shard):
        self.shard = shard
        self.cut = shard.shape[0] // 2

    def near(self):
        shard, cut = self.shard, self.cut
        self.left = along_x(shard, 1)
        self.right = along_x(shard, -1)
        self.z_low = along_z(shard[:cut], 1)
        self.z_high = along_z(shard[cut:], -1)

    def far(self):
        cut = self.cut
        self.far_low = along_x(self.left[:cut], 1)
        self.far_high = along_x(self.right[cut:], -1)
        self.z_left = along_z(self.left, 1)
        self.z_right = along_z(self.right, -1)

    def last(self):
        self.z_far_low = along_z(self.far_low, 1)
        self.z_far_high = along_z(self.far_high, -1)

    def after(self, *values):
        names = [name for name in vars(self) if name not in ("cut",)]
        count = len(names)
        tied = tie(*(getattr(self, name) for name in names), *values)
        for name, value in zip(names, tied):
            setattr(self, name, value)
        return tied[count:] if len(values) != 1 else tied[count]

    def whole(self):
        pieces = (
            self.shard,
            self.left,
            self.right,
            self.far_low,
            self.far_high,
            self.z_low,
            self.z_high,
            self.z_left,
            self.z_right,
            self.z_far_low,
            self.z_far_high,
        )
        return assemble(self.cut, *pieces)


def add(left, right):
    return left.astype(F32) + right.astype(F32)


class GroupSum:
    def __init__(self, pairs):
        self.own, away_low, away_high = sum_pairs(pairs)
        self.low = along_z(away_low, 1)
        self.high = along_z(away_high, -1)

    def far(self):
        self.zero, self.one, self.minus, two_low, two_high = sum_z(self.own, self.low, self.high)
        self.from_left = along_x(two_low, 1)
        self.from_right = along_x(two_high, -1)

    def near(self):
        one, minus = sum_far(self.one, self.minus, self.from_left, self.from_right)
        self.one = along_x(one, 1)
        self.minus = along_x(minus, -1)

    def total(self):
        return self.zero.astype(F32) + self.one.astype(F32) + self.minus.astype(F32)


class RingSum:
    def __init__(self, parts, place, along):
        self.parts, self.place, self.along = parts, place, along
        self.cut = parts.shape[1] // 2

    def piece(self, k):
        return lax.dynamic_index_in_dim(self.parts, lax.rem(self.place + k, 4), 0, keepdims=False)

    def far(self):
        two, cut = self.piece(2), self.cut
        self.from_left = self.along(two[:cut], 1)
        self.from_right = self.along(two[cut:], -1)

    def near(self):
        one, minus, cut = self.piece(1), self.piece(3), self.cut
        one = jnp.concatenate([add(one[:cut], self.from_left).astype(BF), one[cut:]], axis=0)
        minus = jnp.concatenate([minus[:cut], add(minus[cut:], self.from_right).astype(BF)], axis=0)
        self.one = self.along(one, 1)
        self.minus = self.along(minus, -1)

    def total(self):
        return self.piece(0).astype(F32) + self.one.astype(F32) + self.minus.astype(F32)


def over_replica(total):
    y = lax.rem(lax.axis_index("replica"), 4)
    rows, width = total.shape
    quarter = rows // 4
    half = quarter // 2
    ring = RingSum(total.astype(BF).reshape(4, quarter, width), y, along_y)
    ring.far()
    ring.near()
    mine = ring.total().astype(BF)
    mine = add(mine, along_z(mine, 2)).astype(BF)
    left = along_y(mine, 1)
    right = along_y(mine, -1)
    far = jnp.concatenate([along_y(left[:half], 1), along_y(right[half:], -1)], axis=0)
    full = jnp.zeros((4, quarter, width), BF)
    for piece, k in ((mine, 0), (left, 3), (right, 1), (far, 2)):
        full = lax.dynamic_update_slice(full, piece[None], (lax.rem(y + k, 4), 0, 0))
    return full.reshape(rows, width)


def over_all(parts):
    _, rows, width = parts.shape
    piece = rows // 8
    arrived = lax.all_to_all(parts.reshape(64, piece, width), ("group", "replica"), 0, 0, tiled=True)
    mine = jnp.sum(arrived.astype(F32), axis=0).astype(BF)
    spread = jnp.broadcast_to(mine[None], (8, piece, width))
    return lax.all_to_all(spread, "replica", 0, 0, tiled=True).reshape(rows, width)


def dot(left, right):
    return jnp.dot(left, right, preferred_element_type=F32)


def dot_rows(left, right):
    return lax.dot_general(left, right, (((0,), (0,)), ((), ())), preferred_element_type=F32)


def dot_columns(left, right):
    return lax.dot_general(left, right, (((1,), (1,)), ((), ())), preferred_element_type=F32)


def normalized(rows):
    center = rows - jnp.mean(rows, axis=-1, keepdims=True)
    scale = lax.rsqrt(jnp.mean(center * center, axis=-1, keepdims=True) + EPSILON)
    return center * scale, scale


def norm_back(grad, gain, unit, scale):
    inner = grad * gain
    return scale * (
        inner
        - jnp.mean(inner, axis=-1, keepdims=True)
        - unit * jnp.mean(inner * unit, axis=-1, keepdims=True)
    )


def column_sums(rows):
    return jnp.sum(rows, axis=0, keepdims=True)


PLACES = (
    (0, False, False),
    (3, False, False),
    (1, False, False),
    (2, False, False),
    (2, False, True),
    (0, True, False),
    (0, True, True),
    (3, True, False),
    (1, True, False),
    (2, True, False),
    (2, True, True),
)


def assemble_rows(cut, *refs):
    pieces, full = refs[: len(PLACES)], refs[len(PLACES)]
    group = lax.axis_index("group")
    x, z = group // 2, group % 2
    for piece, (dx, flip, high) in zip(pieces, PLACES):
        at = lax.rem(x + dx, 4) * 2 + (1 - z if flip else z)
        row = cut if high else 0
        full[pl.ds(at, 1), row : row + piece.shape[0]] = piece[...][None]


def assemble(cut, *pieces):
    rows = pieces[0].shape[0]
    return pl.pallas_call(
        functools.partial(assemble_rows, cut),
        in_specs=[pl.BlockSpec(memory_space=pltpu.VMEM)] * len(PLACES),
        out_specs=pl.BlockSpec(memory_space=pltpu.VMEM),
        out_shape=jax.ShapeDtypeStruct((GROUPS, rows, WIDTH), BF),
        compiler_params=pltpu.CompilerParams(vmem_limit_bytes=VMEM_BYTES),
        cost_estimate=cost(4),
        name="assemble",
    )(*pieces)


def pack_shard(section_ref, qkv_ref, out_ref, fc_ref, proj_ref, bias_ref, *refs):
    vectors, (keep_ref, away_ref) = refs[:8], refs[8:]
    on_first = section_ref[0] == 0

    def put(row, low, high):
        at = slice(row, row + low.shape[0])
        keep_ref[at, :] = lax.select(on_first, low, high)
        away_ref[at, :] = lax.select(on_first, high, low)

    for j in range(3):
        at = slice(WIDTH * j, WIDTH * (j + 1))
        put(HALF * j, qkv_ref[0, :HALF, at], qkv_ref[0, HALF:, at])
    put(3 * HALF, out_ref[0, :HALF], out_ref[0, HALF:])
    for j in range(4):
        at = slice(WIDTH * j, WIDTH * (j + 1))
        put(SLIM + VEC_ROWS + HALF * j, fc_ref[0, :HALF, at], fc_ref[0, HALF:, at])
    put(SLIM + VEC_ROWS + 4 * HALF, proj_ref[0, : 4 * HALF], proj_ref[0, 4 * HALF :])
    rows = jnp.concatenate([ref[...].astype(F32) for ref in vectors], axis=0)
    rows = jnp.concatenate([rows, jnp.zeros((8, WIDTH - SHARD), F32)], axis=1)
    bias = jnp.concatenate([bias_ref[...].astype(F32), jnp.zeros((1, WIDTH // 2), F32)], axis=1)
    rows = jnp.concatenate([rows, bias, jnp.zeros((7, WIDTH), F32)], axis=0).astype(BF)
    put(SLIM, rows, rows)


def run_pack_shard(section, qkv, out_w, fc, proj, bias, *vectors):
    vmem = pl.BlockSpec(memory_space=pltpu.VMEM)
    shape = jax.ShapeDtypeStruct((SLIM + VEC_ROWS + WIDE, WIDTH), BF)
    return pl.pallas_call(
        pack_shard,
        in_specs=[pl.BlockSpec(memory_space=pltpu.SMEM)] + [vmem] * 13,
        out_specs=[vmem, vmem],
        out_shape=[shape, shape],
        compiler_params=pltpu.CompilerParams(vmem_limit_bytes=VMEM_BYTES),
        cost_estimate=cost(3),
        name="pack_shard",
    )(section, qkv, out_w, fc, proj, bias, *vectors)


def one_hot(group):
    row = lax.broadcasted_iota(jnp.int32, (128, WIDTH), 0)
    lane = lax.broadcasted_iota(jnp.int32, (128, WIDTH), 1)
    return jnp.where((lane == row + SHARD * group) & (row < SHARD), 1.0, 0.0).astype(BF)


def unpack_vectors(mine_ref, vecs_ref):
    total = jnp.zeros((2 * VEC_ROWS, WIDTH), F32)
    for group in range(GROUPS):
        total = total + dot(mine_ref[group, :, :128], one_hot(group))
    for layer in range(2):
        vecs_ref[layer, 0:8, :] = total[VEC_ROWS * layer : VEC_ROWS * layer + 8]
        for j in range(4):
            for side in range(2):
                piece = mine_ref[2 * j + side, VEC_ROWS * layer : VEC_ROWS * (layer + 1), : WIDTH // 2]
                at = slice(side * (WIDTH // 2), (side + 1) * (WIDTH // 2))
                vecs_ref[layer, 8 + j : 9 + j, at] = piece.astype(F32)[8:9]


def run_unpack_vectors(mine):
    return pl.pallas_call(
        unpack_vectors,
        grid=(1,),
        in_specs=[pl.BlockSpec((GROUPS, 2 * VEC_ROWS, WIDTH), lambda step: (0, SLIM // (2 * VEC_ROWS), 0))],
        out_specs=whole(2, 12, WIDTH),
        out_shape=jax.ShapeDtypeStruct((2, 12, WIDTH), F32),
        cost_estimate=cost(2),
        name="unpack_vectors",
    )(mine)


def pack_vectors(vecs_ref, out_ref):
    for group in range(GROUPS):
        for layer in range(2):
            rows = lax.dot_general(
                vecs_ref[layer, 0:8, :].astype(BF),
                one_hot(group),
                (((1,), (1,)), ((), ())),
                preferred_element_type=F32,
            )
            rows = jnp.concatenate([rows, jnp.zeros((8, WIDTH - 128), F32)], axis=1)
            side = group % 2
            at = slice(side * (WIDTH // 2), (side + 1) * (WIDTH // 2))
            bias = vecs_ref[layer, 8 + group // 2 : 9 + group // 2, at]
            bias = jnp.concatenate([bias, jnp.zeros((1, WIDTH // 2), F32)], axis=1)
            rows = jnp.concatenate([rows, bias, jnp.zeros((7, WIDTH), F32)], axis=0)
            out_ref[group, VEC_ROWS * layer : VEC_ROWS * (layer + 1)] = rows.astype(BF)


def run_pack_vectors(vecs):
    return pl.pallas_call(
        pack_vectors,
        grid=(1,),
        in_specs=[whole(2, 12, WIDTH)],
        out_specs=whole(GROUPS, 2 * VEC_ROWS, WIDTH),
        out_shape=jax.ShapeDtypeStruct((GROUPS, 2 * VEC_ROWS, WIDTH), BF),
        cost_estimate=cost(2),
        name="pack_vectors",
    )(vecs)


def put_pairs(ref, rows, *index):
    for pair in range(PAIRS):
        ref[(pair, *index)] = rows[:, pair * 128 : (pair + 1) * 128]
    for pair in range(PAIRS, GROUPS):
        ref[(pair, *index)] = jnp.zeros((ROWS, 128), BF)


def weave(section_ref, mine_ref, other_ref):
    on_first = section_ref[0] == 0
    mine, other = mine_ref[...], other_ref[...]
    both = [lax.select(on_first, mine, other), lax.select(on_first, other, mine)]
    return jnp.concatenate(both, axis=1).reshape(WIDTH, WIDTH)


def unweave(section_ref, rows, keep_ref, away_ref):
    on_first = section_ref[0] == 0
    groups, half, _ = keep_ref.shape
    rows = rows.reshape(groups, 2 * half, WIDTH)
    low, high = rows[:, :half], rows[:, half:]
    keep_ref[...] = lax.select(on_first, low, high)
    away_ref[...] = lax.select(on_first, high, low)


def pre_forward(section_ref, x_ref, vec_ref, mine_ref, other_ref, n1_ref, send_ref):
    step = pl.program_id(0)

    @pl.when(step == 0)
    def _():
        unit, _ = normalized(x_ref[...].astype(F32))
        n1_ref[...] = (unit * vec_ref[0:1, :] + vec_ref[1:2, :]).astype(BF)

    bias = jnp.where(step == 0, vec_ref[2:3, :], jnp.where(step == 2, vec_ref[3:4, :], 0.0))
    product = dot(n1_ref[...], weave(section_ref, mine_ref, other_ref))
    put_pairs(send_ref, (product + bias).astype(BF), 0)


def visible(length_ref, at, columns):
    first_end = length_ref[0]
    second_end = first_end + length_ref[1]
    row = lax.broadcasted_iota(jnp.int32, (BLOCK, 1), 0) + at
    start = jnp.where(row >= second_end, second_end, jnp.where(row >= first_end, first_end, 0))
    column = lax.broadcasted_iota(jnp.int32, (BLOCK, columns), 1)
    return (column >= start) & (column <= row)


def of_head(rows, head):
    lane = lax.broadcasted_iota(jnp.int32, rows.shape, 1)
    keep = lane < 64 if head == 0 else lane >= 64
    return jnp.where(keep, rows, jnp.zeros_like(rows))


def both_heads(first, second):
    lane = lax.broadcasted_iota(jnp.int32, first.shape, 1)
    return jnp.where(lane < 64, first, second)


def attend_forward(length_ref, qkv_ref, out_ref, logsum_ref):
    for block in range(SEQ // BLOCK):
        keys = (block + 1) * BLOCK
        query = qkv_ref[2 * block : 2 * block + 2, 0].reshape(BLOCK, 128)
        query = (query.astype(F32) * 0.125).astype(BF)
        key = qkv_ref[: 2 * block + 2, 1].reshape(keys, 128)
        value = qkv_ref[: 2 * block + 2, 2].reshape(keys, 128)
        allowed = visible(length_ref, block * BLOCK, keys)
        mixed, sums = [], []
        for head in range(2):
            scores = dot_columns(of_head(query, head), key)
            scores = jnp.where(allowed, scores, -1e30)
            maximum = jnp.max(scores, axis=-1, keepdims=True)
            expo = jnp.exp(scores - maximum)
            total = jnp.sum(expo, axis=-1, keepdims=True)
            mixed.append(dot((expo * (1.0 / total)).astype(BF), value))
            sums.append(jnp.broadcast_to(maximum + jnp.log(total), (BLOCK, 128)))
        out_ref[2 * block : 2 * block + 2] = both_heads(*mixed).astype(BF).reshape(2, 128, 128)
        logsum_ref[block * BLOCK : (block + 1) * BLOCK, :] = both_heads(*sums)


def attend_backward(length_ref, qkv_ref, grad_ref, logsum_ref, out_ref, key_acc, value_acc):
    key_acc[...] = jnp.zeros_like(key_acc)
    value_acc[...] = jnp.zeros_like(value_acc)
    for block in range(SEQ // BLOCK):
        keys = (block + 1) * BLOCK
        query = qkv_ref[2 * block : 2 * block + 2, 0].reshape(BLOCK, 128)
        query = (query.astype(F32) * 0.125).astype(BF)
        grad = grad_ref[2 * block : 2 * block + 2].reshape(BLOCK, 128)
        key = qkv_ref[: 2 * block + 2, 1].reshape(keys, 128)
        value = qkv_ref[: 2 * block + 2, 2].reshape(keys, 128)
        allowed = visible(length_ref, block * BLOCK, keys)
        grad_query = []
        for head in range(2):
            query_one, grad_one = of_head(query, head), of_head(grad, head)
            logsum = logsum_ref[block * BLOCK : (block + 1) * BLOCK, 64 * head : 64 * head + 1]
            scores = jnp.where(allowed, dot_columns(query_one, key), -1e30)
            probs = jnp.exp(scores - logsum)
            grad_probs = dot_columns(grad_one, value)
            delta = jnp.sum(probs * grad_probs, axis=-1, keepdims=True)
            grad_scores = (probs * (grad_probs - delta)).astype(BF)
            grad_query.append(dot(grad_scores, key))
            key_acc[:keys, :] += dot_rows(grad_scores, query_one)
            value_acc[:keys, :] += dot_rows(probs.astype(BF), grad_one)
        out = (both_heads(*grad_query) * 0.125).astype(BF)
        out_ref[2 * block : 2 * block + 2, 0] = out.reshape(2, 128, 128)
    out_ref[:, 1] = key_acc[...].astype(BF).reshape(GROUPS, 128, 128)
    out_ref[:, 2] = value_acc[...].astype(BF).reshape(GROUPS, 128, 128)


def post_forward(
    section_ref,
    mixed_ref,
    x_ref,
    vec_ref,
    out_mine,
    out_other,
    fc_mine,
    fc_other,
    proj_mine,
    proj_other,
    y_ref,
    x1_ref,
    n2_ref,
    u_ref,
    acc,
):
    step = pl.program_id(0)

    @pl.when(step == 0)
    def _():
        mixed = jnp.concatenate([mixed_ref[pair] for pair in range(PAIRS)], axis=1)
        x1 = x_ref[...].astype(F32) + dot(mixed, weave(section_ref, out_mine, out_other))
        x1 = x1 + vec_ref[4:5, :]
        x1_ref[...] = x1
        unit, _ = normalized(x1)
        n2_ref[...] = (unit * vec_ref[5:6, :] + vec_ref[6:7, :]).astype(BF)
        acc[...] = x1 + vec_ref[7:8, :]

    u = dot(n2_ref[...], weave(section_ref, fc_mine, fc_other)) + vec_ref[pl.ds(8 + step, 1), :]
    u_ref[0] = u
    active = 0.5 * u * (1.0 + jnp.tanh(GELU_C * (u + 0.044715 * (u * u * u))))
    acc[...] += dot(active.astype(BF), weave(section_ref, proj_mine, proj_other))

    @pl.when(step == 3)
    def _():
        y_ref[...] = acc[...].astype(BF)


def post_backward(
    section_ref,
    dy_ref,
    u_ref,
    n2_ref,
    x1_ref,
    mixed_ref,
    vec_ref,
    out_mine,
    out_other,
    fc_mine,
    fc_other,
    proj_mine,
    proj_other,
    dx1_ref,
    send_ref,
    dvec_ref,
    dout_keep,
    dout_away,
    dfc_keep,
    dfc_away,
    dproj_keep,
    dproj_away,
    acc,
):
    step = pl.program_id(0)
    dy = dy_ref[...].astype(F32)
    low = dy.astype(BF)

    @pl.when(step == 0)
    def _():
        acc[...] = jnp.zeros_like(acc)

    u = u_ref[0]
    square = u * u
    tanh = jnp.tanh(GELU_C * (u + 0.044715 * (square * u)))
    active = (0.5 * u * (1.0 + tanh)).astype(BF)
    slope = 0.5 * (1.0 + tanh) + 0.5 * u * (1.0 - tanh * tanh) * (
        GELU_C * (1.0 + 3.0 * 0.044715 * square)
    )
    du = (dot_columns(low, weave(section_ref, proj_mine, proj_other)) * slope).astype(BF)
    unweave(section_ref, dot_rows(active, low).astype(BF), dproj_keep, dproj_away)
    unweave(section_ref, dot_rows(n2_ref[...], du).astype(BF), dfc_keep, dfc_away)
    dvec_ref[pl.ds(8 + step, 1), :] = column_sums(du.astype(F32))
    acc[...] += dot_columns(du, weave(section_ref, fc_mine, fc_other))

    @pl.when(step == 3)
    def _():
        dn2 = acc[...]
        unit, scale = normalized(x1_ref[...])
        dx1 = dy + norm_back(dn2, vec_ref[5:6, :], unit, scale)
        dx1_ref[...] = dx1
        back = dx1.astype(BF)
        mixed = jnp.concatenate([mixed_ref[pair] for pair in range(PAIRS)], axis=1)
        unweave(section_ref, dot_rows(mixed, back).astype(BF), dout_keep, dout_away)
        put_pairs(send_ref, dot_columns(back, weave(section_ref, out_mine, out_other)).astype(BF))
        dvec_ref[0:4, :] = jnp.zeros((4, WIDTH), F32)
        dvec_ref[4:5, :] = column_sums(back.astype(F32))
        dvec_ref[5:6, :] = column_sums(dn2 * unit)
        dvec_ref[6:7, :] = column_sums(dn2)
        dvec_ref[7:8, :] = column_sums(low.astype(F32))


def pre_backward(
    section_ref,
    grads_ref,
    n1_ref,
    x_ref,
    dx1_ref,
    vec_ref,
    mine_ref,
    other_ref,
    dx_ref,
    dvec_ref,
    keep_ref,
    away_ref,
    acc,
):
    step = pl.program_id(0)

    @pl.when(step == 0)
    def _():
        acc[...] = jnp.zeros_like(acc)
        dvec_ref[...] = jnp.zeros_like(dvec_ref)

    rows = jnp.concatenate([grads_ref[pair, 0] for pair in range(PAIRS)], axis=1)
    unweave(section_ref, dot_rows(n1_ref[...], rows).astype(BF), keep_ref, away_ref)
    acc[...] += dot_columns(rows, weave(section_ref, mine_ref, other_ref))

    @pl.when(step == 0)
    def _():
        dvec_ref[2:3, :] = column_sums(rows.astype(F32))

    @pl.when(step == 2)
    def _():
        dvec_ref[3:4, :] = column_sums(rows.astype(F32))
        dn1 = acc[...]
        unit, scale = normalized(x_ref[...].astype(F32))
        dx_ref[...] = (dx1_ref[...] + norm_back(dn1, vec_ref[0:1, :], unit, scale)).astype(BF)
        dvec_ref[0:1, :] = column_sums(dn1 * unit)
        dvec_ref[1:2, :] = column_sums(dn1)


def whole(*shape):
    return pl.BlockSpec(shape, lambda *_: (0,) * len(shape))


def stepped(*shape):
    return pl.BlockSpec(shape, lambda step: (step,) + (0,) * (len(shape) - 1))


def out(shape, kind):
    return jax.ShapeDtypeStruct(shape, kind)


def params():
    return pltpu.CompilerParams(vmem_limit_bytes=VMEM_BYTES)


def cost(us):
    return pl.CostEstimate(
        flops=int(us * 4e8), bytes_accessed=int(us * 3e6), transcendentals=0
    )


def middle(rows):
    return rows // 32 * 16


def sum_pairs_kernel(*refs):
    own_ref, low_ref, high_ref = refs[-3:]
    pairs = refs[:-3]
    on_first = lax.axis_index("group") % 2 == 0
    cut = low_ref.shape[1]
    total = [add(keep[...], got[...]).astype(BF) for keep, got in zip(pairs[::2], pairs[1::2])]
    total = jnp.concatenate(total, axis=1) if len(total) > 1 else total[0]
    own_ref[0] = lax.select(on_first, total[0], total[1])
    away = lax.select(on_first, total[1], total[0])
    low_ref[0] = away[:cut]
    high_ref[0] = away[cut:]


def sum_pairs(pairs):
    rows = sum(keep.shape[1] for keep, _ in pairs)
    cut = middle(rows)
    specs = [
        pl.BlockSpec((2, keep.shape[1], WIDTH), lambda step: (step, 0, 0))
        for keep, _ in pairs
        for _ in range(2)
    ]
    return pl.pallas_call(
        sum_pairs_kernel,
        grid=(4,),
        in_specs=specs,
        out_specs=[stepped(1, rows, WIDTH), stepped(1, cut, WIDTH), stepped(1, rows - cut, WIDTH)],
        out_shape=[
            out((4, rows, WIDTH), BF),
            out((4, cut, WIDTH), BF),
            out((4, rows - cut, WIDTH), BF),
        ],
        compiler_params=params(),
        cost_estimate=cost(5),
        name="sum_pairs",
    )(*(value for pair in pairs for value in pair))


def sum_z_kernel(own_ref, low_ref, high_ref, zero_ref, one_ref, minus_ref, two_low_ref, two_high_ref):
    x = lax.axis_index("group") // 2
    cut, half = low_ref.shape[1], two_low_ref.shape[0]

    def piece(k):
        at = lax.rem(x + k, 4)
        from_z = jnp.concatenate([low_ref[at], high_ref[at]], axis=0)
        return add(own_ref[at], from_z).astype(BF)

    zero_ref[...] = piece(0)
    one_ref[...] = piece(1)
    minus_ref[...] = piece(3)
    two = piece(2)
    two_low_ref[...] = two[:half]
    two_high_ref[...] = two[half:]


def sum_z(own, low, high):
    rows = own.shape[1]
    half = middle(rows)
    vmem = pl.BlockSpec(memory_space=pltpu.VMEM)
    return pl.pallas_call(
        sum_z_kernel,
        in_specs=[vmem] * 3,
        out_specs=[vmem] * 5,
        out_shape=[out((rows, WIDTH), BF)] * 3 + [out((half, WIDTH), BF), out((rows - half, WIDTH), BF)],
        compiler_params=params(),
        cost_estimate=cost(4),
        name="sum_z",
    )(own, low, high)


def sum_far_kernel(one_ref, minus_ref, left_ref, right_ref, one_out, minus_out):
    half = left_ref.shape[0]
    one_out[:half, :] = add(one_ref[:half, :], left_ref[...]).astype(BF)
    one_out[half:, :] = one_ref[half:, :]
    minus_out[:half, :] = minus_ref[:half, :]
    minus_out[half:, :] = add(minus_ref[half:, :], right_ref[...]).astype(BF)


def sum_far(one, minus, from_left, from_right):
    vmem = pl.BlockSpec(memory_space=pltpu.VMEM)
    return pl.pallas_call(
        sum_far_kernel,
        in_specs=[vmem] * 4,
        out_specs=[vmem] * 2,
        out_shape=[out(one.shape, BF)] * 2,
        compiler_params=params(),
        cost_estimate=cost(2),
        name="sum_far",
    )(one, minus, from_left, from_right)


SMEM_SPEC = pl.BlockSpec(memory_space=pltpu.SMEM)
HEADS_SPEC = pl.BlockSpec((GROUPS, 1, ROWS, 128), lambda step: (0, step, 0, 0))
WIDE_SPEC = pl.BlockSpec((GROUPS, HALF, WIDTH), lambda step: (0, step, 0))
OUT_SPEC = pl.BlockSpec((GROUPS, HALF, WIDTH), lambda step: (0, 3, 0))
PROJ_SPEC = pl.BlockSpec((2, 4 * HALF, WIDTH), lambda step: (step, 1, 0))
DPROJ_SPEC = pl.BlockSpec((2, 4 * HALF, WIDTH), lambda step: (step, 0, 0))


def run_pre_forward(section, x, vec, slim):
    return pl.pallas_call(
        pre_forward,
        grid=(3,),
        in_specs=[SMEM_SPEC, whole(ROWS, WIDTH), whole(12, WIDTH), WIDE_SPEC, WIDE_SPEC],
        out_specs=[whole(ROWS, WIDTH), HEADS_SPEC],
        out_shape=[out((ROWS, WIDTH), BF), out((GROUPS, 3, ROWS, 128), BF)],
        compiler_params=params(),
        cost_estimate=cost(4),
        name="pre_forward",
    )(section, x, vec, *slim)


def run_attend_forward(length_row, qkv):
    return pl.pallas_call(
        attend_forward,
        grid=(1,),
        in_specs=[SMEM_SPEC, whole(GROUPS, 3, ROWS, 128)],
        out_specs=[whole(GROUPS, ROWS, 128), whole(SEQ, 128)],
        out_shape=[out((GROUPS, ROWS, 128), BF), out((SEQ, 128), F32)],
        compiler_params=params(),
        cost_estimate=cost(8),
        name="attend_forward",
    )(length_row, qkv)


def run_attend_backward(length_row, qkv, grad, logsum):
    return pl.pallas_call(
        attend_backward,
        grid=(1,),
        in_specs=[
            SMEM_SPEC,
            whole(GROUPS, 3, ROWS, 128),
            whole(GROUPS, ROWS, 128),
            whole(SEQ, 128),
        ],
        out_specs=whole(GROUPS, 3, ROWS, 128),
        out_shape=out((GROUPS, 3, ROWS, 128), BF),
        scratch_shapes=[pltpu.VMEM((SEQ, 128), F32), pltpu.VMEM((SEQ, 128), F32)],
        compiler_params=params(),
        cost_estimate=cost(16),
        name="attend_backward",
    )(length_row, qkv, grad, logsum)


def run_post_forward(section, mixed, x, vec, slim, wide):
    return pl.pallas_call(
        post_forward,
        grid=(4,),
        in_specs=[
            SMEM_SPEC,
            whole(GROUPS, ROWS, 128),
            whole(ROWS, WIDTH),
            whole(12, WIDTH),
            OUT_SPEC,
            OUT_SPEC,
            WIDE_SPEC,
            WIDE_SPEC,
            PROJ_SPEC,
            PROJ_SPEC,
        ],
        out_specs=[
            whole(ROWS, WIDTH),
            whole(ROWS, WIDTH),
            whole(ROWS, WIDTH),
            stepped(1, ROWS, WIDTH),
        ],
        out_shape=[
            out((ROWS, WIDTH), BF),
            out((ROWS, WIDTH), F32),
            out((ROWS, WIDTH), BF),
            out((4, ROWS, WIDTH), F32),
        ],
        scratch_shapes=[pltpu.VMEM((ROWS, WIDTH), F32)],
        compiler_params=params(),
        cost_estimate=cost(8),
        name="post_forward",
    )(section, mixed, x, vec, *slim, *wide, *wide)


def run_post_backward(section, dy, u, n2, x1, mixed, vec, slim, wide):
    return pl.pallas_call(
        post_backward,
        grid=(4,),
        in_specs=[
            SMEM_SPEC,
            whole(ROWS, WIDTH),
            stepped(1, ROWS, WIDTH),
            whole(ROWS, WIDTH),
            whole(ROWS, WIDTH),
            whole(GROUPS, ROWS, 128),
            whole(12, WIDTH),
            OUT_SPEC,
            OUT_SPEC,
            WIDE_SPEC,
            WIDE_SPEC,
            PROJ_SPEC,
            PROJ_SPEC,
        ],
        out_specs=[
            whole(ROWS, WIDTH),
            whole(GROUPS, ROWS, 128),
            whole(12, WIDTH),
            whole(GROUPS, HALF, WIDTH),
            whole(GROUPS, HALF, WIDTH),
            WIDE_SPEC,
            WIDE_SPEC,
            DPROJ_SPEC,
            DPROJ_SPEC,
        ],
        out_shape=[
            out((ROWS, WIDTH), F32),
            out((GROUPS, ROWS, 128), BF),
            out((12, WIDTH), F32),
            out((GROUPS, HALF, WIDTH), BF),
            out((GROUPS, HALF, WIDTH), BF),
            out((GROUPS, 4 * HALF, WIDTH), BF),
            out((GROUPS, 4 * HALF, WIDTH), BF),
            out((GROUPS, 4 * HALF, WIDTH), BF),
            out((GROUPS, 4 * HALF, WIDTH), BF),
        ],
        scratch_shapes=[pltpu.VMEM((ROWS, WIDTH), F32)],
        compiler_params=params(),
        cost_estimate=cost(14),
        name="post_backward",
    )(section, dy, u, n2, x1, mixed, vec, *slim, *wide, *wide)


def run_pre_backward(section, grads, n1, x, dx1, vec, slim):
    return pl.pallas_call(
        pre_backward,
        grid=(3,),
        in_specs=[
            SMEM_SPEC,
            HEADS_SPEC,
            whole(ROWS, WIDTH),
            whole(ROWS, WIDTH),
            whole(ROWS, WIDTH),
            whole(12, WIDTH),
            WIDE_SPEC,
            WIDE_SPEC,
        ],
        out_specs=[whole(ROWS, WIDTH), whole(12, WIDTH), WIDE_SPEC, WIDE_SPEC],
        out_shape=[
            out((ROWS, WIDTH), BF),
            out((12, WIDTH), F32),
            out((GROUPS, 3 * HALF, WIDTH), BF),
            out((GROUPS, 3 * HALF, WIDTH), BF),
        ],
        scratch_shapes=[pltpu.VMEM((ROWS, WIDTH), F32)],
        compiler_params=params(),
        cost_estimate=cost(8),
        name="pre_backward",
    )(section, grads, n1, x, dx1, vec, *slim)


def exchange(value):
    return lax.all_to_all(value, "group", 0, 0, tiled=True)


def body(
    tokens,
    cotangent,
    lengths,
    ln1_gain,
    ln1_bias,
    w_qkv,
    b_query,
    b_value,
    w_out,
    b_out,
    ln2_gain,
    ln2_bias,
    w_fc,
    b_fc,
    w_proj,
    b_proj,
):
    section = lax.axis_index("section")
    which = section.astype(jnp.int32).reshape(1)
    length_row = lax.dynamic_index_in_dim(lengths, section, 0, keepdims=False)
    tokens_row = lax.dynamic_index_in_dim(tokens, section, 0, keepdims=False)

    vectors = (ln1_gain, ln1_bias, b_query, b_value, b_out, ln2_gain, ln2_bias, b_proj)
    keep, away = run_pack_shard(which, w_qkv, w_out, w_fc, w_proj, b_fc, *vectors)
    got = swap(away)
    shard_zero, shard_one = pick(keep, got), pick(got, keep)
    front = SLIM + VEC_ROWS
    slim_zero = Gather(jnp.concatenate([shard_zero[:front], shard_one[SLIM:front]], axis=0))
    wide_zero = Gather(shard_zero[front:])
    slim_one = Gather(shard_one[:SLIM])
    wide_one = Gather(shard_one[front:])

    slim_zero.near()
    wide_zero.shard = slim_zero.after(wide_zero.shard)
    slim_zero.far()
    wide_zero.shard = slim_zero.after(wide_zero.shard)
    slim_zero.last()
    wide_zero.near()
    mine = slim_zero.whole()
    slim = mine, swap(mine)
    vecs = run_unpack_vectors(mine)

    n1, send = run_pre_forward(which, tokens_row, vecs[0], slim)
    send = wide_zero.after(send)
    wide_zero.far()
    heads = exchange(send)
    heads = wide_zero.after(heads)
    slim_one.shard, heads = tie(slim_one.shard, heads)
    wide_zero.last()
    slim_one.near()
    mixed, logsum = run_attend_forward(length_row, heads)
    mixed = wide_zero.after(mixed)
    mine = wide_zero.whole()
    wide = mine, swap(mine)
    mixed = exchange(mixed)
    mixed = slim_one.after(mixed)
    wide_one.shard, mixed = tie(wide_one.shard, mixed)
    slim_one.far()
    result, x1, n2, u = run_post_forward(which, mixed, tokens_row, vecs[0], slim, wide)
    kept_zero = (tokens_row, n1, heads, logsum, mixed, x1, n2, u, slim, wide)

    result = slim_one.after(result)
    wide_one.shard, result = tie(wide_one.shard, result)
    output_zero = result
    slim_one.last()
    wide_one.near()
    mine = slim_one.whole()
    slim = mine, swap(mine)
    n1, send = run_pre_forward(which, result, vecs[1], slim)
    send = wide_one.after(send)
    wide_one.far()
    heads = exchange(send)
    heads = wide_one.after(heads)
    wide_one.last()
    mixed, logsum = run_attend_forward(length_row, heads)
    mixed = wide_one.after(mixed)
    mine = wide_one.whole()
    wide = mine, swap(mine)
    mixed = exchange(mixed)
    output_one, x1, n2, u = run_post_forward(which, mixed, result, vecs[1], slim, wide)
    kept_one = (result, n1, heads, logsum, mixed, x1, n2, u, slim, wide)

    def first_part(layer, grad, kept):
        _, _, _, _, mixed, x1, n2, u, slim, wide = kept
        dx1, send, dvec, *halves = run_post_backward(
            which, grad, u, n2, x1, mixed, vecs[layer], slim, wide
        )
        pairs = [(keep, swap(away)) for keep, away in zip(halves[::2], halves[1::2])]
        return dx1, send, dvec, pairs

    def second_part(layer, dheads, dx1, kept):
        rows, n1, _, _, _, _, _, _, slim, _ = kept
        grad, dvec, keep, away = run_pre_backward(which, dheads, n1, rows, dx1, vecs[layer], slim)
        return grad, dvec, (keep, swap(away))

    grad = lax.dynamic_index_in_dim(cotangent, section, 0, keepdims=False)
    dx1, send, dvec_two, pairs = first_part(1, grad, kept_one)
    bulk_one = GroupSum(pairs)
    dheads = run_attend_backward(length_row, kept_one[2], exchange(send), kept_one[3])
    dheads = exchange(dheads)
    bulk_one.low, bulk_one.high, dheads = tie(bulk_one.low, bulk_one.high, dheads)
    bulk_one.far()
    grad_one, dvec_one, slim_pair = second_part(1, dheads, dx1, kept_one)
    dvec_last = dvec_one + dvec_two

    dx1, send, dvec_two, pairs = first_part(0, grad_one, kept_zero)
    bulk_one.from_left, bulk_one.from_right, send = tie(
        bulk_one.from_left, bulk_one.from_right, send
    )
    bulk = GroupSum([*pairs, slim_pair])
    grad_heads = exchange(send)
    bulk_one.from_left, bulk_one.from_right, grad_heads = tie(
        bulk_one.from_left, bulk_one.from_right, grad_heads
    )
    bulk_one.near()
    dheads = run_attend_backward(length_row, kept_zero[2], grad_heads, kept_zero[3])
    dheads = exchange(dheads)
    bulk.low, bulk.high, bulk_one.one, bulk_one.minus, dheads = tie(
        bulk.low, bulk.high, bulk_one.one, bulk_one.minus, dheads
    )
    bulk.far()
    grad_zero, dvec_one, slim_pair = second_part(0, dheads, dx1, kept_zero)
    dvecs = jnp.stack([dvec_one + dvec_two, dvec_last])
    dvecs = dvecs + swap(dvecs)
    slim_sum = add(*slim_pair).astype(BF)
    last = jnp.concatenate([slim_sum, run_pack_vectors(dvecs)], axis=1)
    last, bulk.from_left, bulk.from_right = tie(last, bulk.from_left, bulk.from_right)
    bulk.near()
    last = over_all(last)
    split = HALF + WIDE
    both = jnp.concatenate([bulk.total(), bulk_one.total()], axis=0)
    both = over_replica(both)
    bulk, sum_one = both[: split + 3 * HALF], both[split + 3 * HALF :]

    def own_layer(zero, one):
        mine, other = pick(zero, one), swap(pick(one, zero))
        return pick(mine, other).astype(F32), pick(other, mine).astype(F32)

    first, second = own_layer(bulk[:split], sum_one)
    first_slim, second_slim = own_layer(last[: 3 * HALF], bulk[split:])

    def block(low, high, j):
        at = slice(HALF * j, HALF * j + HALF)
        return jnp.concatenate([low[at], high[at]], axis=0)

    grad_qkv = jnp.concatenate([block(first_slim, second_slim, j) for j in range(3)], axis=1)
    grad_out = block(first, second, 0)
    grad_fc = jnp.concatenate([block(first, second, 1 + j) for j in range(4)], axis=1)
    grad_proj = jnp.concatenate([first[5 * HALF :], second[5 * HALF :]], axis=0)
    v = last[3 * HALF :].astype(F32)
    v = pick(v[:VEC_ROWS], v[VEC_ROWS:])

    def both_micro(zero, one):
        mine, other = pick(zero, one), swap(pick(one, zero))
        return jnp.stack([pick(mine, other), pick(other, mine)])[None]

    acts = both_micro(output_zero, output_one)
    in_grads = both_micro(grad_zero, grad_one)
    return (
        acts,
        in_grads,
        v[0:1, :SHARD],
        v[1:2, :SHARD],
        grad_qkv[None],
        v[2:3, :SHARD],
        v[3:4, :SHARD],
        grad_out[None],
        v[4:5, :SHARD],
        v[5:6, :SHARD],
        v[6:7, :SHARD],
        grad_fc[None],
        v[8:9, : 4 * SHARD],
        grad_proj[None],
        v[7:8, :SHARD],
    )


def solution(mesh):
    placed = (
        P("replica", "group", None),
        P("replica", "group", None),
        P("replica", None),
        P("section", "group"),
        P("section", "group"),
        P("section", "group", None),
        P("section", "group"),
        P("section", "group"),
        P("section", "group", None),
        P("section", "group"),
        P("section", "group"),
        P("section", "group"),
        P("section", "group", None),
        P("section", "group"),
        P("section", "group", None),
        P("section", "group"),
    )
    return jax.shard_map(
        body,
        mesh=mesh,
        in_specs=placed,
        out_specs=(
            P("section", "replica", "group", None),
            P("section", "replica", "group", None),
            P("section", "group"),
            P("section", "group"),
            P("section", "group", None),
            P("section", "group"),
            P("section", "group"),
            P("section", "group", None),
            P("section", "group"),
            P("section", "group"),
            P("section", "group"),
            P("section", "group", None),
            P("section", "group"),
            P("section", "group", None),
            P("section", "group"),
        ),
        check_vma=False,
    )
```

time: 716 us -> 598 us (0.84)
  the two profiles are of different devices: /device:TPU:121 before, /device:TPU:1 now
where the time goes in v2:
time: 598 us; the launch traced here: 586 us
  starting transfers between devices  150 us (25%)
  waiting for transfers between devices  146 us (24%)
  Pallas kernels  106 us (18%)
  local copies, waits for them, and re-layouts  92.5 us (15%)
  blocking collectives  68.7 us (11%)
  other arithmetic  20.6 us (3%)
    all_to_all x2, blocking collectives, exchange(): return lax.all_to_all(value, 'group', 0, 0, tiled=True)  68.7 us
    ppermute x24, waiting for transfers between devices, along_x(): lax.ppermute(value, ('group', 'replica'), torus_pairs(lambda x, y, z: (x...  66 us
    unnamed x264, local copies, waits for them, and re-layouts  60.1 us
    ppermute x29, starting transfers between devices, along_z(): lax.ppermute(value, ('group', 'replica'), torus_pairs(lambda x, y, z: (x,...  43.6 us
    ppermute x29, waiting for transfers between devices, along_z(): lax.ppermute(value, ('group', 'replica'), torus_pairs(lambda x, y, z: (x,...  32.1 us
    ppermute x24, starting transfers between devices, along_x(): lax.ppermute(value, ('group', 'replica'), torus_pairs(lambda x, y, z: (x...  30.8 us
    ppermute x18, starting transfers between devices, swap(): return lax.ppermute(value, 'section', [(0, 1), (1, 0)])  30.1 us
    ppermute x8, waiting for transfers between devices, along_y(): lax.ppermute(value, ('group', 'replica'), torus_pairs(lambda x, y, z: (x,...  28 us
  transfers between devices with their start and end apart: 87, of which 31 were waited for; matrix products, arithmetic and copies ran while one was open for 7% of the time, Pallas kernels for 10%

profile of v2, /device:TPU:1, one launch (start us, length us, event | category | flops | bytes accessed | tf_op | source)
XLA Modules:
  0.0 585.8 jit_solution(7462660483613718159)
XLA Ops:
  18.3 3.9 collective-permute-start.4
  25.0 3.1 collective-permute-done.3.refs_5_
  28.1 2.7 collective-permute-start.8
  30.9 2.6 collective-permute-start.6
  33.5 3.1 collective-permute-done.5.refs_3_
  39.4 2.8 collective-permute-done.13.refs_9_
  42.4 4.8 collective-permute-start.15
  48.8 2.9 collective-permute-start.10
  53.6 3.0 collective-permute-start.12
  62.6 3.9 pre_forward.2
  67.6 3.6 all-to-all-start
  80.6 8.9 %collective-permute-done.16.refs_3_ = bf16[192,768]{1,0:T(8,128)(2,1)S(1)} collective-permute-done((bf16[192,768]{1,0:T(8,128)(2,1)S(1)}, bf16[192,768]{1,0:T(8,128)(2,1)S(1)}, u32[]{:S(2)}, u32[]{:S(2)}) %collective-permute-start.16) | collective-permute-done | bytes 294944 | tf_op jit(solution)/shard_map/ppermute | solution.py:40
  89.5 2.6 collective-permute-done.18.refs_7_
  94.4 3.1 collective-permute-start.25
  97.5 4.9 attend_forward.2
  104.0 3.9 assemble.5.fc_mine.proj_mine
  107.9 2.3 collective-permute-start.30
  112.8 4.1 all-to-all-start.1
  129.7 2.2 collective-permute-start.29
  131.9 2.7 collective-permute-start.27
  136.4 6.5 %post_forward.2 = (bf16[128,768]{1,0:T(8,128)(2,1)S(1)}, f32[128,768]{1,0:T(8,128)S(1)}, bf16[128,768]{1,0:T(8,128)(2,1)S(1)}, f32[4,128,768]{2,1,0:T(8,128)S(1)}) custom-call(s32[1]{0:T(128)} %bitcast.section_ref, bf16[8,128,128]{2,1,0:T(8,128)(2,1)} %all-to-all-done.1.mixed_ref, bf16[128,768]{1,0:T(8,128)(2,1)S(1)} %copy-done.34, ...), custom_call_target="tpu_custom_call" | custom-call | flops 3200000000 | bytes 24000000 | tf_op jit(solution)/shard_map/post_forward/pallas_call | solution.py:773
  144.4 2.7 collective-permute-start.36
  147.1 2.5 collective-permute-done.35.refs_9_
  151.0 3.1 collective-permute-start.37
  154.0 2.7 collective-permute-start.32
  156.8 3.2 collective-permute-start.34
  163.3 3.3 collective-permute-done.33.refs_5_
  171.7 4.2 all-to-all-start.2
  183.7 10.5 %collective-permute-done.38.refs_3_ = bf16[192,768]{1,0:T(8,128)(2,1)S(1)} collective-permute-done((bf16[192,768]{1,0:T(8,128)(2,1)S(1)}, bf16[192,768]{1,0:T(8,128)(2,1)S(1)}, u32[]{:S(2)}, u32[]{:S(2)}) %collective-permute-start.38) | collective-permute-done | bytes 294944 | tf_op jit(solution)/shard_map/ppermute | solution.py:40
  194.2 2.7 collective-permute-done.40.refs_7_
  202.8 5.5 attend_forward.3
  211.8 2.4 assemble.7.fc_mine.proj_mine
  216.2 4.2 all-to-all-start.3
  221.1 5.9 %all-to-all-done.3.mixed_ref = bf16[8,128,128]{2,1,0:T(8,128)(2,1)S(1)} async-done(((bf16[8,128,128]{2,1,0:T(8,128)(2,1)}), bf16[8,128,128]{2,1,0:T(8,128)(2,1)S(1)}, u32[]{:S(2)}, u32[]{:S(2)}) %all-to-all-start.3) | async-done | bytes 262176 | tf_op jit(solution)/shard_map/all_to_all | solution.py:884
  229.7 6.2 %post_forward.3 = (bf16[128,768]{1,0:T(8,128)(2,1)S(1)}, f32[128,768]{1,0:T(8,128)S(1)}, bf16[128,768]{1,0:T(8,128)(2,1)S(1)}, f32[4,128,768]{2,1,0:T(8,128)S(1)}) custom-call(s32[1]{0:T(128)} %bitcast.section_ref, bf16[8,128,128]{2,1,0:T(8,128)(2,1)S(1)} %all-to-all-done.3.mixed_ref, bf16[128,768]{1,0:T(8,128)(2,1)S(1)} %copy-done.19, ...), custom_call_target="tpu_custom_call" | custom-call | flops 3200000000 | bytes 24000000 | tf_op jit(solution)/shard_map/post_forward/pallas_call | solution.py:773
  236.5 11.3 %post_backward.2 = (f32[128,768]{1,0:T(8,128)S(1)}, bf16[8,128,128]{2,1,0:T(8,128)(2,1)S(1)}, f32[12,768]{1,0:T(8,128)S(1)}, bf16[8,48,768]{2,1,0:T(8,128)(2,1)S...) custom-call(s32[1]{0:T(128)} %bitcast.section_ref, ...), custom_call_target="tpu_custom_call" | custom-call | flops 5600000000 | bytes 42000000 | tf_op jit(solution)/shard_map/post_backward/pallas_call | solution.py:808
  253.9 3.4 all-to-all-start.4
  265.7 5.5 sum_pairs.2
  271.2 2.8 collective-permute-start.50
  275.1 7.2 %attend_backward.2 = bf16[8,3,128,128]{3,2,1,0:T(8,128)(2,1)S(1)} custom-call(s32[3]{0:T(128)S(1)} %fusion.6.length_ref, bf16[8,3,128,128]{3,2,1,0:T(8,128)(2,1)} %all-to-all-done.2.qkv_ref, bf16[8,128,128]{2,1,0:T(8,128)(2,1)S(1)} %all-to-all-done.4.grad_ref, f32[1024,128]{1,0:T(8,128)S(1)} %copy-done.126), custom_call_target="tpu_custom_call" | custom-call | flops 6400000000 | bytes 48000000 | tf_op jit(solution)/shard_map/attend_backward/pallas_call | solution.py:754
  282.3 29.0 %all_to_all.50.grads_ref = bf16[8,3,128,128]{3,2,1,0:T(8,128)(2,1)S(1)} all-to-all(bf16[8,3,128,128]{3,2,1,0:T(8,128)(2,1)S(1)} %attend_backward.2), channel_id=1, replica_groups=mesh['section'=2,'group'=8,'replica'=8] {'group'}, dimensions={0} | all-to-all | bytes 1572864 | tf_op jit(solution)/shard_map/all_to_all | solution.py:884
  312.4 3.5 pre_backward.2
  316.6 10.9 %post_backward.3 = (f32[128,768]{1,0:T(8,128)S(1)}, bf16[8,128,128]{2,1,0:T(8,128)(2,1)S(1)}, f32[12,768]{1,0:T(8,128)S(1)}, bf16[8,48,768]{2,1,0:T(8,128)(2,1)S...) custom-call(s32[1]{0:T(128)} %bitcast.section_ref, ...), custom_call_target="tpu_custom_call" | custom-call | flops 5600000000 | bytes 42000000 | tf_op jit(solution)/shard_map/post_backward/pallas_call | solution.py:808
  335.9 6.4 %collective-permute-done.51.refs_1_ = bf16[8,48,768]{2,1,0:T(8,128)(2,1)S(1)} collective-permute-done((bf16[8,48,768]{2,1,0:T(8,128)(2,1)S(1)}, bf16[8,48,768]{2,1,0:T(8,128)(2,1)S(1)}, u32[]{:S(2)}, u32[]{:S(2)}) %collective-permute-start.51) | collective-permute-done | bytes 589856 | tf_op jit(solution)/shard_map/ppermute | solution.py:52
  342.4 6.3 %sum_pairs.3 = (bf16[4,576,768]{2,1,0:T(8,128)(2,1)}, bf16[4,288,768]{2,1,0:T(8,128)(2,1)}, bf16[4,288,768]{2,1,0:T(8,128)(2,1)}) custom-call(bf16[8,48,768]{2,1,0:T(8,128)(2,1)S(1)} %get-tuple-element.312.refs_0_, bf16[8,48,768]{2,1,0:T(8,128)(2,1)S(1)} %collective-permute-done.51.refs_1_, bf16[8,192,768]{2,1,0:T(8,128)(2,1)S(1)} %get-tuple-element.314.refs_2_, ...), custom_call_target="tpu_custom_call" | custom-call | flops 2000000000 | bytes 15000000 | tf_op jit(solution)/shard_map/sum_pairs/pallas_call | solution.py:650
  353.0 39.7 %all_to_all.51.grad_ref = bf16[8,128,128]{2,1,0:T(8,128)(2,1)S(1)} all-to-all(bf16[8,128,128]{2,1,0:T(8,128)(2,1)S(1)} %get-tuple-element.332), channel_id=1, replica_groups=mesh['section'=2,'group'=8,'replica'=8] {'group'}, dimensions={0} | all-to-all | bytes 524288 | tf_op jit(solution)/shard_map/all_to_all | solution.py:884
  392.8 7.3 %attend_backward.3 = bf16[8,3,128,128]{3,2,1,0:T(8,128)(2,1)} custom-call(s32[3]{0:T(128)S(1)} %fusion.6.length_ref, bf16[8,3,128,128]{3,2,1,0:T(8,128)(2,1)S(1)} %copy-done.37, bf16[8,128,128]{2,1,0:T(8,128)(2,1)S(1)} %all_to_all.51.grad_ref, f32[1024,128]{1,0:T(8,128)S(1)} %copy-done.124), custom_call_target="tpu_custom_call" | custom-call | flops 6400000000 | bytes 48000000 | tf_op jit(solution)/shard_map/attend_backward/pallas_call | solution.py:754
  400.1 4.4 all-to-all-start.7
  410.6 19.4 %collective-permute-done.59 = bf16[432,768]{1,0:T(8,128)(2,1)S(1)} collective-permute-done((bf16[432,768]{1,0:T(8,128)(2,1)S(1)}, bf16[432,768]{1,0:T(8,128)(2,1)S(1)}, u32[]{:S(2)}, u32[]{:S(2)}) %collective-permute-start.59) | collective-permute-done | bytes 663584 | tf_op jit(solution)/shard_map/ppermute | solution.py:40
  434.5 5.7 pre_backward.3
  443.2 3.4 sum_z.3
  448.4 2.7 collective-permute-start.65
  457.4 3.7 collective-permute-done.64.left_ref
  463.2 2.7 collective-permute-start.67
  467.4 17.1 %collective-permute-done.66 = bf16[576,768]{1,0:T(8,128)(2,1)} collective-permute-done((bf16[576,768]{1,0:T(8,128)(2,1)}, bf16[576,768]{1,0:T(8,128)(2,1)}, u32[]{:S(2)}, u32[]{:S(2)}) %collective-permute-start.66) | collective-permute-done | bytes 884768 | tf_op jit(solution)/shard_map/ppermute | solution.py:40
  487.6 2.6 convert_element_type.107
  497.1 7.4 %all-to-all-start.8 = ((bf16[64,22,768]{2,1,0:T(8,128)(2,1)}), bf16[64,22,768]{2,1,0:T(8,128)(2,1)S(1)}, u32[]{:S(2)}, u32[]{:S(2)}) async-start(bf16[64,22,768]{2,1,0:T(8,128)(2,1)} %reshape.59), calls=%async_computation.8 | async-start | bytes 4718592 | tf_op jit(solution)/shard_map/all_to_all | solution.py:181
  509.6 4.0 collective-permute-start.45
  513.6 27.3 %collective-permute-done.69 = bf16[252,768]{1,0:T(8,128)(2,1)} collective-permute-done((bf16[252,768]{1,0:T(8,128)(2,1)S(1)}, bf16[252,768]{1,0:T(8,128)(2,1)}, u32[]{:S(2)}, u32[]{:S(2)}) %collective-permute-start.69) | collective-permute-done | bytes 387104 | tf_op jit(solution)/shard_map/ppermute | solution.py:44
  542.2 2.3 collective-permute-start.72
  546.7 6.2 %collective-permute-done.72 = bf16[252,768]{1,0:T(8,128)(2,1)S(1)} collective-permute-done((bf16[252,768]{1,0:T(8,128)(2,1)S(1)}, bf16[252,768]{1,0:T(8,128)(2,1)S(1)}, u32[]{:S(2)}, u32[]{:S(2)}) %collective-permute-start.72) | collective-permute-done | bytes 387104 | tf_op jit(solution)/shard_map/ppermute | solution.py:48
  555.1 2.7 collective-permute-start.74
  560.5 3.4 all-to-all-start.9
  575.3 4.7 collective-permute-start.77
  (474 shorter events, 194.4 us)
Async XLA Ops:
  15.5 12.6 %collective-permute-start.1 = (bf16[224,768]{1,0:T(8,128)(2,1)S(1)}, bf16[224,768]{1,0:T(8,128)(2,1)S(1)}, u32[]{:S(2)}, u32[]{:S(2)}) collective-permute-start(bf16[224,768]{1,0:T(8,128)(2,1)S(1)} %pad_maximum_fusion.2.refs_0_), channel_id=1, source_target_pairs={{0,16},{1,17},{2,18},{3,19},{4,20},{5,21},{6,22},{7,23},{8,24},{9,... | collective-permute-start | bytes 1032200 | tf_op jit(solution)/shard_map/ppermute | solution.py:40
  16.9 11.2 %collective-permute-start.2 = (bf16[224,768]{1,0:T(8,128)(2,1)S(1)}, bf16[224,768]{1,0:T(8,128)(2,1)S(1)}, u32[]{:S(2)}, u32[]{:S(2)}) collective-permute-start(bf16[224,768]{1,0:T(8,128)(2,1)S(1)} %pad_maximum_fusion.2.refs_0_), channel_id=1, source_target_pairs={{0,48},{1,49},{2,50},{3,51},{4,52},{5,53},{6,54},{7,55},{8,56},{9,... | collective-permute-start | bytes 1032200 | tf_op jit(solution)/shard_map/ppermute | solution.py:40
  42.4 17.5 %collective-permute-start.15 = (bf16[8,224,768]{2,1,0:T(8,128)(2,1)S(1)}, bf16[8,224,768]{2,1,0:T(8,128)(2,1)}, u32[]{:S(2)}, u32[]{:S(2)}) collective-permute-start(bf16[8,224,768]{2,1,0:T(8,128)(2,1)S(1)} %assemble.4.mine_ref.out_mine), channel_id=1, source_target_pairs={{0,64},{64,0},{1,65},{65,1},{2,66},{66,2},{3,67},{67,3},{4,68},{68... | collective-permute-start | bytes 8257544 | tf_op jit(solution)/shard_map/ppermute | solution.py:52
  48.8 18.4 %collective-permute-start.10 = (bf16[384,768]{1,0:T(8,128)(2,1)}, bf16[384,768]{1,0:T(8,128)(2,1)}, u32[]{:S(2)}, u32[]{:S(2)}) collective-permute-start(bf16[384,768]{1,0:T(8,128)(2,1)} %slice.295.refs_0_), channel_id=1, source_target_pairs={{0,48},{1,49},{2,50},{3,51},{4,52},{5,53},{6,54},{7,55},{8,56},{9,... | collective-permute-start | bytes 1769480 | tf_op jit(solution)/shard_map/ppermute | solution.py:40
  51.7 15.9 %collective-permute-start.9 = (bf16[384,768]{1,0:T(8,128)(2,1)}, bf16[384,768]{1,0:T(8,128)(2,1)}, u32[]{:S(2)}, u32[]{:S(2)}) collective-permute-start(bf16[384,768]{1,0:T(8,128)(2,1)} %slice.295.refs_0_), channel_id=1, source_target_pairs={{0,16},{1,17},{2,18},{3,19},{4,20},{5,21},{6,22},{7,23},{8,24},{9,... | collective-permute-start | bytes 1769480 | tf_op jit(solution)/shard_map/ppermute | solution.py:40
  53.6 13.6 %collective-permute-start.11 = (bf16[192,768]{1,0:T(8,128)(2,1)}, bf16[192,768]{1,0:T(8,128)(2,1)}, u32[]{:S(2)}, u32[]{:S(2)}) collective-permute-start(bf16[192,768]{1,0:T(8,128)(2,1)} %get-tuple-element.396), channel_id=1, source_target_pairs={{0,8},{1,9},{2,10},{3,11},{4,12},{5,13},{6,14},{7,15},{8,4},{9,5},... | collective-permute-start | bytes 884744 | tf_op jit(solution)/shard_map/ppermute | solution.py:48
  53.6 13.6 %collective-permute-start.12 = (bf16[192,768]{1,0:T(8,128)(2,1)}, bf16[192,768]{1,0:T(8,128)(2,1)}, u32[]{:S(2)}, u32[]{:S(2)}) collective-permute-start(bf16[192,768]{1,0:T(8,128)(2,1)} %get-tuple-element.395), channel_id=1, source_target_pairs={{0,12},{1,13},{2,14},{3,15},{4,8},{5,9},{6,10},{7,11},{8,0},{9,1},... | collective-permute-start | bytes 884744 | tf_op jit(solution)/shard_map/ppermute | solution.py:48
  67.6 26.7 %all-to-all-start = ((bf16[8,3,128,128]{3,2,1,0:T(8,128)(2,1)}), bf16[8,3,128,128]{3,2,1,0:T(8,128)(2,1)S(1)}, u32[]{:S(2)}, u32[]{:S(2)}) async-start(bf16[8,3,128,128]{3,2,1,0:T(8,128)(2,1)} %get-tuple-element.214), calls=%async_computation | async-start | bytes 1572864 | tf_op jit(solution)/shard_map/all_to_all | solution.py:884
  71.2 21.0 %collective-permute-start.18 = (bf16[384,768]{1,0:T(8,128)(2,1)}, bf16[384,768]{1,0:T(8,128)(2,1)S(1)}, u32[]{:S(2)}, u32[]{:S(2)}) collective-permute-start(bf16[384,768]{1,0:T(8,128)(2,1)} %collective-permute-done.9.refs_1_), channel_id=1, source_target_pairs={{0,8},{1,9},{2,10},{3,11},{4,12},{5,13},{6,14},{7,15},{8,4},{9,5},... | collective-permute-start | bytes 1769480 | tf_op jit(solution)/shard_map/ppermute | solution.py:48
  72.7 21.6 %collective-permute-start.19 = (bf16[384,768]{1,0:T(8,128)(2,1)}, bf16[384,768]{1,0:T(8,128)(2,1)S(1)}, u32[]{:S(2)}, u32[]{:S(2)}) collective-permute-start(bf16[384,768]{1,0:T(8,128)(2,1)} %collective-permute-done.10.refs_2_), channel_id=1, source_target_pairs={{0,12},{1,13},{2,14},{3,15},{4,8},{5,9},{6,10},{7,11},{8,0},{9,1},... | collective-permute-start | bytes 1769480 | tf_op jit(solution)/shard_map/ppermute | solution.py:48
  76.2 13.4 %collective-permute-start.16 = (bf16[192,768]{1,0:T(8,128)(2,1)S(1)}, bf16[192,768]{1,0:T(8,128)(2,1)S(1)}, u32[]{:S(2)}, u32[]{:S(2)}) collective-permute-start(bf16[192,768]{1,0:T(8,128)(2,1)S(1)} %slice.231), channel_id=1, source_target_pairs={{0,16},{1,17},{2,18},{3,19},{4,20},{5,21},{6,22},{7,23},{8,24},{9,... | collective-permute-start | bytes 884744 | tf_op jit(solution)/shard_map/ppermute | solution.py:40
  77.4 12.1 %collective-permute-start.17 = (bf16[192,768]{1,0:T(8,128)(2,1)S(1)}, bf16[192,768]{1,0:T(8,128)(2,1)S(1)}, u32[]{:S(2)}, u32[]{:S(2)}) collective-permute-start(bf16[192,768]{1,0:T(8,128)(2,1)S(1)} %slice.232), channel_id=1, source_target_pairs={{0,48},{1,49},{2,50},{3,51},{4,52},{5,53},{6,54},{7,55},{8,56},{9,... | collective-permute-start | bytes 884744 | tf_op jit(solution)/shard_map/ppermute | solution.py:40
  94.3 9.6 %collective-permute-start.24 = (bf16[192,768]{1,0:T(8,128)(2,1)}, bf16[192,768]{1,0:T(8,128)(2,1)S(1)}, u32[]{:S(2)}, u32[]{:S(2)}) collective-permute-start(bf16[192,768]{1,0:T(8,128)(2,1)} %copy-done.64), channel_id=1, source_target_pairs={{0,8},{1,9},{2,10},{3,11},{4,12},{5,13},{6,14},{7,15},{8,4},{9,5},... | collective-permute-start | bytes 884744 | tf_op jit(solution)/shard_map/ppermute | solution.py:48
  94.4 9.6 %collective-permute-start.25 = (bf16[192,768]{1,0:T(8,128)(2,1)}, bf16[192,768]{1,0:T(8,128)(2,1)S(1)}, u32[]{:S(2)}, u32[]{:S(2)}) collective-permute-start(bf16[192,768]{1,0:T(8,128)(2,1)} %copy-done.68), channel_id=1, source_target_pairs={{0,12},{1,13},{2,14},{3,15},{4,8},{5,9},{6,10},{7,11},{8,0},{9,1},... | collective-permute-start | bytes 884744 | tf_op jit(solution)/shard_map/ppermute | solution.py:48
  107.9 26.7 %collective-permute-start.30 = (bf16[8,384,768]{2,1,0:T(8,128)(2,1)}, bf16[8,384,768]{2,1,0:T(8,128)(2,1)}, u32[]{:S(2)}, u32[]{:S(2)}) collective-permute-start(bf16[8,384,768]{2,1,0:T(8,128)(2,1)} %assemble.5.fc_mine.proj_mine), channel_id=1, source_target_pairs={{0,64},{64,0},{1,65},{65,1},{2,66},{66,2},{3,67},{67,3},{4,68},{68... | collective-permute-start | bytes 14155784 | tf_op jit(solution)/shard_map/ppermute | solution.py:52
  110.2 17.1 %collective-permute-start.20 = (bf16[192,768]{1,0:T(8,128)(2,1)}, bf16[192,768]{1,0:T(8,128)(2,1)}, u32[]{:S(2)}, u32[]{:S(2)}) collective-permute-start(bf16[192,768]{1,0:T(8,128)(2,1)} %slice.289.refs_0_), channel_id=1, source_target_pairs={{0,16},{1,17},{2,18},{3,19},{4,20},{5,21},{6,22},{7,23},{8,24},{9,... | collective-permute-start | bytes 884744 | tf_op jit(solution)/shard_map/ppermute | solution.py:40
  111.3 15.9 %collective-permute-start.21 = (bf16[192,768]{1,0:T(8,128)(2,1)}, bf16[192,768]{1,0:T(8,128)(2,1)}, u32[]{:S(2)}, u32[]{:S(2)}) collective-permute-start(bf16[192,768]{1,0:T(8,128)(2,1)} %slice.289.refs_0_), channel_id=1, source_target_pairs={{0,48},{1,49},{2,50},{3,51},{4,52},{5,53},{6,54},{7,55},{8,56},{9,... | collective-permute-start | bytes 884744 | tf_op jit(solution)/shard_map/ppermute | solution.py:40
  112.8 14.4 %all-to-all-start.1 = ((bf16[8,128,128]{2,1,0:T(8,128)(2,1)}), bf16[8,128,128]{2,1,0:T(8,128)(2,1)}, u32[]{:S(2)}, u32[]{:S(2)}) async-start(bf16[8,128,128]{2,1,0:T(8,128)(2,1)} %copy-done.72), calls=%async_computation.1 | async-start | bytes 524288 | tf_op jit(solution)/shard_map/all_to_all | solution.py:884
  128.2 16.1 %collective-permute-start.28 = (bf16[192,768]{1,0:T(8,128)(2,1)}, bf16[192,768]{1,0:T(8,128)(2,1)S(1)}, u32[]{:S(2)}, u32[]{:S(2)}) collective-permute-start(bf16[192,768]{1,0:T(8,128)(2,1)} %collective-permute-done.20.refs_1_), channel_id=1, source_target_pairs={{0,8},{1,9},{2,10},{3,11},{4,12},{5,13},{6,14},{7,15},{8,4},{9,5},... | collective-permute-start | bytes 884744 | tf_op jit(solution)/shard_map/ppermute | solution.py:48
  129.7 14.6 %collective-permute-start.29 = (bf16[192,768]{1,0:T(8,128)(2,1)}, bf16[192,768]{1,0:T(8,128)(2,1)S(1)}, u32[]{:S(2)}, u32[]{:S(2)}) collective-permute-start(bf16[192,768]{1,0:T(8,128)(2,1)} %collective-permute-done.21.refs_2_), channel_id=1, source_target_pairs={{0,12},{1,13},{2,14},{3,15},{4,8},{5,9},{6,10},{7,11},{8,0},{9,1},... | collective-permute-start | bytes 884744 | tf_op jit(solution)/shard_map/ppermute | solution.py:48
  131.9 12.3 %collective-permute-start.26 = (bf16[96,768]{1,0:T(8,128)(2,1)S(1)}, bf16[96,768]{1,0:T(8,128)(2,1)S(1)}, u32[]{:S(2)}, u32[]{:S(2)}) collective-permute-start(bf16[96,768]{1,0:T(8,128)(2,1)S(1)} %slice.235), channel_id=1, source_target_pairs={{0,16},{1,17},{2,18},{3,19},{4,20},{5,21},{6,22},{7,23},{8,24},{9,... | collective-permute-start | bytes 442376 | tf_op jit(solution)/shard_map/ppermute | solution.py:40
  131.9 12.3 %collective-permute-start.27 = (bf16[96,768]{1,0:T(8,128)(2,1)S(1)}, bf16[96,768]{1,0:T(8,128)(2,1)S(1)}, u32[]{:S(2)}, u32[]{:S(2)}) collective-permute-start(bf16[96,768]{1,0:T(8,128)(2,1)S(1)} %slice.236), channel_id=1, source_target_pairs={{0,48},{1,49},{2,50},{3,51},{4,52},{5,53},{6,54},{7,55},{8,56},{9,... | collective-permute-start | bytes 442376 | tf_op jit(solution)/shard_map/ppermute | solution.py:40
  154.0 16.1 %collective-permute-start.31 = (bf16[384,768]{1,0:T(8,128)(2,1)S(1)}, bf16[384,768]{1,0:T(8,128)(2,1)S(1)}, u32[]{:S(2)}, u32[]{:S(2)}) collective-permute-start(bf16[384,768]{1,0:T(8,128)(2,1)S(1)} %copy-done.11), channel_id=1, source_target_pairs={{0,16},{1,17},{2,18},{3,19},{4,20},{5,21},{6,22},{7,23},{8,24},{9,... | collective-permute-start | bytes 1769480 | tf_op jit(solution)/shard_map/ppermute | solution.py:40
  154.0 16.1 %collective-permute-start.32 = (bf16[384,768]{1,0:T(8,128)(2,1)S(1)}, bf16[384,768]{1,0:T(8,128)(2,1)S(1)}, u32[]{:S(2)}, u32[]{:S(2)}) collective-permute-start(bf16[384,768]{1,0:T(8,128)(2,1)S(1)} %copy-done.11), channel_id=1, source_target_pairs={{0,48},{1,49},{2,50},{3,51},{4,52},{5,53},{6,54},{7,55},{8,56},{9,... | collective-permute-start | bytes 1769480 | tf_op jit(solution)/shard_map/ppermute | solution.py:40
  156.8 9.8 %collective-permute-start.33 = (bf16[192,768]{1,0:T(8,128)(2,1)S(1)}, bf16[192,768]{1,0:T(8,128)(2,1)S(1)}, u32[]{:S(2)}, u32[]{:S(2)}) collective-permute-start(bf16[192,768]{1,0:T(8,128)(2,1)S(1)} %get-tuple-element.394), channel_id=1, source_target_pairs={{0,8},{1,9},{2,10},{3,11},{4,12},{5,13},{6,14},{7,15},{8,4},{9,5},... | collective-permute-start | bytes 884744 | tf_op jit(solution)/shard_map/ppermute | solution.py:48
  156.8 10.4 %collective-permute-start.34 = (bf16[192,768]{1,0:T(8,128)(2,1)S(1)}, bf16[192,768]{1,0:T(8,128)(2,1)S(1)}, u32[]{:S(2)}, u32[]{:S(2)}) collective-permute-start(bf16[192,768]{1,0:T(8,128)(2,1)S(1)} %get-tuple-element.393), channel_id=1, source_target_pairs={{0,12},{1,13},{2,14},{3,15},{4,8},{5,9},{6,10},{7,11},{8,0},{9,1},... | collective-permute-start | bytes 884744 | tf_op jit(solution)/shard_map/ppermute | solution.py:48
  171.7 28.3 %all-to-all-start.2 = ((bf16[8,3,128,128]{3,2,1,0:T(8,128)(2,1)}), bf16[8,3,128,128]{3,2,1,0:T(8,128)(2,1)}, u32[]{:S(2)}, u32[]{:S(2)}) async-start(bf16[8,3,128,128]{3,2,1,0:T(8,128)(2,1)} %copy-done.38), calls=%async_computation.2 | async-start | bytes 1572864 | tf_op jit(solution)/shard_map/all_to_all | solution.py:884
  176.0 20.9 %collective-permute-start.40 = (bf16[384,768]{1,0:T(8,128)(2,1)}, bf16[384,768]{1,0:T(8,128)(2,1)S(1)}, u32[]{:S(2)}, u32[]{:S(2)}) collective-permute-start(bf16[384,768]{1,0:T(8,128)(2,1)} %copy-done.29), channel_id=1, source_target_pairs={{0,8},{1,9},{2,10},{3,11},{4,12},{5,13},{6,14},{7,15},{8,4},{9,5},... | collective-permute-start | bytes 1769480 | tf_op jit(solution)/shard_map/ppermute | solution.py:48
  177.3 21.9 %collective-permute-start.41 = (bf16[384,768]{1,0:T(8,128)(2,1)}, bf16[384,768]{1,0:T(8,128)(2,1)S(1)}, u32[]{:S(2)}, u32[]{:S(2)}) collective-permute-start(bf16[384,768]{1,0:T(8,128)(2,1)} %copy-done.31), channel_id=1, source_target_pairs={{0,12},{1,13},{2,14},{3,15},{4,8},{5,9},{6,10},{7,11},{8,0},{9,1},... | collective-permute-start | bytes 1769480 | tf_op jit(solution)/shard_map/ppermute | solution.py:48
  181.0 13.2 %collective-permute-start.38 = (bf16[192,768]{1,0:T(8,128)(2,1)S(1)}, bf16[192,768]{1,0:T(8,128)(2,1)S(1)}, u32[]{:S(2)}, u32[]{:S(2)}) collective-permute-start(bf16[192,768]{1,0:T(8,128)(2,1)S(1)} %slice.240), channel_id=1, source_target_pairs={{0,16},{1,17},{2,18},{3,19},{4,20},{5,21},{6,22},{7,23},{8,24},{9,... | collective-permute-start | bytes 884744 | tf_op jit(solution)/shard_map/ppermute | solution.py:40
  182.0 12.2 %collective-permute-start.39 = (bf16[192,768]{1,0:T(8,128)(2,1)S(1)}, bf16[192,768]{1,0:T(8,128)(2,1)S(1)}, u32[]{:S(2)}, u32[]{:S(2)}) collective-permute-start(bf16[192,768]{1,0:T(8,128)(2,1)S(1)} %slice.241), channel_id=1, source_target_pairs={{0,48},{1,49},{2,50},{3,51},{4,52},{5,53},{6,54},{7,55},{8,56},{9,... | collective-permute-start | bytes 884744 | tf_op jit(solution)/shard_map/ppermute | solution.py:40
  200.1 9.8 %collective-permute-start.42 = (bf16[192,768]{1,0:T(8,128)(2,1)}, bf16[192,768]{1,0:T(8,128)(2,1)S(1)}, u32[]{:S(2)}, u32[]{:S(2)}) collective-permute-start(bf16[192,768]{1,0:T(8,128)(2,1)} %copy-done.66), channel_id=1, source_target_pairs={{0,8},{1,9},{2,10},{3,11},{4,12},{5,13},{6,14},{7,15},{8,4},{9,5},... | collective-permute-start | bytes 884744 | tf_op jit(solution)/shard_map/ppermute | solution.py:48
  214.3 12.8 %collective-permute-start.44 = (bf16[8,384,768]{2,1,0:T(8,128)(2,1)}, bf16[8,384,768]{2,1,0:T(8,128)(2,1)}, u32[]{:S(2)}, u32[]{:S(2)}) collective-permute-start(bf16[8,384,768]{2,1,0:T(8,128)(2,1)} %assemble.7.fc_mine.proj_mine), channel_id=1, source_target_pairs={{0,64},{64,0},{1,65},{65,1},{2,66},{66,2},{3,67},{67,3},{4,68},{68... | collective-permute-start | bytes 14155784 | tf_op jit(solution)/shard_map/ppermute | solution.py:52
  216.2 10.9 %all-to-all-start.3 = ((bf16[8,128,128]{2,1,0:T(8,128)(2,1)}), bf16[8,128,128]{2,1,0:T(8,128)(2,1)S(1)}, u32[]{:S(2)}, u32[]{:S(2)}) async-start(bf16[8,128,128]{2,1,0:T(8,128)(2,1)} %copy-done.74), calls=%async_computation.3 | async-start | bytes 524288 | tf_op jit(solution)/shard_map/all_to_all | solution.py:884
  253.9 20.1 %all-to-all-start.4 = ((bf16[8,128,128]{2,1,0:T(8,128)(2,1)}), bf16[8,128,128]{2,1,0:T(8,128)(2,1)S(1)}, u32[]{:S(2)}, u32[]{:S(2)}) async-start(bf16[8,128,128]{2,1,0:T(8,128)(2,1)} %copy-done.73), calls=%async_computation.4 | async-start | bytes 524288 | tf_op jit(solution)/shard_map/all_to_all | solution.py:884
  271.2 40.0 %collective-permute-start.50 = (bf16[4,224,768]{2,1,0:T(8,128)(2,1)}, bf16[4,224,768]{2,1,0:T(8,128)(2,1)S(1)}, u32[]{:S(2)}, u32[]{:S(2)}) collective-permute-start(bf16[4,224,768]{2,1,0:T(8,128)(2,1)} %get-tuple-element.302), channel_id=1, source_target_pairs={{0,12},{1,13},{2,14},{3,15},{4,8},{5,9},{6,10},{7,11},{8,0},{9,1},... | collective-permute-start | bytes 4128776 | tf_op jit(solution)/shard_map/ppermute | solution.py:48
  274.1 37.2 %collective-permute-start.49 = (bf16[4,208,768]{2,1,0:T(8,128)(2,1)}, bf16[4,208,768]{2,1,0:T(8,128)(2,1)}, u32[]{:S(2)}, u32[]{:S(2)}) collective-permute-start(bf16[4,208,768]{2,1,0:T(8,128)(2,1)} %get-tuple-element.301), channel_id=1, source_target_pairs={{0,8},{1,9},{2,10},{3,11},{4,12},{5,13},{6,14},{7,15},{8,4},{9,5},... | collective-permute-start | bytes 3833864 | tf_op jit(solution)/shard_map/ppermute | solution.py:48
  330.2 12.2 %collective-permute-start.52 = (bf16[8,192,768]{2,1,0:T(8,128)(2,1)}, bf16[8,192,768]{2,1,0:T(8,128)(2,1)S(1)}, u32[]{:S(2)}, u32[]{:S(2)}) collective-permute-start(bf16[8,192,768]{2,1,0:T(8,128)(2,1)} %get-tuple-element.315), channel_id=1, source_target_pairs={{0,64},{64,0},{1,65},{65,1},{2,66},{66,2},{3,67},{67,3},{4,68},{68... | collective-permute-start | bytes 7077896 | tf_op jit(solution)/shard_map/ppermute | solution.py:52
  331.4 11.0 %collective-permute-start.53 = (bf16[8,192,768]{2,1,0:T(8,128)(2,1)S(1)}, bf16[8,192,768]{2,1,0:T(8,128)(2,1)}, u32[]{:S(2)}, u32[]{:S(2)}) collective-permute-start(bf16[8,192,768]{2,1,0:T(8,128)(2,1)S(1)} %get-tuple-element.317), channel_id=1, source_target_pairs={{0,64},{64,0},{1,65},{65,1},{2,66},{66,2},{3,67},{67,3},{4,68},{68... | collective-permute-start | bytes 7077896 | tf_op jit(solution)/shard_map/ppermute | solution.py:52
  331.4 11.0 %collective-permute-start.54 = (bf16[8,144,768]{2,1,0:T(8,128)(2,1)S(1)}, bf16[8,144,768]{2,1,0:T(8,128)(2,1)S(1)}, u32[]{:S(2)}, u32[]{:S(2)}) collective-permute-start(bf16[8,144,768]{2,1,0:T(8,128)(2,1)S(1)} %get-tuple-element.319), channel_id=1, source_target_pairs={{0,64},{64,0},{1,65},{65,1},{2,66},{66,2},{3,67},{67,3},{4,68},{68... | collective-permute-start | bytes 5308424 | tf_op jit(solution)/shard_map/ppermute | solution.py:52
  331.9 10.4 %collective-permute-start.51 = (bf16[8,48,768]{2,1,0:T(8,128)(2,1)S(1)}, bf16[8,48,768]{2,1,0:T(8,128)(2,1)S(1)}, u32[]{:S(2)}, u32[]{:S(2)}) collective-permute-start(bf16[8,48,768]{2,1,0:T(8,128)(2,1)S(1)} %get-tuple-element.313), channel_id=1, source_target_pairs={{0,64},{64,0},{1,65},{65,1},{2,66},{66,2},{3,67},{67,3},{4,68},{68... | collective-permute-start | bytes 1769480 | tf_op jit(solution)/shard_map/ppermute | solution.py:52
  335.2 17.8 %collective-permute-start.58 = (bf16[224,768]{1,0:T(8,128)(2,1)S(1)}, bf16[224,768]{1,0:T(8,128)(2,1)S(1)}, u32[]{:S(2)}, u32[]{:S(2)}) collective-permute-start(bf16[224,768]{1,0:T(8,128)(2,1)S(1)} %get-tuple-element.328), channel_id=1, source_target_pairs={{0,48},{1,49},{2,50},{3,51},{4,52},{5,53},{6,54},{7,55},{8,56},{9,... | collective-permute-start | bytes 1032200 | tf_op jit(solution)/shard_map/ppermute | solution.py:40
  342.3 10.0 %collective-permute-start.57 = (bf16[208,768]{1,0:T(8,128)(2,1)S(1)}, bf16[208,768]{1,0:T(8,128)(2,1)S(1)}, u32[]{:S(2)}, u32[]{:S(2)}) collective-permute-start(bf16[208,768]{1,0:T(8,128)(2,1)S(1)} %get-tuple-element.327), channel_id=1, source_target_pairs={{0,16},{1,17},{2,18},{3,19},{4,20},{5,21},{6,22},{7,23},{8,24},{9,... | collective-permute-start | bytes 958472 | tf_op jit(solution)/shard_map/ppermute | solution.py:40
  348.8 81.3 %collective-permute-start.55 = (bf16[4,288,768]{2,1,0:T(8,128)(2,1)}, bf16[4,288,768]{2,1,0:T(8,128)(2,1)}, u32[]{:S(2)}, u32[]{:S(2)}) collective-permute-start(bf16[4,288,768]{2,1,0:T(8,128)(2,1)} %get-tuple-element.320), channel_id=1, source_target_pairs={{0,8},{1,9},{2,10},{3,11},{4,12},{5,13},{6,14},{7,15},{8,4},{9,5},... | collective-permute-start | bytes 5308424 | tf_op jit(solution)/shard_map/ppermute | solution.py:48
  349.8 80.2 %collective-permute-start.56 = (bf16[4,288,768]{2,1,0:T(8,128)(2,1)}, bf16[4,288,768]{2,1,0:T(8,128)(2,1)}, u32[]{:S(2)}, u32[]{:S(2)}) collective-permute-start(bf16[4,288,768]{2,1,0:T(8,128)(2,1)} %get-tuple-element.321), channel_id=1, source_target_pairs={{0,12},{1,13},{2,14},{3,15},{4,8},{5,9},{6,10},{7,11},{8,0},{9,1},... | collective-permute-start | bytes 5308424 | tf_op jit(solution)/shard_map/ppermute | solution.py:48
  400.1 29.9 %all-to-all-start.7 = ((bf16[8,3,128,128]{3,2,1,0:T(8,128)(2,1)}), bf16[8,3,128,128]{3,2,1,0:T(8,128)(2,1)}, u32[]{:S(2)}, u32[]{:S(2)}) async-start(bf16[8,3,128,128]{3,2,1,0:T(8,128)(2,1)} %attend_backward.3), calls=%async_computation.7 | async-start | bytes 1572864 | tf_op jit(solution)/shard_map/all_to_all | solution.py:884
  407.9 22.1 %collective-permute-start.59 = (bf16[432,768]{1,0:T(8,128)(2,1)S(1)}, bf16[432,768]{1,0:T(8,128)(2,1)S(1)}, u32[]{:S(2)}, u32[]{:S(2)}) collective-permute-start(bf16[432,768]{1,0:T(8,128)(2,1)S(1)} %get-tuple-element.335), channel_id=1, source_target_pairs={{0,16},{1,17},{2,18},{3,19},{4,20},{5,21},{6,22},{7,23},{8,24},{9,... | collective-permute-start | bytes 1990664 | tf_op jit(solution)/shard_map/ppermute | solution.py:40
  409.3 20.7 %collective-permute-start.60 = (bf16[432,768]{1,0:T(8,128)(2,1)S(1)}, bf16[432,768]{1,0:T(8,128)(2,1)}, u32[]{:S(2)}, u32[]{:S(2)}) collective-permute-start(bf16[432,768]{1,0:T(8,128)(2,1)S(1)} %get-tuple-element.336), channel_id=1, source_target_pairs={{0,48},{1,49},{2,50},{3,51},{4,52},{5,53},{6,54},{7,55},{8,56},{9,... | collective-permute-start | bytes 1990664 | tf_op jit(solution)/shard_map/ppermute | solution.py:40
  441.4 12.5 %collective-permute-start.62 = (bf16[8,144,768]{2,1,0:T(8,128)(2,1)}, bf16[8,144,768]{2,1,0:T(8,128)(2,1)}, u32[]{:S(2)}, u32[]{:S(2)}) collective-permute-start(bf16[8,144,768]{2,1,0:T(8,128)(2,1)} %get-tuple-element.344), channel_id=1, source_target_pairs={{0,64},{64,0},{1,65},{65,1},{2,66},{66,2},{3,67},{67,3},{4,68},{68... | collective-permute-start | bytes 5308424 | tf_op jit(solution)/shard_map/ppermute | solution.py:52
  448.4 12.7 %collective-permute-start.64 = (bf16[288,768]{1,0:T(8,128)(2,1)}, bf16[288,768]{1,0:T(8,128)(2,1)S(1)}, u32[]{:S(2)}, u32[]{:S(2)}) collective-permute-start(bf16[288,768]{1,0:T(8,128)(2,1)} %get-tuple-element.352), channel_id=1, source_target_pairs={{0,16},{1,17},{2,18},{3,19},{4,20},{5,21},{6,22},{7,23},{8,24},{9,... | collective-permute-start | bytes 1327112 | tf_op jit(solution)/shard_map/ppermute | solution.py:40
  448.4 12.7 %collective-permute-start.65 = (bf16[288,768]{1,0:T(8,128)(2,1)}, bf16[288,768]{1,0:T(8,128)(2,1)}, u32[]{:S(2)}, u32[]{:S(2)}) collective-permute-start(bf16[288,768]{1,0:T(8,128)(2,1)} %get-tuple-element.353), channel_id=1, source_target_pairs={{0,48},{1,49},{2,50},{3,51},{4,52},{5,53},{6,54},{7,55},{8,56},{9,... | collective-permute-start | bytes 1327112 | tf_op jit(solution)/shard_map/ppermute | solution.py:40
  463.2 21.3 %collective-permute-start.66 = (bf16[576,768]{1,0:T(8,128)(2,1)}, bf16[576,768]{1,0:T(8,128)(2,1)}, u32[]{:S(2)}, u32[]{:S(2)}) collective-permute-start(bf16[576,768]{1,0:T(8,128)(2,1)} %get-tuple-element.360), channel_id=1, source_target_pairs={{0,16},{1,17},{2,18},{3,19},{4,20},{5,21},{6,22},{7,23},{8,24},{9,... | collective-permute-start | bytes 2654216 | tf_op jit(solution)/shard_map/ppermute | solution.py:40
  463.2 21.3 %collective-permute-start.67 = (bf16[576,768]{1,0:T(8,128)(2,1)S(1)}, bf16[576,768]{1,0:T(8,128)(2,1)}, u32[]{:S(2)}, u32[]{:S(2)}) collective-permute-start(bf16[576,768]{1,0:T(8,128)(2,1)S(1)} %get-tuple-element.361), channel_id=1, source_target_pairs={{0,48},{1,49},{2,50},{3,51},{4,52},{5,53},{6,54},{7,55},{8,56},{9,... | collective-permute-start | bytes 2654216 | tf_op jit(solution)/shard_map/ppermute | solution.py:40
  492.2 12.4 %collective-permute-start.68 = (bf16[126,768]{1,0:T(8,128)(2,1)}, bf16[126,768]{1,0:T(8,128)(2,1)S(1)}, u32[]{:S(2)}, u32[]{:S(2)}) collective-permute-start(bf16[126,768]{1,0:T(8,128)(2,1)} %get-tuple-element.375), channel_id=1, source_target_pairs={{0,1},{1,2},{2,3},{3,0},{4,5},{5,6},{6,7},{7,4},{8,9},{9,10},{10,1... | collective-permute-start | bytes 580616 | tf_op jit(solution)/shard_map/ppermute | solution.py:44
  493.4 11.1 %collective-permute-start.70 = (bf16[126,768]{1,0:T(8,128)(2,1)S(1)}, bf16[126,768]{1,0:T(8,128)(2,1)}, u32[]{:S(2)}, u32[]{:S(2)}) collective-permute-start(bf16[126,768]{1,0:T(8,128)(2,1)S(1)} %get-tuple-element.377), channel_id=1, source_target_pairs={{0,3},{1,0},{2,1},{3,2},{4,7},{5,4},{6,5},{7,6},{8,11},{9,8},{10,9... | collective-permute-start | bytes 580616 | tf_op jit(solution)/shard_map/ppermute | solution.py:44
  497.1 62.3 %all-to-all-start.8 = ((bf16[64,22,768]{2,1,0:T(8,128)(2,1)}), bf16[64,22,768]{2,1,0:T(8,128)(2,1)S(1)}, u32[]{:S(2)}, u32[]{:S(2)}) async-start(bf16[64,22,768]{2,1,0:T(8,128)(2,1)} %reshape.59), calls=%async_computation.8 | async-start | bytes 4718592 | tf_op jit(solution)/shard_map/all_to_all | solution.py:181
  506.0 34.9 %collective-permute-start.69 = (bf16[252,768]{1,0:T(8,128)(2,1)S(1)}, bf16[252,768]{1,0:T(8,128)(2,1)}, u32[]{:S(2)}, u32[]{:S(2)}) collective-permute-start(bf16[252,768]{1,0:T(8,128)(2,1)S(1)} %pad_maximum_fusion.3), channel_id=1, source_target_pairs={{0,1},{1,2},{2,3},{3,0},{4,5},{5,6},{6,7},{7,4},{8,9},{9,10},{10,1... | collective-permute-start | bytes 1161224 | tf_op jit(solution)/shard_map/ppermute | solution.py:44
  507.8 33.0 %collective-permute-start.71 = (bf16[252,768]{1,0:T(8,128)(2,1)}, bf16[252,768]{1,0:T(8,128)(2,1)}, u32[]{:S(2)}, u32[]{:S(2)}) collective-permute-start(bf16[252,768]{1,0:T(8,128)(2,1)} %pad_maximum_fusion.4), channel_id=1, source_target_pairs={{0,3},{1,0},{2,1},{3,2},{4,7},{5,4},{6,5},{7,6},{8,11},{9,8},{10,9... | collective-permute-start | bytes 1161224 | tf_op jit(solution)/shard_map/ppermute | solution.py:44
  509.6 34.9 %collective-permute-start.45 = (bf16[128,768]{1,0:T(8,128)(2,1)S(1)}, bf16[128,768]{1,0:T(8,128)(2,1)S(1)}, u32[]{:S(2)}, u32[]{:S(2)}) collective-permute-start(bf16[128,768]{1,0:T(8,128)(2,1)S(1)} %broadcast_select_fusion.8), channel_id=1, source_target_pairs={{0,64},{64,0},{1,65},{65,1},{2,66},{66,2},{3,67},{67,3},{4,68},{68... | collective-permute-start | bytes 589832 | tf_op jit(solution)/shard_map/ppermute | solution.py:52
  542.2 10.7 %collective-permute-start.72 = (bf16[252,768]{1,0:T(8,128)(2,1)S(1)}, bf16[252,768]{1,0:T(8,128)(2,1)S(1)}, u32[]{:S(2)}, u32[]{:S(2)}) collective-permute-start(bf16[252,768]{1,0:T(8,128)(2,1)S(1)} %fusion.1), channel_id=1, source_target_pairs={{0,4},{1,5},{2,6},{3,7},{4,0},{5,1},{6,2},{7,3},{8,12},{9,13},{10,... | collective-permute-start | bytes 1161224 | tf_op jit(solution)/shard_map/ppermute | solution.py:48
  544.6 14.0 %collective-permute-start.61 = (bf16[128,768]{1,0:T(8,128)(2,1)S(1)}, bf16[128,768]{1,0:T(8,128)(2,1)S(1)}, u32[]{:S(2)}, u32[]{:S(2)}) collective-permute-start(bf16[128,768]{1,0:T(8,128)(2,1)S(1)} %broadcast_select_fusion.6), channel_id=1, source_target_pairs={{0,64},{64,0},{1,65},{65,1},{2,66},{66,2},{3,67},{67,3},{4,68},{68... | collective-permute-start | bytes 589832 | tf_op jit(solution)/shard_map/ppermute | solution.py:52
  555.1 9.6 %collective-permute-start.73 = (bf16[252,768]{1,0:T(8,128)(2,1)}, bf16[252,768]{1,0:T(8,128)(2,1)S(1)}, u32[]{:S(2)}, u32[]{:S(2)}) collective-permute-start(bf16[252,768]{1,0:T(8,128)(2,1)} %get-tuple-element.366), channel_id=1, source_target_pairs={{0,1},{1,2},{2,3},{3,0},{4,5},{5,6},{6,7},{7,4},{8,9},{9,10},{10,1... | collective-permute-start | bytes 1161224 | tf_op jit(solution)/shard_map/ppermute | solution.py:44
  555.1 10.3 %collective-permute-start.74 = (bf16[252,768]{1,0:T(8,128)(2,1)}, bf16[252,768]{1,0:T(8,128)(2,1)}, u32[]{:S(2)}, u32[]{:S(2)}) collective-permute-start(bf16[252,768]{1,0:T(8,128)(2,1)} %get-tuple-element.366), channel_id=1, source_target_pairs={{0,3},{1,0},{2,1},{3,2},{4,7},{5,4},{6,5},{7,6},{8,11},{9,8},{10,9... | collective-permute-start | bytes 1161224 | tf_op jit(solution)/shard_map/ppermute | solution.py:44
  560.5 11.2 %all-to-all-start.9 = ((bf16[8,22,768]{2,1,0:T(8,128)(2,1)}), bf16[8,22,768]{2,1,0:T(8,128)(2,1)S(1)}, u32[]{:S(2)}, u32[]{:S(2)}) async-start(bf16[8,22,768]{2,1,0:T(8,128)(2,1)} %broadcast_in_dim.41), calls=%async_computation.9 | async-start | bytes 589824 | tf_op jit(solution)/shard_map/all_to_all | solution.py:184
  (155 other events, 1357.2 us)
